TPU v7x, 128 devices: a whole 4x4x4 slice. The times are simulated.
128 devices in a mesh: leaf: 4 (over x), box: 32 (over y, z, core).
Axes of the slice: x: 4, y: 4, z: 4, core: 2. Of those that a mesh axis runs over, the one named last changes fastest.
Arguments:
- charges: bfloat16 [8192, 32, 256], P(('leaf', 'box')), may hold values from -6 to 6
- counts: int32 [8192], P(('leaf', 'box')), may hold values from 32 to 256
- leaf_basis: bfloat16 [8192, 64, 256], P(('leaf', 'box')), may hold values from -0.375 to 0.375
- out_basis: bfloat16 [8192, 64, 256], P(('leaf', 'box')), may hold values from -0.75 to 0.75
- leaf_transfer: bfloat16 [8192, 64, 64], P(('leaf', 'box')), may hold values from -0.25 to 0.25
- leaf_descend: bfloat16 [8192, 64, 64], P(('leaf', 'box')), may hold values from -0.75 to 0.75
- parent_transfer: bfloat16 [1024, 64, 64], P(('leaf', 'box')), may hold values from -0.25 to 0.25
- parent_descend: bfloat16 [1024, 64, 64], P(('leaf', 'box')), may hold values from -0.75 to 0.75
- leaf_coupling: bfloat16 [8192, 16, 64, 64], P(('leaf', 'box')), may hold values from -0.1875 to 0.1875
- far_owner: int32 [8192, 16], P(('leaf', 'box')), may hold values from 0 to 31, as said below
- far_local: int32 [8192, 16], P(('leaf', 'box')), may hold values from 0 to 63
- parent_coupling: bfloat16 [1024, 16, 64, 64], P(('leaf', 'box')), may hold values from -0.1875 to 0.1875
- parent_owner: int32 [1024, 16], P(('leaf', 'box')), may hold values from 0 to 31
- parent_index: int32 [1024, 16], P(('leaf', 'box')), may hold values from 0 to 7
- top_coupling: bfloat16 [128, 16, 64, 64], P(('leaf', 'box')), may hold values from -0.1875 to 0.1875
- top_source: int32 [128, 16], P(('leaf', 'box')), may hold values from 0 to 127
Outputs:
- potential: bfloat16 [8192, 32, 256], P(('leaf', 'box'))
Inputs may be any that keep to these rules, and one draw needn't show every extreme that they name: `far_owner`: among the 1024 entries of the rows of one device, at most 48 name the same device, and one device is named by exactly 48 entries of every device's rows.
All inputs are finite; a program needn't handle non-finite values.
Results may differ from a plain program's by a relative error of at most 0.014.
Values may be sent and summed in bfloat16 or wider, within the bound.
No kernel may reach another device: no remote copies, remote signals or barrier semaphores. Data moves between devices by JAX's collectives and lax.ppermute only.
A program may use at most 128 MiB of HBM per device.

v0:
```python
import jax
import jax.numpy as jnp
from jax import lax
from jax.sharding import PartitionSpec as P


def ascend(coeffs, transfer):
    groups = coeffs.shape[0] // 8
    grouped = coeffs.reshape(groups, 8, coeffs.shape[1], coeffs.shape[2])
    matrices = transfer.reshape(groups, 8, transfer.shape[1], transfer.shape[2])
    return jnp.einsum(
        "pcrk,pckq->prq", grouped, matrices, preferred_element_type=jnp.float32
    ).astype(jnp.bfloat16)


def descend(field, matrices):
    groups = field.shape[0]
    grouped = matrices.reshape(groups, 8, matrices.shape[1], matrices.shape[2])
    result = jnp.einsum("prq,pcqk->pcrk", field, grouped, preferred_element_type=jnp.float32)
    return result.reshape(groups * 8, field.shape[1], matrices.shape[2])


def couple_picked(picked, couplings, vectors):
    targets = couplings.shape[0]
    slot_count = couplings.shape[1]
    skeleton = couplings.shape[2]
    blocks = picked.reshape(targets, slot_count, vectors, skeleton)
    return jnp.einsum("tjrk,tjkq->trq", blocks, couplings, preferred_element_type=jnp.float32)


def body(
    charges,
    counts,
    leaf_basis,
    out_basis,
    leaf_transfer,
    leaf_descend,
    parent_transfer,
    parent_descend,
    leaf_coupling,
    far_owner,
    far_local,
    parent_coupling,
    parent_owner,
    parent_index,
    top_coupling,
    top_source,
):
    vectors = charges.shape[1]
    points = charges.shape[2]
    leaf_count = charges.shape[0]
    inside = jnp.arange(points, dtype=jnp.int32)[None, None, :] < counts[:, None, None]
    masked = jnp.where(inside, charges, jnp.zeros_like(charges))
    leaf_coeff = jnp.einsum(
        "brp,bkp->brk", masked, leaf_basis, preferred_element_type=jnp.float32
    ).astype(jnp.bfloat16)
    parent_coeff = ascend(leaf_coeff, leaf_transfer)
    top_coeff = ascend(parent_coeff, parent_transfer)
    parent_count = parent_coeff.shape[0]
    top_all = lax.all_gather(
        top_coeff.reshape(top_coeff.shape[0], -1), ("leaf", "box"), axis=0, tiled=True
    )
    top_picked = top_all[top_source.reshape(-1)]
    top_field = couple_picked(top_picked, top_coupling, vectors).astype(jnp.bfloat16)
    parent_all = lax.all_gather(parent_coeff.reshape(parent_count, -1), "box", axis=0, tiled=True)
    parent_rows = (parent_owner * parent_count + parent_index).reshape(-1)
    parent_far = couple_picked(parent_all[parent_rows], parent_coupling, vectors)
    parent_field = (parent_far + descend(top_field, parent_descend)).astype(jnp.bfloat16)
    leaf_flat = leaf_coeff.reshape(leaf_count, -1)
    leaf_all = lax.all_gather(leaf_flat, "box", axis=0, tiled=True)
    picked = leaf_all[(far_owner * leaf_count + far_local).reshape(-1)]
    leaf_far = couple_picked(picked, leaf_coupling, vectors)
    leaf_field = (leaf_far + descend(parent_field, leaf_descend)).astype(jnp.bfloat16)
    values = jnp.einsum("brk,bkp->brp", leaf_field, out_basis, preferred_element_type=jnp.float32)
    return jnp.where(inside, values, jnp.zeros_like(values)).astype(jnp.bfloat16)


def solution(mesh):
    in_specs = (
        P(("leaf", "box"), None, None),
        P(("leaf", "box")),
        P(("leaf", "box"), None, None),
        P(("leaf", "box"), None, None),
        P(("leaf", "box"), None, None),
        P(("leaf", "box"), None, None),
        P(("leaf", "box"), None, None),
        P(("leaf", "box"), None, None),
        P(("leaf", "box"), None, None, None),
        P(("leaf", "box"), None),
        P(("leaf", "box"), None),
        P(("leaf", "box"), None, None, None),
        P(("leaf", "box"), None),
        P(("leaf", "box"), None),
        P(("leaf", "box"), None, None, None),
        P(("leaf", "box"), None),
    )
    out_specs = P(("leaf", "box"), None, None)
    return jax.shard_map(body, mesh=mesh, in_specs=in_specs, out_specs=out_specs, check_vma=False)
```

profile of v0, /device:TPU:1, one launch (start us, length us, event | category | flops | bytes accessed | tf_op | source)
XLA Modules:
  0.0 159.1 jit_solution(5422638580587998963)
XLA Ops:
  6.6 0.0 all-gather.6.cloned.1.call-start
  6.6 0.9 iota_compare_fusion
  7.5 0.0 copy-start.8
  7.5 2.6 %convolution_convert_fusion = bf16[64,32,64]{2,1,0:T(8,128)(2,1)S(1)} fusion(bf16[64,64,256]{2,1,0:T(8,128)(2,1)} %param.18, bf16[64,32,256]{2,1,0:T(8,128)(2,1)} %param.16, pred[64,256]{1,0:T(8,128)(4,1)S(1)} %iota_compare_fusion), kind=kOutput, calls=%fused_computation.5 | convolution fusion | flops 67764224 | bytes 3424256 | tf_op jit(solution)/shard_map/brp,bkp->brk/dot_general | solution.py:54
  10.1 0.0 copy-start.1
  10.1 1.6 %fusion.3 = bf16[8,32,64]{2,1,0:T(8,128)(2,1)S(1)} fusion(bf16[8,8,32,64]{3,2,1,0:T(8,128)(2,1)S(1)} %bitcast.84, bf16[8,8,64,64]{3,2,1,0:T(8,128)(2,1)} %bitcast.87), kind=kOutput, calls=%fused_computation.12 | convolution fusion | flops 16793600 | bytes 819200 | tf_op jit(solution)/shard_map/pcrk,pckq->prq/dot_general | solution.py:11
  11.7 0.7 reshape.174
  12.5 0.0 all-gather.6.cloned.1.call-update
  12.5 0.0 all-gather.4.cloned.1.call-start
  12.5 1.2 reshape.169
  13.7 0.0 all-gather.4.cloned.1.call-update
  13.8 0.1 reshape.175
  13.8 0.1 copy.21
  13.9 0.1 reshape.170
  14.0 0.2 fusion.7
  14.2 0.1 reshape.208
  14.3 39.7 %all-gather = bf16[128,1,2048]{2,1,0:T(2,128)(2,1)S(1)} all-gather(bf16[1,1,2048]{2,1,0:T(2,128)(2,1)S(1)} %reshape.208), channel_id=1, replica_groups=mesh['leaf'=4,'box'=32] {'leaf','box'}, dimensions={0}, use_global_device_ids=true | all-gather | bytes 528384 | tf_op jit(solution)/shard_map/all_gather | solution.py:60
  54.0 0.3 copy.28
  54.3 0.0 copy-done.8
  54.4 0.6 gather_fusion.2
  55.0 0.2 reshape.179
  55.2 0.2 fusion.8
  55.4 0.0 copy-start.2
  55.4 3.9 %all-gather.6.cloned.1.call-done = bf16[256,2048]{1,0:T(8,128)(2,1)} async-done(((bf16[8,2048]{1,0:T(8,128)(2,1)}), bf16[256,2048]{1,0:T(8,128)(2,1)}) %all-gather.6.cloned.1.call-update) | async-done | bytes 1048592 | tf_op jit(solution)/shard_map/all_gather | solution.py:65
  59.3 3.6 %gather_fusion.1 = bf16[128,2048]{1,0:T(8,128)(2,1)} fusion(bf16[256,2048]{1,0:T(8,128)(2,1)} %all-gather.6.cloned.1.call-done, s32[1024]{0:T(1024)S(1)} %pad_clamp_fusion.1), kind=kCustom, calls=%fused_computation.1 | custom fusion | bytes 1049088 | tf_op jit(solution)/shard_map/gather | solution.py:67
  62.9 2.1 %reshape.176 = bf16[8,16,32,64]{3,2,1,0:T(8,128)(2,1)S(1)} reshape(bf16[128,2048]{1,0:T(8,128)(2,1)} %gather_fusion.1) | data formatting | bytes 1048576 | tf_op jit(solution)/shard_map/reshape | solution.py:27
  65.0 2.1 %convolution_bitcast_fusion.2 = f32[8,32,64]{2,1,0:T(8,128)S(1)} fusion(bf16[8,16,32,64]{3,2,1,0:T(8,128)(2,1)S(1)} %reshape.176, bf16[8,16,64,64]{3,2,1,0:T(8,128)(2,1)} %param.27), kind=kOutput, calls=%fused_computation.10 | convolution fusion | flops 33554432 | bytes 1638400 | tf_op jit(solution)/shard_map/tjrk,tjkq->trq/dot_general | solution.py:28
  67.1 1.6 %fusion.11 = f32[8,32,8,64]{3,1,2,0:T(8,128)S(1)} fusion(bf16[8,8,64,64]{3,2,1,0:T(8,128)(2,1)} %bitcast.88, f32[8,32,64]{2,1,0:T(8,128)S(1)} %convolution_bitcast_fusion.2, bf16[32,64,1]{1,0,2:T(8,128)(2,1)S(1)} %fusion.8, bf16[8,64,64]{2,1,0:T(8,128)(2,1)S(1)} %copy-done.2), kind=kOutput, calls=%fused_computation.22 | convolution fusion | flops 18907136 | bytes 1183744 | tf_op jit(solution)/shard_map/prq,pcqk->pcrk/dot_general | solution.py:19
  68.7 45.0 %all-gather.4.cloned.1.call-done = bf16[2048,2048]{1,0:T(8,128)(2,1)} async-done(((bf16[64,2048]{1,0:T(8,128)(2,1)}), bf16[2048,2048]{1,0:T(8,128)(2,1)}) %all-gather.4.cloned.1.call-update) | async-done | bytes 8388624 | tf_op jit(solution)/shard_map/all_gather | solution.py:70
  113.7 13.3 %gather_fusion = bf16[1024,2048]{1,0:T(8,128)(2,1)} fusion(bf16[2048,2048]{1,0:T(8,128)(2,1)} %all-gather.4.cloned.1.call-done, s32[1024]{0:T(1024)S(1)} %broadcast_clamp_fusion), kind=kCustom, calls=%fused_computation | custom fusion | bytes 8392704 | tf_op jit(solution)/shard_map/gather | solution.py:71
  127.0 12.9 %reshape.171 = bf16[64,16,32,64]{3,2,1,0:T(8,128)(2,1)} reshape(bf16[1024,2048]{1,0:T(8,128)(2,1)} %gather_fusion) | data formatting | bytes 8388608 | tf_op jit(solution)/shard_map/reshape | solution.py:27
  139.9 12.4 %select_convert_fusion = bf16[64,32,256]{2,1,0:T(8,128)(2,1)} fusion(bf16[64,64,256]{2,1,0:T(8,128)(2,1)S(1)} %copy-done, f32[64,32,64]{2,1,0:T(8,128)S(1)} %bitcast.85, bf16[64,16,32,64]{3,2,1,0:T(8,128)(2,1)} %reshape.171, bf16[64,16,64,64]{3,2,1,0:T(8,128)(2,1)} %param.24, pred[64,256]{1,0:T(8,128)(4,1)S(1)} %iota_compare_fusion), kind=kOutput, calls=%fused_computation.3 | convolution fusion | flops 336855040 | bytes 16269312 | tf_op jit(solution)/shard_map/brk,bkp->brp/dot_general | solution.py:74
  (22 shorter events, 0.1 us)
Async XLA Ops:
  6.5 133.3 %copy-start = (bf16[64,64,256]{2,1,0:T(8,128)(2,1)S(1)}, bf16[64,64,256]{2,1,0:T(8,128)(2,1)}, u32[]{:S(2)}) copy-start(bf16[64,64,256]{2,1,0:T(8,128)(2,1)} %param.19) | copy-start | bytes 6291460
  6.5 7.2 %copy-start.6 = (s32[8,16]{1,0:T(8,128)S(1)}, s32[8,16]{1,0:T(8,128)}, u32[]{:S(2)}) copy-start(s32[8,16]{1,0:T(8,128)} %param.29) | copy-start | bytes 1540
  6.5 7.2 %copy-start.7 = (s32[8,16]{1,0:T(8,128)S(1)}, s32[8,16]{1,0:T(8,128)}, u32[]{:S(2)}) copy-start(s32[8,16]{1,0:T(8,128)} %param.28) | copy-start | bytes 1540
  6.5 7.3 %copy-start.4 = (s32[64,16]{0,1:T(8,128)S(1)}, s32[64,16]{0,1:T(8,128)}, u32[]{:S(2)}) copy-start(s32[64,16]{0,1:T(8,128)} %param.26) | copy-start | bytes 12292
  6.5 7.3 %copy-start.5 = (s32[64,16]{0,1:T(8,128)S(1)}, s32[64,16]{0,1:T(8,128)}, u32[]{:S(2)}) copy-start(s32[64,16]{0,1:T(8,128)} %param.25) | copy-start | bytes 12292
  6.5 7.5 %copy-start.3 = (bf16[8,64,64]{2,1,0:T(8,128)(2,1)S(1)}, bf16[8,64,64]{2,1,0:T(8,128)(2,1)}, u32[]{:S(2)}) copy-start(bf16[8,64,64]{2,1,0:T(8,128)(2,1)} %param.22) | copy-start | bytes 196612
  6.6 52.8 %all-gather.6.cloned.1.call-start = ((), (), s32[]{:S(2)}) async-start(), calls=%async_computation.1 | async-start | bytes 1081344 | tf_op jit(solution)/shard_map/all_gather | solution.py:65
  7.5 46.8 %copy-start.8 = (s32[1,16]{1,0:T(1,128)S(1)}, s32[1,16]{1,0:T(1,128)}, u32[]{:S(2)}) copy-start(s32[1,16]{1,0:T(1,128)} %param.31) | copy-start | bytes 196
  10.1 45.1 %copy-start.1 = (bf16[1,16,64,64]{3,2,1,0:T(8,128)(2,1)S(1)}, bf16[1,16,64,64]{3,2,1,0:T(8,128)(2,1)}, u32[]{:S(2)}) copy-start(bf16[1,16,64,64]{3,2,1,0:T(8,128)(2,1)} %param.30) | copy-start | bytes 393220
  12.5 101.3 %all-gather.4.cloned.1.call-start = ((), (), s32[]{:S(2)}) async-start(), calls=%async_computation | async-start | bytes 8650752 | tf_op jit(solution)/shard_map/all_gather | solution.py:70
  55.4 11.6 %copy-start.2 = (bf16[8,64,64]{2,1,0:T(8,128)(2,1)S(1)}, bf16[8,64,64]{2,1,0:T(8,128)(2,1)}, u32[]{:S(2)}) copy-start(bf16[8,64,64]{2,1,0:T(8,128)(2,1)} %param.23) | copy-start | bytes 196612
Sparse Core Ops, SparseCore 0:
  12.6 46.6 all-gather.5
  61.6 52.1 all-gather.3
where the time goes:
time: 160 us; the launch traced here: 159 us
  waiting for transfers between devices  49 us (31%)
  blocking collectives  39.7 us (25%)
  local copies, waits for them, and re-layouts  35.2 us (22%)
  matrix products  20.7 us (13%)
  between operations  13.6 us (8%)
    all_gather x1, waiting for transfers between devices, body(): leaf_all = lax.all_gather(leaf_flat, 'box', axis=0, tiled=True)  45 us
    all_gather x1, blocking collectives, body(): lax.all_gather(top_coeff.reshape(top_coeff.shape[0], -1), ('leaf', 'box')...  39.7 us
    reshape x2, local copies, waits for them, and re-layouts, couple_picked(): blocks = picked.reshape(targets, slot_count, vectors, skeleton)  14.9 us
    gather x1, local copies, waits for them, and re-layouts, body(): picked = leaf_all[(far_owner * leaf_count + far_local).reshape(-1)]  13.3 us
    dot_general x1, matrix products, body(): jnp.einsum('brk,bkp->brp', leaf_field, out_basis, preferred_element_type=...  12.4 us
    all_gather x1, waiting for transfers between devices, body(): lax.all_gather(parent_coeff.reshape(parent_count, -1), 'box', axis=0, til...  3.89 us
    gather x1, local copies, waits for them, and re-layouts, body(): parent_all[parent_rows]  3.59 us
  transfers between devices with their start and end apart: 2, of which 2 were waited for; matrix products, arithmetic and copies ran while one was open for 8% of the time, Pallas kernels for 0%

commit v1 on v0

v1 whole, which is shorter than its diff:
```python
import functools

import jax
import jax.numpy as jnp
from jax import lax
from jax.experimental import pallas as pl
from jax.experimental.pallas import tpu as pltpu
from jax.sharding import Mesh
from jax.sharding import PartitionSpec as P

BF16 = jnp.bfloat16
F32 = jnp.float32
LEAF, PARENT = 64, 8
ROWS = LEAF + PARENT + 1
CUT = 37
NT = (((1,), (1,)), ((), ()))
MIB = 1 << 20


def dot(a, b):
    return jnp.dot(a, b, preferred_element_type=F32)


def pack(c):
    return jnp.concatenate([c[:16], c[16:]], axis=1)


def up_kernel(per, counts, charges, basis, transfer, parent_transfer, out, top):
    step = pl.program_id(0)
    column = lax.broadcasted_iota(jnp.int32, (32, 256), 1)

    @pl.when(step == 0)
    def _():
        top[...] = jnp.zeros_like(top)

    for p in range(per):
        total = jnp.zeros((32, 64), F32)
        for i in range(8):
            b = p * 8 + i
            live = column < counts[step * per * 8 + b]
            masked = jnp.where(live, charges[b], jnp.zeros((32, 256), BF16))
            coeff = lax.dot_general(masked, basis[b], NT, preferred_element_type=F32).astype(BF16)
            out[step * per * 8 + b] = pack(coeff)
            total += dot(coeff, transfer[b])
        parent = total.astype(BF16)
        out[LEAF + step * per + p] = pack(parent)
        top[...] += dot(parent, parent_transfer[p])

    @pl.when(step == pl.num_programs(0) - 1)
    def _():
        out[ROWS - 1] = pack(top[...].astype(BF16))


def up(counts, charges, basis, transfer, parent_transfer):
    per = 2
    steps = PARENT // per
    block = lambda *s: pl.BlockSpec(s, lambda i: (i,) + (0,) * (len(s) - 1))
    return pl.pallas_call(
        functools.partial(up_kernel, per),
        grid=(steps,),
        in_specs=[
            pl.BlockSpec(memory_space=pltpu.SMEM),
            block(8 * per, 32, 256),
            block(8 * per, 64, 256),
            block(8 * per, 64, 64),
            block(per, 64, 64),
        ],
        out_specs=pl.BlockSpec((ROWS, 16, 128), lambda i: (0, 0, 0)),
        out_shape=jax.ShapeDtypeStruct((ROWS, 16, 128), BF16),
        scratch_shapes=[pltpu.VMEM((32, 64), F32)],
        compiler_params=pltpu.CompilerParams(vmem_limit_bytes=16 * MIB),
        cost_estimate=pl.CostEstimate(flops=2 * 64 * 32 * 64 * 320, bytes_accessed=5 * MIB, transcendentals=0),
        name="up",
    )(counts, charges, basis, transfer, parent_transfer)


def pairs(second, mask):
    out = []
    for y in range(4):
        for z in range(4):
            for c in range(2):
                along_y = (c == 0) != second
                ty, tz = (y ^ mask, z) if along_y else (y, z ^ mask)
                out.append(((y * 4 + z) * 2 + c, (ty * 4 + tz) * 2 + c))
    return out


def send(x, second, mask):
    return lax.ppermute(x, ("y", "z", "c"), pairs(second, mask))


def other_core(x):
    return lax.ppermute(x, "c", [(0, 1), (1, 0)])


def gather_pieces(s):
    s = s[None]
    full, low, high = (0, ROWS), (0, CUT), (CUT, ROWS - CUT)
    a, b = send(s, False, 1), send(s, False, 3)
    va1, vb1 = send(s, True, 1), send(s, True, 3)
    o_low = send(a[:, :CUT], False, 3)
    o_high = send(b[:, CUT:], False, 1)
    t2 = jnp.concatenate([a, b])
    va2, vb2 = send(t2, True, 1), send(t2, True, 3)
    o = jnp.concatenate([o_low, o_high], axis=1)
    va3, vb3 = send(o, True, 1), send(o, True, 3)
    f1_low = send(va1[:, :CUT], True, 3)
    f1_high = send(vb1[:, CUT:], True, 1)
    f2_a = send(va2[:1], True, 3)
    f2_b = send(vb2[1:], True, 1)
    f3_low = send(va3[:, :CUT], True, 3)
    f3_high = send(vb3[:, CUT:], True, 1)
    own = [
        (s, [(0, 0) + full]),
        (t2, [(0, 1) + full, (0, 3) + full]),
        (o, [(0, 2) + full]),
        (va1, [(1, 0) + full]),
        (vb1, [(3, 0) + full]),
        (va2, [(1, 1) + full, (1, 3) + full]),
        (vb2, [(3, 1) + full, (3, 3) + full]),
        (va3, [(1, 2) + full]),
        (vb3, [(3, 2) + full]),
        (f1_low, [(2, 0) + low]),
        (f1_high, [(2, 0) + high]),
        (f2_a, [(2, 1) + full]),
        (f2_b, [(2, 3) + full]),
        (f3_low, [(2, 2) + low]),
        (f3_high, [(2, 2) + high]),
    ]
    pieces = []
    for x, places in own:
        pieces.append((x, [(0,) + p for p in places]))
        pieces.append((other_core(x), [(1,) + p for p in places]))
    return pieces


def assemble_kernel(places, *refs):
    n = len(places)
    sources, rows, tops, sem = refs[:n], refs[n], refs[n + 1], refs[n + 2]
    copies = []
    for ref, spots in zip(sources, places):
        for i, (core, v, u, first, count) in enumerate(spots):
            slot = core * 16 + v * 4 + u
            copies.append((ref.at[i], rows.at[pl.ds(slot * ROWS + first, count)]))
            if first + count == ROWS:
                copies.append((ref.at[i, count - 1], tops.at[slot]))
    started = []
    for k, (src, dst) in enumerate(copies):
        copy = pltpu.make_async_copy(src, dst, sem.at[k])
        copy.start()
        started.append(copy)
    for copy in started:
        copy.wait()


def assemble(pieces):
    arrays = [x for x, _ in pieces]
    places = [p for _, p in pieces]
    return pl.pallas_call(
        functools.partial(assemble_kernel, places),
        in_specs=[pl.BlockSpec(memory_space=pl.ANY)] * len(arrays),
        out_specs=[pl.BlockSpec(memory_space=pl.ANY)] * 2,
        out_shape=[
            jax.ShapeDtypeStruct((32 * ROWS, 16, 128), BF16),
            jax.ShapeDtypeStruct((32, 16, 128), BF16),
        ],
        scratch_shapes=[pltpu.SemaphoreType.DMA((96,))],
        name="assemble",
    )(*arrays)


def slots(owner, y, z, c):
    oy, oz, oc = owner // 8, owner // 2 % 4, owner % 2
    ry, rz = oy ^ y, oz ^ z
    return (oc ^ c) * 16 + jnp.where(oc == 0, rz * 4 + ry, ry * 4 + rz)


def picked(rows, gathered, base, entries):
    lane = lax.broadcasted_iota(jnp.int32, (16, 128), 1) < 64
    low, high = [], []
    for j in range(0, entries, 2):
        a, b = gathered[rows[base + j]], gathered[rows[base + j + 1]]
        low.append(jnp.where(lane, a, jnp.concatenate([b[:, 64:], b[:, :64]], axis=1)))
        high.append(jnp.where(lane, jnp.concatenate([a[:, 64:], a[:, :64]], axis=1), b))
    return jnp.concatenate([jnp.concatenate(low, axis=1), jnp.concatenate(high, axis=1)], axis=0)


def couple_kernel(leaf_rows, parent_rows, gathered, coupling, parent_coupling, leaf_far, parent_far):
    step = pl.program_id(0)
    for i in range(8):
        block = picked(leaf_rows, gathered, (step * 8 + i) * 16, 16)
        leaf_far[i] = dot(block, coupling[i].reshape(1024, 64))
    block = picked(parent_rows, gathered, step * 16, 16)
    parent_far[0] = dot(block, parent_coupling[0].reshape(1024, 64))


def couple(leaf_rows, parent_rows, gathered, coupling, parent_coupling):
    block = lambda *s: pl.BlockSpec(s, lambda i: (i,) + (0,) * (len(s) - 1))
    return pl.pallas_call(
        couple_kernel,
        grid=(8,),
        in_specs=[
            pl.BlockSpec(memory_space=pltpu.SMEM),
            pl.BlockSpec(memory_space=pltpu.SMEM),
            pl.BlockSpec(memory_space=pltpu.VMEM),
            block(8, 16, 64, 64),
            block(1, 16, 64, 64),
        ],
        out_specs=[block(8, 32, 64), block(1, 32, 64)],
        out_shape=[jax.ShapeDtypeStruct((64, 32, 64), F32), jax.ShapeDtypeStruct((8, 32, 64), F32)],
        compiler_params=pltpu.CompilerParams(vmem_limit_bytes=32 * MIB),
        cost_estimate=pl.CostEstimate(flops=2 * 72 * 32 * 64 * 1024, bytes_accessed=28 * MIB, transcendentals=0),
        name="couple",
    )(leaf_rows, parent_rows, gathered, coupling, parent_coupling)


def down_kernel(
    counts, top_rows, tops, top_coupling, parent_far, parent_descend, leaf_far, leaf_descend, out_basis, out, top_field
):
    step = pl.program_id(0)

    @pl.when(step == 0)
    def _():
        block = picked(top_rows, tops, 0, 16)
        top_field[...] = dot(block, top_coupling[0].reshape(1024, 64)).astype(BF16)

    parent = (parent_far[0] + dot(top_field[...], parent_descend[0])).astype(BF16)
    column = lax.broadcasted_iota(jnp.int32, (32, 256), 1)
    for i in range(8):
        field = (leaf_far[i] + dot(parent, leaf_descend[i])).astype(BF16)
        values = dot(field, out_basis[i])
        live = column < counts[step * 8 + i]
        out[i] = jnp.where(live, values, jnp.zeros_like(values)).astype(BF16)


def down(counts, top_rows, tops, top_coupling, parent_far, parent_descend, leaf_far, leaf_descend, out_basis):
    block = lambda *s: pl.BlockSpec(s, lambda i: (i,) + (0,) * (len(s) - 1))
    whole = pl.BlockSpec(memory_space=pltpu.VMEM)
    return pl.pallas_call(
        down_kernel,
        grid=(8,),
        in_specs=[
            pl.BlockSpec(memory_space=pltpu.SMEM),
            pl.BlockSpec(memory_space=pltpu.SMEM),
            whole,
            whole,
            block(1, 32, 64),
            block(1, 64, 64),
            block(8, 32, 64),
            block(8, 64, 64),
            block(8, 64, 256),
        ],
        out_specs=block(8, 32, 256),
        out_shape=jax.ShapeDtypeStruct((64, 32, 256), BF16),
        scratch_shapes=[pltpu.VMEM((32, 64), BF16)],
        compiler_params=pltpu.CompilerParams(vmem_limit_bytes=16 * MIB),
        cost_estimate=pl.CostEstimate(flops=2 * 64 * 32 * 64 * 320, bytes_accessed=6 * MIB, transcendentals=0),
        name="down",
    )(counts, top_rows, tops, top_coupling, parent_far, parent_descend, leaf_far, leaf_descend, out_basis)


def body(
    charges,
    counts,
    leaf_basis,
    out_basis,
    leaf_transfer,
    leaf_descend,
    parent_transfer,
    parent_descend,
    leaf_coupling,
    far_owner,
    far_local,
    parent_coupling,
    parent_owner,
    parent_index,
    top_coupling,
    top_source,
):
    x, y, z, c = (lax.axis_index(a) for a in "xyzc")
    leaf_rows = (slots(far_owner, y, z, c) * ROWS + far_local).reshape(-1)
    parent_rows = (slots(parent_owner, y, z, c) * ROWS + LEAF + parent_index).reshape(-1)
    top_rows = (((top_source // 32) ^ x) * 32 + slots(top_source % 32, y, z, c)).reshape(-1)

    coeffs = up(counts, charges, leaf_basis, leaf_transfer, parent_transfer)
    gathered, tops = assemble(gather_pieces(coeffs))
    planes = [tops] + [lax.ppermute(tops, "x", [(i, i ^ m) for i in range(4)]) for m in (1, 2, 3)]
    leaf_far, parent_far = couple(leaf_rows, parent_rows, gathered, leaf_coupling, parent_coupling)
    return down(
        counts,
        top_rows,
        jnp.concatenate(planes),
        top_coupling,
        parent_far,
        parent_descend,
        leaf_far,
        leaf_descend,
        out_basis,
    )


def solution(mesh):
    fine = Mesh(mesh.devices.reshape(4, 4, 4, 2), ("x", "y", "z", "c"))
    spec = P(("x", "y", "z", "c"))
    return jax.shard_map(body, mesh=fine, in_specs=(spec,) * 16, out_specs=spec, check_vma=False)
```

time: 160 us -> 387 us (2.42)
  Pallas kernels: 0 us -> 316 us
  starting transfers between devices: 0.08 us -> 47.9 us
  waiting for transfers between devices: 49 us -> 8.51 us
  blocking collectives: 39.7 us -> 0 us
  local copies, waits for them, and re-layouts: 35.2 us -> 13.3 us
  matrix products: 20.7 us -> 0 us
  between operations: 13.6 us -> 0.55 us
    pallas_call x0 -> x4, Pallas kernels: none -> 316 us  [the longest x1 296 us: assemble(): pl.pallas_call(functools.partial(assemble_kernel, places), in_specs=[pl.B...]
    all_gather x2 -> x0, waiting for transfers between devices: 48.9 us -> none  [the longest x1 45 us: body(): leaf_all = lax.all_gather(leaf_flat, 'box', axis=0, tiled=True)]
    ppermute x0 -> x34, starting transfers between devices: none -> 47.9 us  [the longest x16 22.5 us: send(): return lax.ppermute(x, ('y', 'z', 'c'), pairs(second, mask))]
    all_gather x1 -> x0, blocking collectives: 39.7 us -> none  [body(): lax.all_gather(top_coeff.reshape(top_coeff.shape[0], -1), ('leaf', 'box')...]
    dot_general x7 -> x0, matrix products: 20.7 us -> none  [the longest x1 12.4 us: body(): jnp.einsum('brk,bkp->brp', leaf_field, out_basis, preferred_element_type=...]
    gather x3 -> x0, local copies, waits for them, and re-layouts: 17.5 us -> none  [the longest x1 13.3 us: body(): picked = leaf_all[(far_owner * leaf_count + far_local).reshape(-1)]]
    reshape x6 -> x2, local copies, waits for them, and re-layouts: 17 us -> 0.16 us  [the longest x1 0.08 us: body(): (slots(parent_owner, y, z, c) * ROWS + LEAF + parent_index).reshape(-1)]
    unnamed x20 -> x82, local copies, waits for them, and re-layouts: 0.43 us -> 11.2 us
  transfers between devices with their start and end apart: 2 -> 34, of which waited for: 2 -> 5; matrix products, arithmetic and copies ran while one was open for 8% -> 1% of each run, Pallas kernels for 0% -> 3%
where the time goes in v1:
time: 387 us
  Pallas kernels  316 us (82%)
  starting transfers between devices  47.9 us (12%)
  local copies, waits for them, and re-layouts  13.3 us (3%)
  waiting for transfers between devices  8.51 us (2%)
    pallas_call x1, Pallas kernels, assemble(): pl.pallas_call(functools.partial(assemble_kernel, places), in_specs=[pl.B...  296 us
    ppermute x16, starting transfers between devices, send(): return lax.ppermute(x, ('y', 'z', 'c'), pairs(second, mask))  22.5 us
    ppermute x15, starting transfers between devices, other_core(): return lax.ppermute(x, 'c', [(0, 1), (1, 0)])  21.5 us
    unnamed x82, local copies, waits for them, and re-layouts  11.2 us
    pallas_call x1, Pallas kernels, couple(): pl.pallas_call(couple_kernel, grid=(8,), in_specs=[pl.BlockSpec(memory_sp...  9.93 us
  transfers between devices with their start and end apart: 34, of which 5 were waited for; matrix products, arithmetic and copies ran while one was open for 1% of the time, Pallas kernels for 3%

profile of v1, /device:TPU:1, one launch (start us, length us, event | category | flops | bytes accessed | tf_op | source)
XLA Modules:
  0.0 386.6 jit_solution(5417117064244327453)
XLA Ops:
  0.0 1.6 copy-done.1
  1.6 1.2 copy-done.5
  2.8 1.2 copy-done.6
  5.6 4.7 %up.1 = bf16[73,16,128]{2,1,0:T(8,128)(2,1)S(1)} custom-call(s32[64]{0:T(128)S(1)} %copy-done.11, bf16[64,32,256]{2,1,0:T(8,128)(2,1)S(1)} %copy-done.5, bf16[64,64,256]{2,1,0:T(8,128)(2,1)S(1)} %copy-done.1, bf16[64,64,64]{2,1,0:T(8,128)(2,1)S(1)} %copy-done.6, bf16[8,64,64]{2,1,0:T(8,128)(2,1)S(1)} %copy-done.9), custom_call_target="tpu_custom_call" | custom-call | flops 83886080 | bytes 5242880 | tf_op jit(solution)/shard_map/up/pallas_call | solution.py:58
  10.3 3.6 collective-permute-start.9
  13.9 1.6 collective-permute-start.1
  15.6 2.2 collective-permute-start.2
  17.8 1.9 collective-permute-start
  20.2 4.4 %collective-permute-start.4 = (bf16[1,37,16,128]{3,2,1,0:T(8,128)(2,1)S(1)}, bf16[1,37,16,128]{3,2,1,0:T(8,128)(2,1)S(1)}, u32[]{:S(2)}, u32[]{:S(2)}) collective-permute-start(bf16[1,37,16,128]{3,2,1,0:T(8,128)(2,1)S(1)} %slice.32), channel_id=1, source_target_pairs={{0,24},{1,7},{2,26},{3,5},{4,28},{5,3},{6,30},{7,1},{8,16},{9,15},... | collective-permute-start | bytes 454664 | tf_op jit(solution)/shard_map/ppermute | solution.py:89
  25.5 1.0 collective-permute-start.19
  26.5 3.5 collective-permute-start.10
  30.2 3.0 collective-permute-start.22
  33.3 2.1 collective-permute-start.13
  36.2 3.0 collective-permute-start.20
  40.2 1.6 collective-permute-start.15
  41.8 5.1 %collective-permute-done.17.refs_16_ = bf16[1,73,16,128]{3,2,1,0:T(8,128)(2,1)S(1)} collective-permute-done((bf16[1,73,16,128]{3,2,1,0:T(8,128)(2,1)S(1)}, bf16[1,73,16,128]{3,2,1,0:T(8,128)(2,1)S(1)}, u32[]{:S(2)}, u32[]{:S(2)}) %collective-permute-start.17) | collective-permute-done | bytes 299040 | tf_op jit(solution)/shard_map/ppermute | solution.py:89
  46.9 3.3 collective-permute-start.6
  50.2 1.7 collective-permute-start.29
  52.9 1.0 slice.37
  53.9 2.7 collective-permute-start.23
  56.7 1.1 collective-permute-start.30
  57.8 1.3 collective-permute-start.12
  59.9 1.4 collective-permute-done.23.refs_22_
  61.3 1.7 collective-permute-start.24
  63.0 1.5 collective-permute-start.26
  65.4 0.9 collective-permute-done.28.refs_27_
  67.0 295.8 %assemble.1 = (bf16[2336,16,128]{2,1,0:T(8,128)(2,1)}, bf16[32,16,128]{2,1,0:T(8,128)(2,1)}) custom-call(bf16[1,73,16,128]{3,2,1,0:T(8,128)(2,1)} %bitcast.8, bf16[1,73,16,128]{3,2,1,0:T(8,128)(2,1)} %copy-done.21, bf16[2,73,16,128]{3,2,1,0:T(8,128)(2,1)} %copy-done.14, bf16[2,73,16,128]{3,2,1,0:T(8,128)(2,1)} %copy-done.20, ...), custom_call_target="tpu_custom_call" | custom-call | tf_op jit(solution)/shard_map/assemble/pallas_call | solution.py:159
  362.8 1.3 collective-permute-start.31
  364.1 2.4 collective-permute-start.32
  367.0 3.7 copy-done
  370.8 9.9 %couple.1 = (f32[64,32,64]{2,1,0:T(8,128)S(1)}, f32[8,32,64]{2,1,0:T(8,128)S(1)}) custom-call(s32[1024]{0:T(1024)S(1)} %reshape.10.leaf_rows, s32[128]{0:T(128)S(1)} %reshape.11.parent_rows, bf16[2336,16,128]{2,1,0:T(8,128)(2,1)S(1)} %copy-done, bf16[64,16,64,64]{3,2,1,0:T(8,128)(2,1)} %coupling.1, bf16[8,16,64,64]{3,2,1,0:T(8,128)(2,1)S(1)} %copy-done.3), custom_call_target="tpu_custom_call" | custom-call | flops 301989888 | bytes 29360128 | tf_op jit(solution)/shard_map/couple/pallas_call | solution.py:199
  380.9 5.7 %down.1 = bf16[64,32,256]{2,1,0:T(8,128)(2,1)} custom-call(s32[64]{0:T(128)S(1)} %copy-done.12, s32[16]{0:T(128)S(1)} %fusion.16.top_rows, bf16[128,16,128]{2,1,0:T(8,128)(2,1)S(1)} %pad_maximum_fusion.tops, bf16[1,16,64,64]{3,2,1,0:T(8,128)(2,1)S(1)} %copy-done.8, f32[8,32,64]{2,1,0:T(8,128)S(1)} %get-tuple-element.11.parent_far, ...), custom_call_target="tpu_custom_call" | custom-call | flops 83886080 | bytes 6291456 | tf_op jit(solution)/shard_map/down/pallas_call | solution.py:239
  (139 shorter events, 8.8 us)
Async XLA Ops:
  10.3 9.3 %collective-permute-start.9 = (bf16[1,73,16,128]{3,2,1,0:T(8,128)(2,1)S(1)}, bf16[1,73,16,128]{3,2,1,0:T(8,128)(2,1)S(1)}, u32[]{:S(2)}, u32[]{:S(2)}) collective-permute-start(bf16[1,73,16,128]{3,2,1,0:T(8,128)(2,1)S(1)} %bitcast.3), channel_id=1, source_target_pairs={{0,6},{1,25},{2,4},{3,27},{4,2},{5,29},{6,0},{7,31},{8,14},{9,17},... | collective-permute-start | bytes 897032 | tf_op jit(solution)/shard_map/ppermute | solution.py:89
  13.9 6.2 %collective-permute-start.1 = (bf16[1,73,16,128]{3,2,1,0:T(8,128)(2,1)S(1)}, bf16[1,73,16,128]{3,2,1,0:T(8,128)(2,1)S(1)}, u32[]{:S(2)}, u32[]{:S(2)}) collective-permute-start(bf16[1,73,16,128]{3,2,1,0:T(8,128)(2,1)S(1)} %bitcast.4), channel_id=1, source_target_pairs={{0,8},{1,3},{2,10},{3,1},{4,12},{5,7},{6,14},{7,5},{8,0},{9,11},{1... | collective-permute-start | bytes 897032 | tf_op jit(solution)/shard_map/ppermute | solution.py:89
  15.6 9.1 %collective-permute-start.2 = (bf16[1,73,16,128]{3,2,1,0:T(8,128)(2,1)S(1)}, bf16[1,73,16,128]{3,2,1,0:T(8,128)(2,1)S(1)}, u32[]{:S(2)}, u32[]{:S(2)}) collective-permute-start(bf16[1,73,16,128]{3,2,1,0:T(8,128)(2,1)S(1)} %bitcast.5), channel_id=1, source_target_pairs={{0,24},{1,7},{2,26},{3,5},{4,28},{5,3},{6,30},{7,1},{8,16},{9,15},... | collective-permute-start | bytes 897032 | tf_op jit(solution)/shard_map/ppermute | solution.py:89
  17.8 7.7 %collective-permute-start.7 = (bf16[1,73,16,128]{3,2,1,0:T(8,128)(2,1)S(1)}, bf16[1,73,16,128]{3,2,1,0:T(8,128)(2,1)S(1)}, u32[]{:S(2)}, u32[]{:S(2)}) collective-permute-start(bf16[1,73,16,128]{3,2,1,0:T(8,128)(2,1)S(1)} %bitcast.6), channel_id=1, source_target_pairs={{0,2},{1,9},{2,0},{3,11},{4,6},{5,13},{6,4},{7,15},{8,10},{9,1},{1... | collective-permute-start | bytes 897032 | tf_op jit(solution)/shard_map/ppermute | solution.py:89
  17.8 8.7 %collective-permute-start = (bf16[1,73,16,128]{3,2,1,0:T(8,128)(2,1)S(1)}, bf16[1,73,16,128]{3,2,1,0:T(8,128)(2,1)S(1)}, u32[]{:S(2)}, u32[]{:S(2)}) collective-permute-start(bf16[1,73,16,128]{3,2,1,0:T(8,128)(2,1)S(1)} %bitcast.7), channel_id=1, source_target_pairs={{0,1},{1,0},{2,3},{3,2},{4,5},{5,4},{6,7},{7,6},{8,9},{9,8},{10,11... | collective-permute-start | bytes 897032 | tf_op jit(solution)/shard_map/ppermute | solution.py:93
  19.7 10.3 %collective-permute-start.21 = (bf16[1,36,16,128]{3,2,1,0:T(8,128)(2,1)S(1)}, bf16[1,36,16,128]{3,2,1,0:T(8,128)(2,1)S(1)}, u32[]{:S(2)}, u32[]{:S(2)}) collective-permute-start(bf16[1,36,16,128]{3,2,1,0:T(8,128)(2,1)S(1)} %slice.35), channel_id=1, source_target_pairs={{0,2},{1,9},{2,0},{3,11},{4,6},{5,13},{6,4},{7,15},{8,10},{9,1},{1... | collective-permute-start | bytes 442376 | tf_op jit(solution)/shard_map/ppermute | solution.py:89
  20.2 9.9 %collective-permute-start.4 = (bf16[1,37,16,128]{3,2,1,0:T(8,128)(2,1)S(1)}, bf16[1,37,16,128]{3,2,1,0:T(8,128)(2,1)S(1)}, u32[]{:S(2)}, u32[]{:S(2)}) collective-permute-start(bf16[1,37,16,128]{3,2,1,0:T(8,128)(2,1)S(1)} %slice.32), channel_id=1, source_target_pairs={{0,24},{1,7},{2,26},{3,5},{4,28},{5,3},{6,30},{7,1},{8,16},{9,15},... | collective-permute-start | bytes 454664 | tf_op jit(solution)/shard_map/ppermute | solution.py:89
  24.6 8.5 %collective-permute-start.5 = (bf16[1,36,16,128]{3,2,1,0:T(8,128)(2,1)S(1)}, bf16[1,36,16,128]{3,2,1,0:T(8,128)(2,1)S(1)}, u32[]{:S(2)}, u32[]{:S(2)}) collective-permute-start(bf16[1,36,16,128]{3,2,1,0:T(8,128)(2,1)S(1)} %slice.33), channel_id=1, source_target_pairs={{0,8},{1,3},{2,10},{3,1},{4,12},{5,7},{6,14},{7,5},{8,0},{9,11},{1... | collective-permute-start | bytes 442376 | tf_op jit(solution)/shard_map/ppermute | solution.py:89
  25.5 7.8 %collective-permute-start.19 = (bf16[1,37,16,128]{3,2,1,0:T(8,128)(2,1)S(1)}, bf16[1,37,16,128]{3,2,1,0:T(8,128)(2,1)S(1)}, u32[]{:S(2)}, u32[]{:S(2)}) collective-permute-start(bf16[1,37,16,128]{3,2,1,0:T(8,128)(2,1)S(1)} %slice.34), channel_id=1, source_target_pairs={{0,6},{1,25},{2,4},{3,27},{4,2},{5,29},{6,0},{7,31},{8,14},{9,17},... | collective-permute-start | bytes 454664 | tf_op jit(solution)/shard_map/ppermute | solution.py:89
  26.5 9.7 %collective-permute-start.10 = (bf16[1,73,16,128]{3,2,1,0:T(8,128)(2,1)S(1)}, bf16[1,73,16,128]{3,2,1,0:T(8,128)(2,1)S(1)}, u32[]{:S(2)}, u32[]{:S(2)}) collective-permute-start(bf16[1,73,16,128]{3,2,1,0:T(8,128)(2,1)S(1)} %collective-permute-done.9.refs_8_), channel_id=1, source_target_pairs={{0,1},{1,0},{2,3},{3,2},{4,5},{5,4},{6,7},{7,6},{8,9},{9,8},{10,11... | collective-permute-start | bytes 897032 | tf_op jit(solution)/shard_map/ppermute | solution.py:93
  30.0 9.2 %collective-permute-start.8 = (bf16[1,73,16,128]{3,2,1,0:T(8,128)(2,1)S(1)}, bf16[1,73,16,128]{3,2,1,0:T(8,128)(2,1)}, u32[]{:S(2)}, u32[]{:S(2)}) collective-permute-start(bf16[1,73,16,128]{3,2,1,0:T(8,128)(2,1)S(1)} %collective-permute-done.7.refs_6_), channel_id=1, source_target_pairs={{0,1},{1,0},{2,3},{3,2},{4,5},{5,4},{6,7},{7,6},{8,9},{9,8},{10,11... | collective-permute-start | bytes 897032 | tf_op jit(solution)/shard_map/ppermute | solution.py:93
  30.2 5.3 %collective-permute-start.22 = (bf16[1,36,16,128]{3,2,1,0:T(8,128)(2,1)S(1)}, bf16[1,36,16,128]{3,2,1,0:T(8,128)(2,1)S(1)}, u32[]{:S(2)}, u32[]{:S(2)}) collective-permute-start(bf16[1,36,16,128]{3,2,1,0:T(8,128)(2,1)S(1)} %collective-permute-done.21.refs_20_), channel_id=1, source_target_pairs={{0,1},{1,0},{2,3},{3,2},{4,5},{5,4},{6,7},{7,6},{8,9},{9,8},{10,11... | collective-permute-start | bytes 442376 | tf_op jit(solution)/shard_map/ppermute | solution.py:93
  33.2 18.7 %collective-permute-start.11 = (bf16[2,73,16,128]{3,2,1,0:T(8,128)(2,1)S(1)}, bf16[2,73,16,128]{3,2,1,0:T(8,128)(2,1)S(1)}, u32[]{:S(2)}, u32[]{:S(2)}) collective-permute-start(bf16[2,73,16,128]{3,2,1,0:T(8,128)(2,1)S(1)} %constant_dynamic-update-slice_fusion.refs_2_), channel_id=1, source_target_pairs={{0,2},{1,9},{2,0},{3,11},{4,6},{5,13},{6,4},{7,15},{8,10},{9,1},{1... | collective-permute-start | bytes 1794056 | tf_op jit(solution)/shard_map/ppermute | solution.py:89
  33.3 18.8 %collective-permute-start.13 = (bf16[2,73,16,128]{3,2,1,0:T(8,128)(2,1)S(1)}, bf16[2,73,16,128]{3,2,1,0:T(8,128)(2,1)}, u32[]{:S(2)}, u32[]{:S(2)}) collective-permute-start(bf16[2,73,16,128]{3,2,1,0:T(8,128)(2,1)S(1)} %constant_dynamic-update-slice_fusion.refs_2_), channel_id=1, source_target_pairs={{0,6},{1,25},{2,4},{3,27},{4,2},{5,29},{6,0},{7,31},{8,14},{9,17},... | collective-permute-start | bytes 1794056 | tf_op jit(solution)/shard_map/ppermute | solution.py:89
  35.4 11.4 %collective-permute-start.17 = (bf16[1,73,16,128]{3,2,1,0:T(8,128)(2,1)S(1)}, bf16[1,73,16,128]{3,2,1,0:T(8,128)(2,1)S(1)}, u32[]{:S(2)}, u32[]{:S(2)}) collective-permute-start(bf16[1,73,16,128]{3,2,1,0:T(8,128)(2,1)S(1)} %constant_dynamic-update-slice_fusion.2.refs_4_), channel_id=1, source_target_pairs={{0,6},{1,25},{2,4},{3,27},{4,2},{5,29},{6,0},{7,31},{8,14},{9,17},... | collective-permute-start | bytes 897032 | tf_op jit(solution)/shard_map/ppermute | solution.py:89
  36.2 4.0 %collective-permute-start.20 = (bf16[1,37,16,128]{3,2,1,0:T(8,128)(2,1)S(1)}, bf16[1,37,16,128]{3,2,1,0:T(8,128)(2,1)S(1)}, u32[]{:S(2)}, u32[]{:S(2)}) collective-permute-start(bf16[1,37,16,128]{3,2,1,0:T(8,128)(2,1)S(1)} %collective-permute-done.19.refs_18_), channel_id=1, source_target_pairs={{0,1},{1,0},{2,3},{3,2},{4,5},{5,4},{6,7},{7,6},{8,9},{9,8},{10,11... | collective-permute-start | bytes 454664 | tf_op jit(solution)/shard_map/ppermute | solution.py:93
  39.2 17.5 %collective-permute-start.3 = (bf16[2,73,16,128]{3,2,1,0:T(8,128)(2,1)S(1)}, bf16[2,73,16,128]{3,2,1,0:T(8,128)(2,1)S(1)}, u32[]{:S(2)}, u32[]{:S(2)}) collective-permute-start(bf16[2,73,16,128]{3,2,1,0:T(8,128)(2,1)S(1)} %constant_dynamic-update-slice_fusion.refs_2_), channel_id=1, source_target_pairs={{0,1},{1,0},{2,3},{3,2},{4,5},{5,4},{6,7},{7,6},{8,9},{9,8},{10,11... | collective-permute-start | bytes 1794056 | tf_op jit(solution)/shard_map/ppermute | solution.py:93
  40.2 10.0 %collective-permute-start.15 = (bf16[1,73,16,128]{3,2,1,0:T(8,128)(2,1)S(1)}, bf16[1,73,16,128]{3,2,1,0:T(8,128)(2,1)S(1)}, u32[]{:S(2)}, u32[]{:S(2)}) collective-permute-start(bf16[1,73,16,128]{3,2,1,0:T(8,128)(2,1)S(1)} %constant_dynamic-update-slice_fusion.2.refs_4_), channel_id=1, source_target_pairs={{0,2},{1,9},{2,0},{3,11},{4,6},{5,13},{6,4},{7,15},{8,10},{9,1},{1... | collective-permute-start | bytes 897032 | tf_op jit(solution)/shard_map/ppermute | solution.py:89
  46.9 7.0 %collective-permute-start.6 = (bf16[1,73,16,128]{3,2,1,0:T(8,128)(2,1)S(1)}, bf16[1,73,16,128]{3,2,1,0:T(8,128)(2,1)S(1)}, u32[]{:S(2)}, u32[]{:S(2)}) collective-permute-start(bf16[1,73,16,128]{3,2,1,0:T(8,128)(2,1)S(1)} %constant_dynamic-update-slice_fusion.2.refs_4_), channel_id=1, source_target_pairs={{0,1},{1,0},{2,3},{3,2},{4,5},{5,4},{6,7},{7,6},{8,9},{9,8},{10,11... | collective-permute-start | bytes 897032 | tf_op jit(solution)/shard_map/ppermute | solution.py:93
  50.2 6.4 %collective-permute-start.29 = (bf16[1,36,16,128]{3,2,1,0:T(8,128)(2,1)S(1)}, bf16[1,36,16,128]{3,2,1,0:T(8,128)(2,1)S(1)}, u32[]{:S(2)}, u32[]{:S(2)}) collective-permute-start(bf16[1,36,16,128]{3,2,1,0:T(8,128)(2,1)S(1)} %slice.39), channel_id=1, source_target_pairs={{0,2},{1,9},{2,0},{3,11},{4,6},{5,13},{6,4},{7,15},{8,10},{9,1},{1... | collective-permute-start | bytes 442376 | tf_op jit(solution)/shard_map/ppermute | solution.py:89
  51.9 7.9 %collective-permute-start.16 = (bf16[1,73,16,128]{3,2,1,0:T(8,128)(2,1)S(1)}, bf16[1,73,16,128]{3,2,1,0:T(8,128)(2,1)S(1)}, u32[]{:S(2)}, u32[]{:S(2)}) collective-permute-start(bf16[1,73,16,128]{3,2,1,0:T(8,128)(2,1)S(1)} %collective-permute-done.15.refs_14_), channel_id=1, source_target_pairs={{0,1},{1,0},{2,3},{3,2},{4,5},{5,4},{6,7},{7,6},{8,9},{9,8},{10,11... | collective-permute-start | bytes 897032 | tf_op jit(solution)/shard_map/ppermute | solution.py:93
  52.0 5.8 %collective-permute-start.27 = (bf16[1,37,16,128]{3,2,1,0:T(8,128)(2,1)S(1)}, bf16[1,37,16,128]{3,2,1,0:T(8,128)(2,1)}, u32[]{:S(2)}, u32[]{:S(2)}) collective-permute-start(bf16[1,37,16,128]{3,2,1,0:T(8,128)(2,1)S(1)} %slice.38), channel_id=1, source_target_pairs={{0,6},{1,25},{2,4},{3,27},{4,2},{5,29},{6,0},{7,31},{8,14},{9,17},... | collective-permute-start | bytes 454664 | tf_op jit(solution)/shard_map/ppermute | solution.py:89
  53.9 7.4 %collective-permute-start.23 = (bf16[1,73,16,128]{3,2,1,0:T(8,128)(2,1)}, bf16[1,73,16,128]{3,2,1,0:T(8,128)(2,1)S(1)}, u32[]{:S(2)}, u32[]{:S(2)}) collective-permute-start(bf16[1,73,16,128]{3,2,1,0:T(8,128)(2,1)} %slice.36), channel_id=1, source_target_pairs={{0,6},{1,25},{2,4},{3,27},{4,2},{5,29},{6,0},{7,31},{8,14},{9,17},... | collective-permute-start | bytes 897032 | tf_op jit(solution)/shard_map/ppermute | solution.py:89
  56.6 6.4 %collective-permute-start.25 = (bf16[1,73,16,128]{3,2,1,0:T(8,128)(2,1)S(1)}, bf16[1,73,16,128]{3,2,1,0:T(8,128)(2,1)}, u32[]{:S(2)}, u32[]{:S(2)}) collective-permute-start(bf16[1,73,16,128]{3,2,1,0:T(8,128)(2,1)S(1)} %slice.37), channel_id=1, source_target_pairs={{0,2},{1,9},{2,0},{3,11},{4,6},{5,13},{6,4},{7,15},{8,10},{9,1},{1... | collective-permute-start | bytes 897032 | tf_op jit(solution)/shard_map/ppermute | solution.py:89
  57.8 8.5 %collective-permute-start.12 = (bf16[2,73,16,128]{3,2,1,0:T(8,128)(2,1)S(1)}, bf16[2,73,16,128]{3,2,1,0:T(8,128)(2,1)}, u32[]{:S(2)}, u32[]{:S(2)}) collective-permute-start(bf16[2,73,16,128]{3,2,1,0:T(8,128)(2,1)S(1)} %collective-permute-done.11.refs_10_), channel_id=1, source_target_pairs={{0,1},{1,0},{2,3},{3,2},{4,5},{5,4},{6,7},{7,6},{8,9},{9,8},{10,11... | collective-permute-start | bytes 1794056 | tf_op jit(solution)/shard_map/ppermute | solution.py:93
  59.1 7.8 %collective-permute-start.14 = (bf16[2,73,16,128]{3,2,1,0:T(8,128)(2,1)}, bf16[2,73,16,128]{3,2,1,0:T(8,128)(2,1)}, u32[]{:S(2)}, u32[]{:S(2)}) collective-permute-start(bf16[2,73,16,128]{3,2,1,0:T(8,128)(2,1)} %collective-permute-done.13.refs_12_), channel_id=1, source_target_pairs={{0,1},{1,0},{2,3},{3,2},{4,5},{5,4},{6,7},{7,6},{8,9},{9,8},{10,11... | collective-permute-start | bytes 1794056 | tf_op jit(solution)/shard_map/ppermute | solution.py:93
  59.8 4.8 %collective-permute-start.18 = (bf16[1,73,16,128]{3,2,1,0:T(8,128)(2,1)S(1)}, bf16[1,73,16,128]{3,2,1,0:T(8,128)(2,1)S(1)}, u32[]{:S(2)}, u32[]{:S(2)}) collective-permute-start(bf16[1,73,16,128]{3,2,1,0:T(8,128)(2,1)S(1)} %collective-permute-done.17.refs_16_), channel_id=1, source_target_pairs={{0,1},{1,0},{2,3},{3,2},{4,5},{5,4},{6,7},{7,6},{8,9},{9,8},{10,11... | collective-permute-start | bytes 897032 | tf_op jit(solution)/shard_map/ppermute | solution.py:93
  61.3 5.0 %collective-permute-start.24 = (bf16[1,73,16,128]{3,2,1,0:T(8,128)(2,1)S(1)}, bf16[1,73,16,128]{3,2,1,0:T(8,128)(2,1)}, u32[]{:S(2)}, u32[]{:S(2)}) collective-permute-start(bf16[1,73,16,128]{3,2,1,0:T(8,128)(2,1)S(1)} %collective-permute-done.23.refs_22_), channel_id=1, source_target_pairs={{0,1},{1,0},{2,3},{3,2},{4,5},{5,4},{6,7},{7,6},{8,9},{9,8},{10,11... | collective-permute-start | bytes 897032 | tf_op jit(solution)/shard_map/ppermute | solution.py:93
  63.0 3.3 collective-permute-start.26
  362.8 17.9 %collective-permute-start.31 = (bf16[32,16,128]{2,1,0:T(8,128)(2,1)}, bf16[32,16,128]{2,1,0:T(8,128)(2,1)S(1)}, u32[]{:S(2)}, u32[]{:S(2)}) collective-permute-start(bf16[32,16,128]{2,1,0:T(8,128)(2,1)} %get-tuple-element.9), channel_id=1, source_target_pairs={{0,32},{32,0},{64,96},{96,64},{1,33},{33,1},{65,97},{97,65},{2,34}... | collective-permute-start | bytes 393224 | tf_op jit(solution)/shard_map/ppermute | solution.py:287
  364.1 16.6 %collective-permute-start.32 = (bf16[32,16,128]{2,1,0:T(8,128)(2,1)}, bf16[32,16,128]{2,1,0:T(8,128)(2,1)S(1)}, u32[]{:S(2)}, u32[]{:S(2)}) collective-permute-start(bf16[32,16,128]{2,1,0:T(8,128)(2,1)} %get-tuple-element.9), channel_id=1, source_target_pairs={{0,64},{32,96},{64,0},{96,32},{1,65},{33,97},{65,1},{97,33},{2,66}... | collective-permute-start | bytes 393224 | tf_op jit(solution)/shard_map/ppermute | solution.py:287
  366.6 14.2 %collective-permute-start.33 = (bf16[32,16,128]{2,1,0:T(8,128)(2,1)}, bf16[32,16,128]{2,1,0:T(8,128)(2,1)S(1)}, u32[]{:S(2)}, u32[]{:S(2)}) collective-permute-start(bf16[32,16,128]{2,1,0:T(8,128)(2,1)} %get-tuple-element.9), channel_id=1, source_target_pairs={{0,96},{32,64},{64,32},{96,0},{1,97},{33,65},{65,33},{97,1},{2,98}... | collective-permute-start | bytes 393224 | tf_op jit(solution)/shard_map/ppermute | solution.py:287
  (42 other events, 1169.1 us)

commit v2 on v0

v2 whole, which is shorter than its diff:
```python
import functools

import jax
import jax.numpy as jnp
from jax import lax
from jax.experimental import pallas as pl
from jax.experimental.pallas import tpu as pltpu
from jax.sharding import Mesh
from jax.sharding import PartitionSpec as P

BF16 = jnp.bfloat16
F32 = jnp.float32
LEAF, PARENT = 64, 8
ROWS = LEAF + PARENT + 1
NT = (((1,), (1,)), ((), ()))
MIB = 1 << 20


def dot(a, b):
    return jnp.dot(a, b, preferred_element_type=F32)


def pack(c):
    return jnp.concatenate([c[:16], c[16:]], axis=1)


def up_kernel(counts, charges, basis, transfer, parent_transfer, out, live, charge, base, move, lift, sem):
    chunks = 2
    size = LEAF // chunks
    count_copy = pltpu.make_async_copy(counts, live, sem.at[0])
    count_copy.start()
    copies = []
    for k in range(chunks):
        part = pl.ds(k * size, size)
        copies.append(
            [
                pltpu.make_async_copy(charges.at[part], charge.at[part], sem.at[3 + 2 * k]),
                pltpu.make_async_copy(basis.at[part], base.at[part], sem.at[4 + 2 * k]),
            ]
        )
        for copy in copies[k]:
            copy.start()
    transfers = [
        pltpu.make_async_copy(transfer, move, sem.at[1]),
        pltpu.make_async_copy(parent_transfer, lift, sem.at[2]),
    ]
    for copy in transfers:
        copy.start()
    count_copy.wait()
    column = lax.broadcasted_iota(jnp.int32, (32, 256), 1)
    coeffs = []
    for k in range(chunks):
        for copy in copies[k]:
            copy.wait()
        for b in range(k * size, (k + 1) * size):
            masked = jnp.where(column < live[b], charge[b], jnp.zeros((32, 256), BF16))
            coeff = lax.dot_general(masked, base[b], NT, preferred_element_type=F32).astype(BF16)
            out[b] = pack(coeff)
            coeffs.append(coeff)
    for copy in transfers:
        copy.wait()
    parents = []
    for q in range(PARENT):
        family = jnp.concatenate(coeffs[q * 8 : q * 8 + 8], axis=1)
        parents.append(dot(family, move[q * 8 : q * 8 + 8].reshape(512, 64)).astype(BF16))
        out[LEAF + q] = pack(parents[q])
    top = dot(jnp.concatenate(parents, axis=1), lift[...].reshape(512, 64))
    out[ROWS - 1] = pack(top.astype(BF16))


def up(*operands):
    hbm = pl.BlockSpec(memory_space=pltpu.HBM)
    return pl.pallas_call(
        up_kernel,
        in_specs=[hbm] * 5,
        out_specs=pl.BlockSpec(memory_space=pltpu.VMEM),
        out_shape=jax.ShapeDtypeStruct((ROWS, 16, 128), BF16),
        scratch_shapes=[pltpu.SMEM((LEAF,), jnp.int32)]
        + [pltpu.VMEM(x.shape, BF16) for x in operands[1:]]
        + [pltpu.SemaphoreType.DMA((7,))],
        compiler_params=pltpu.CompilerParams(vmem_limit_bytes=8 * MIB),
        cost_estimate=pl.CostEstimate(flops=2 * 64 * 32 * 64 * 320, bytes_accessed=5 * MIB, transcendentals=0),
        name="up",
    )(*operands)


def pairs(second, mask):
    out = []
    for y in range(4):
        for z in range(4):
            for c in range(2):
                along_y = (c == 0) != second
                ty, tz = (y ^ mask, z) if along_y else (y, z ^ mask)
                out.append(((y * 4 + z) * 2 + c, (ty * 4 + tz) * 2 + c))
    return out


def send(x, second, mask):
    return lax.ppermute(x, ("y", "z", "c"), pairs(second, mask))


def other_core(x):
    return lax.ppermute(x, "c", [(0, 1), (1, 0)])


def gather(s):
    s = s[None]
    a, o, b = (send(s, False, m) for m in (1, 2, 3))
    near, far = jnp.concatenate([s, a]), jnp.concatenate([o, b])
    near_a, near_b = send(near, True, 1), send(near, True, 3)
    far_a, far_b = send(far, True, 1), send(far, True, 3)
    near_o, far_o = send(near_a, True, 3), send(far_b, True, 1)
    early = [(near, 0), (far, 2), (near_a, 4), (far_a, 6), (near_b, 12), (far_b, 14)]
    return early, [(near_o, 8), (far_o, 10)]


def early_kernel(firsts, *refs):
    n = len(firsts)
    out, sem = refs[n:]
    copies = []
    for ref, first in zip(refs[:n], firsts):
        for i in range(2):
            spot = out.at[pl.ds((first + i) * ROWS, ROWS)]
            copies.append(pltpu.make_async_copy(ref.at[i], spot, sem.at[len(copies)]))
            copies[-1].start()
    for copy in copies:
        copy.wait()


def assemble_early(pieces):
    n = len(pieces)
    return pl.pallas_call(
        functools.partial(early_kernel, [first for _, first in pieces]),
        in_specs=[pl.BlockSpec(memory_space=pltpu.HBM)] * n,
        out_specs=pl.BlockSpec(memory_space=pltpu.VMEM),
        out_shape=jax.ShapeDtypeStruct((32 * ROWS, 16, 128), BF16),
        scratch_shapes=[pltpu.SemaphoreType.DMA((2 * n,))],
        compiler_params=pltpu.CompilerParams(vmem_limit_bytes=8 * MIB),
        cost_estimate=pl.CostEstimate(flops=0, bytes_accessed=4096, transcendentals=0),
        name="assemble_early",
    )(*[x for x, _ in pieces])


def late_kernel(firsts, *refs):
    out = refs[len(firsts) + 1]
    for ref, first in zip(refs, firsts):
        for i in range(2):
            out[(first + i) * ROWS : (first + i + 1) * ROWS] = ref[i]


def assemble_late(pieces, gathered):
    vmem = pl.BlockSpec(memory_space=pltpu.VMEM)
    n = len(pieces)
    return pl.pallas_call(
        functools.partial(late_kernel, [first for _, first in pieces]),
        in_specs=[vmem] * (n + 1),
        out_specs=vmem,
        out_shape=jax.ShapeDtypeStruct((32 * ROWS, 16, 128), BF16),
        input_output_aliases={n: 0},
        compiler_params=pltpu.CompilerParams(vmem_limit_bytes=8 * MIB),
        cost_estimate=pl.CostEstimate(flops=0, bytes_accessed=4096, transcendentals=0),
        name="assemble_late",
    )(*[x for x, _ in pieces], gathered)


def tops_kernel(firsts, *refs):
    n = len(firsts)
    out, sem = refs[n:]
    copies = []
    for ref, first in zip(refs[:n], firsts):
        for i in range(2):
            copies.append(pltpu.make_async_copy(ref.at[i, ROWS - 1], out.at[first + i], sem.at[len(copies)]))
            copies[-1].start()
    for copy in copies:
        copy.wait()


def column_tops(pieces):
    n = len(pieces)
    return pl.pallas_call(
        functools.partial(tops_kernel, [first for _, first in pieces]),
        in_specs=[pl.BlockSpec(memory_space=pltpu.HBM)] * n,
        out_specs=pl.BlockSpec(memory_space=pltpu.VMEM),
        out_shape=jax.ShapeDtypeStruct((16, 16, 128), BF16),
        scratch_shapes=[pltpu.SemaphoreType.DMA((2 * n,))],
        compiler_params=pltpu.CompilerParams(vmem_limit_bytes=4 * MIB),
        cost_estimate=pl.CostEstimate(flops=0, bytes_accessed=4096, transcendentals=0),
        name="tops",
    )(*[x for x, _ in pieces])


def slots(owner, y, z, c):
    oy, oz, oc = owner // 8, owner // 2 % 4, owner % 2
    ry, rz = oy ^ y, oz ^ z
    return (oc ^ c) * 16 + jnp.where(oc == 0, rz * 4 + ry, ry * 4 + rz)


def picked(load, entries):
    lane = lax.broadcasted_iota(jnp.int32, (16, 128), 1) < 64
    low, high = [], []
    for j in range(0, entries, 2):
        a, b = load(j), load(j + 1)
        low.append(jnp.where(lane, a, jnp.concatenate([b[:, 64:], b[:, :64]], axis=1)))
        high.append(jnp.where(lane, jnp.concatenate([a[:, 64:], a[:, :64]], axis=1), b))
    return jnp.concatenate([jnp.concatenate(low, axis=1), jnp.concatenate(high, axis=1)], axis=0)


def couple_kernel(
    place,
    far_owner,
    far_local,
    parent_owner,
    parent_index,
    gathered,
    coupling,
    parent_coupling,
    leaf_far,
    parent_far,
    leaf_rows,
    parent_rows,
    leaf_named,
    parent_named,
    sem,
):
    y, z, c = place[1], place[2], place[3]
    leaf_rows[...] = slots(far_owner[...], y, z, c) * ROWS + far_local[...]
    parent_rows[...] = slots(parent_owner[...], y, z, c) * ROWS + LEAF + parent_index[...]
    copies = [
        pltpu.make_async_copy(leaf_rows, leaf_named, sem.at[0]),
        pltpu.make_async_copy(parent_rows, parent_named, sem.at[1]),
    ]
    for copy in copies:
        copy.start()
    for copy in copies:
        copy.wait()

    def leaf(b, _):
        block = picked(lambda j: gathered[leaf_named[j, b]], 16)
        leaf_far[b] = dot(block, coupling[b].reshape(1024, 64))
        return 0

    def parent(q, _):
        block = picked(lambda j: gathered[parent_named[q, j]], 16)
        parent_far[q] = dot(block, parent_coupling[q].reshape(1024, 64))
        return 0

    lax.fori_loop(0, LEAF, leaf, 0, unroll=16)
    lax.fori_loop(0, PARENT, parent, 0, unroll=8)


def couple(place, far_owner, far_local, parent_owner, parent_index, gathered, coupling, parent_coupling):
    smem, vmem = pl.BlockSpec(memory_space=pltpu.SMEM), pl.BlockSpec(memory_space=pltpu.VMEM)
    return pl.pallas_call(
        couple_kernel,
        in_specs=[smem] + [vmem] * 7,
        out_specs=[vmem, vmem],
        out_shape=[jax.ShapeDtypeStruct((LEAF, 32, 64), F32), jax.ShapeDtypeStruct((PARENT, 32, 64), F32)],
        scratch_shapes=[
            pltpu.VMEM(far_owner.shape, jnp.int32),
            pltpu.VMEM(parent_owner.shape, jnp.int32),
            pltpu.SMEM(far_owner.shape, jnp.int32),
            pltpu.SMEM(parent_owner.shape, jnp.int32),
            pltpu.SemaphoreType.DMA((2,)),
        ],
        compiler_params=pltpu.CompilerParams(vmem_limit_bytes=4 * MIB),
        cost_estimate=pl.CostEstimate(flops=2 * 72 * 32 * 64 * 1024, bytes_accessed=28 * MIB, transcendentals=0),
        name="couple",
    )(place, far_owner, far_local, parent_owner, parent_index, gathered, coupling, parent_coupling)


def down_kernel(
    counts, place, top_source, tops, top_coupling, parent_far, parent_descend, leaf_far, leaf_descend, out_basis, out, values, sem
):
    x, y, z, c = (place[i] for i in range(4))

    def top(j):
        source = top_source[0, j]
        slot = slots(source % 32, y, z, c)
        return tops[slot // 16 * 64 + ((source // 32) ^ x) * 16 + slot % 16]

    block = picked(top, 16)
    top_field = dot(block, top_coupling[0].reshape(1024, 64)).astype(BF16)
    column = lax.broadcasted_iota(jnp.int32, (32, 256), 1)
    parents = [(parent_far[q] + dot(top_field, parent_descend[q])).astype(BF16) for q in range(PARENT)]
    copies = []
    for q in range(PARENT):
        for b in range(q * 8, q * 8 + 8):
            field = (leaf_far[b] + dot(parents[q], leaf_descend[b])).astype(BF16)
            value = dot(field, out_basis[b])
            values[b] = jnp.where(column < counts[b], value, jnp.zeros_like(value)).astype(BF16)
        part = pl.ds(q * 8, 8)
        copies.append(pltpu.make_async_copy(values.at[part], out.at[part], sem.at[q]))
        copies[q].start()
    for copy in copies:
        copy.wait()


def down(counts, place, top_source, *operands):
    smem, vmem = pl.BlockSpec(memory_space=pltpu.SMEM), pl.BlockSpec(memory_space=pltpu.VMEM)
    return pl.pallas_call(
        down_kernel,
        in_specs=[smem] * 3 + [vmem] * len(operands),
        out_specs=pl.BlockSpec(memory_space=pltpu.HBM),
        out_shape=jax.ShapeDtypeStruct((64, 32, 256), BF16),
        scratch_shapes=[pltpu.VMEM((64, 32, 256), BF16), pltpu.SemaphoreType.DMA((PARENT,))],
        compiler_params=pltpu.CompilerParams(vmem_limit_bytes=4 * MIB),
        cost_estimate=pl.CostEstimate(flops=2 * 64 * 32 * 64 * 320, bytes_accessed=6 * MIB, transcendentals=0),
        name="down",
    )(counts, place, top_source, *operands)


def body(
    charges,
    counts,
    leaf_basis,
    out_basis,
    leaf_transfer,
    leaf_descend,
    parent_transfer,
    parent_descend,
    leaf_coupling,
    far_owner,
    far_local,
    parent_coupling,
    parent_owner,
    parent_index,
    top_coupling,
    top_source,
):
    x, y, z, c = (lax.axis_index(a) for a in "xyzc")
    place = jnp.stack([x, y, z, c]).astype(jnp.int32)
    place, charges = lax.optimization_barrier((place, charges))

    hbm = lambda a: pltpu.with_memory_space_constraint(a, pltpu.HBM)
    coeffs = up(*map(hbm, (counts, charges, leaf_basis, leaf_transfer, parent_transfer)))
    early, late = gather(coeffs)
    swap = lambda pieces: [(other_core(piece), 16 + first) for piece, first in pieces]
    gathered = assemble_early(early + swap(early))
    gathered = assemble_late(late + swap(late), gathered)
    tops = column_tops(early + late)
    planes = [tops] + [lax.ppermute(tops, "x", [(i, i ^ m) for i in range(4)]) for m in (1, 2, 3)]

    names = (far_owner.T, far_local.T, parent_owner, parent_index)
    leaf_far, parent_far = couple(place, *names, gathered, leaf_coupling, parent_coupling)
    planes, leaf_far = lax.optimization_barrier((planes, leaf_far))
    tops = jnp.concatenate(planes)
    tops = jnp.concatenate([tops, other_core(tops)])
    return down(
        counts, place, top_source, tops, top_coupling, parent_far, parent_descend, leaf_far, leaf_descend, out_basis
    )


def solution(mesh):
    fine = Mesh(mesh.devices.reshape(4, 4, 4, 2), ("x", "y", "z", "c"))
    spec = P(("x", "y", "z", "c"))
    return jax.shard_map(body, mesh=fine, in_specs=(spec,) * 16, out_specs=spec, check_vma=False)
```

time: 160 us -> 66.2 us (0.41)
  blocking collectives: 39.7 us -> 0 us
  waiting for transfers between devices: 49 us -> 17.4 us
  local copies, waits for them, and re-layouts: 35.2 us -> 4.78 us
  starting transfers between devices: 0.08 us -> 30.3 us
  matrix products: 20.7 us -> 0 us
  between operations: 13.6 us -> 0.32 us
  Pallas kernels: 0 us -> 13.2 us
    all_gather x2 -> x0, waiting for transfers between devices: 48.9 us -> none  [the longest x1 45 us: body(): leaf_all = lax.all_gather(leaf_flat, 'box', axis=0, tiled=True)]
    all_gather x1 -> x0, blocking collectives: 39.7 us -> none  [body(): lax.all_gather(top_coeff.reshape(top_coeff.shape[0], -1), ('leaf', 'box')...]
    ppermute x0 -> x21, starting transfers between devices: none -> 30.3 us  [the longest x9 14.3 us: other_core(): return lax.ppermute(x, 'c', [(0, 1), (1, 0)])]
    dot_general x7 -> x0, matrix products: 20.7 us -> none  [the longest x1 12.4 us: body(): jnp.einsum('brk,bkp->brp', leaf_field, out_basis, preferred_element_type=...]
    gather x3 -> x0, local copies, waits for them, and re-layouts: 17.5 us -> none  [the longest x1 13.3 us: body(): picked = leaf_all[(far_owner * leaf_count + far_local).reshape(-1)]]
    ppermute x0 -> x21, waiting for transfers between devices: none -> 17.4 us  [the longest x9 16.2 us: send(): return lax.ppermute(x, ('y', 'z', 'c'), pairs(second, mask))]
    reshape x6 -> x0, local copies, waits for them, and re-layouts: 17 us -> none  [the longest x2 14.9 us: couple_picked(): blocks = picked.reshape(targets, slot_count, vectors, skeleton)]
    pallas_call x0 -> x6, Pallas kernels: none -> 13.2 us  [the longest x1 5.24 us: couple(): pl.pallas_call(couple_kernel, in_specs=[smem] + [vmem] * 7, out_specs=[vm...]
  transfers between devices with their start and end apart: 2 -> 21, of which waited for: 2 -> 8; matrix products, arithmetic and copies ran while one was open for 8% -> 0% of each run, Pallas kernels for 0% -> 11%
where the time goes in v2:
time: 66.2 us; the launch traced here: 66.1 us
  starting transfers between devices  30.3 us (46%)
  waiting for transfers between devices  17.4 us (26%)
  Pallas kernels  13.2 us (20%)
  local copies, waits for them, and re-layouts  4.78 us (7%)
    ppermute x9, waiting for transfers between devices, send(): return lax.ppermute(x, ('y', 'z', 'c'), pairs(second, mask))  16.2 us
    ppermute x9, starting transfers between devices, other_core(): return lax.ppermute(x, 'c', [(0, 1), (1, 0)])  14.3 us
    ppermute x9, starting transfers between devices, send(): return lax.ppermute(x, ('y', 'z', 'c'), pairs(second, mask))  12.6 us
    pallas_call x1, Pallas kernels, couple(): pl.pallas_call(couple_kernel, in_specs=[smem] + [vmem] * 7, out_specs=[vm...  5.24 us
    unnamed x35, local copies, waits for them, and re-layouts  4.71 us
    ppermute x3, starting transfers between devices, body(): lax.ppermute(tops, 'x', [(i, i ^ m) for i in range(4)])  3.33 us
    pallas_call x1, Pallas kernels, up(): pl.pallas_call(up_kernel, in_specs=[hbm] * 5, out_specs=pl.BlockSpec(memo...  2.98 us
    pallas_call x1, Pallas kernels, down(): pl.pallas_call(down_kernel, in_specs=[smem] * 3 + [vmem] * len(operands),...  2.79 us
  transfers between devices with their start and end apart: 21, of which 8 were waited for; matrix products, arithmetic and copies ran while one was open for 0% of the time, Pallas kernels for 11%

profile of v2, /device:TPU:1, one launch (start us, length us, event | category | flops | bytes accessed | tf_op | source)
XLA Modules:
  0.0 66.1 jit_solution(11929063710314045043)
XLA Ops:
  0.1 3.0 %up.1 = bf16[73,16,128]{2,1,0:T(8,128)(2,1)S(1)} custom-call(s32[64]{0:T(128)} %counts.3, bf16[64,32,256]{2,1,0:T(8,128)(2,1)} %charges, bf16[64,64,256]{2,1,0:T(8,128)(2,1)} %basis.1, bf16[64,64,64]{2,1,0:T(8,128)(2,1)} %transfer.1, bf16[8,64,64]{2,1,0:T(8,128)(2,1)} %parent_transfer.1), custom_call_target="tpu_custom_call" | custom-call | flops 83886080 | bytes 5242880 | tf_op jit(solution)/shard_map/up/pallas_call | solution.py:73
  3.1 2.5 %collective-permute-start = (bf16[1,73,16,128]{3,2,1,0:T(8,128)(2,1)S(1)}, bf16[1,73,16,128]{3,2,1,0:T(8,128)(2,1)S(1)}, u32[]{:S(2)}, u32[]{:S(2)}) collective-permute-start(bf16[1,73,16,128]{3,2,1,0:T(8,128)(2,1)S(1)} %bitcast.9), channel_id=1, source_target_pairs={{0,8},{1,3},{2,10},{3,1},{4,12},{5,7},{6,14},{7,5},{8,0},{9,11},{1... | collective-permute-start | bytes 897032 | tf_op jit(solution)/shard_map/ppermute | solution.py:99
  5.6 3.3 %collective-permute-start.1 = (bf16[1,73,16,128]{3,2,1,0:T(8,128)(2,1)S(1)}, bf16[1,73,16,128]{3,2,1,0:T(8,128)(2,1)S(1)}, u32[]{:S(2)}, u32[]{:S(2)}) collective-permute-start(bf16[1,73,16,128]{3,2,1,0:T(8,128)(2,1)S(1)} %bitcast.10), channel_id=1, source_target_pairs={{0,16},{1,5},{2,18},{3,7},{4,20},{5,1},{6,22},{7,3},{8,24},{9,13},... | collective-permute-start | bytes 897032 | tf_op jit(solution)/shard_map/ppermute | solution.py:99
  8.9 1.1 %collective-permute-done = bf16[1,73,16,128]{3,2,1,0:T(8,128)(2,1)S(1)} collective-permute-done((bf16[1,73,16,128]{3,2,1,0:T(8,128)(2,1)S(1)}, bf16[1,73,16,128]{3,2,1,0:T(8,128)(2,1)S(1)}, u32[]{:S(2)}, u32[]{:S(2)}) %collective-permute-start) | collective-permute-done | bytes 299040 | tf_op jit(solution)/shard_map/ppermute | solution.py:99
  10.1 1.3 %collective-permute-start.14 = (bf16[2,73,16,128]{3,2,1,0:T(8,128)(2,1)S(1)}, bf16[2,73,16,128]{3,2,1,0:T(8,128)(2,1)S(1)}, u32[]{:S(2)}, u32[]{:S(2)}) collective-permute-start(bf16[2,73,16,128]{3,2,1,0:T(8,128)(2,1)S(1)} %pad_maximum_fusion.refs_0_), channel_id=1, source_target_pairs={{0,1},{1,0},{2,3},{3,2},{4,5},{5,4},{6,7},{7,6},{8,9},{9,8},{10,11... | collective-permute-start | bytes 1794056 | tf_op jit(solution)/shard_map/ppermute | solution.py:103
  11.5 2.8 %collective-permute-start.5 = (bf16[2,73,16,128]{3,2,1,0:T(8,128)(2,1)S(1)}, bf16[2,73,16,128]{3,2,1,0:T(8,128)(2,1)S(1)}, u32[]{:S(2)}, u32[]{:S(2)}) collective-permute-start(bf16[2,73,16,128]{3,2,1,0:T(8,128)(2,1)S(1)} %pad_maximum_fusion.refs_0_), channel_id=1, source_target_pairs={{0,6},{1,25},{2,4},{3,27},{4,2},{5,29},{6,0},{7,31},{8,14},{9,17},... | collective-permute-start | bytes 1794056 | tf_op jit(solution)/shard_map/ppermute | solution.py:99
  14.3 2.3 %collective-permute-done.1 = bf16[1,73,16,128]{3,2,1,0:T(8,128)(2,1)S(1)} collective-permute-done((bf16[1,73,16,128]{3,2,1,0:T(8,128)(2,1)S(1)}, bf16[1,73,16,128]{3,2,1,0:T(8,128)(2,1)S(1)}, u32[]{:S(2)}, u32[]{:S(2)}) %collective-permute-start.1) | collective-permute-done | bytes 299040 | tf_op jit(solution)/shard_map/ppermute | solution.py:99
  16.6 4.9 %collective-permute-done.2 = bf16[1,73,16,128]{3,2,1,0:T(8,128)(2,1)S(1)} collective-permute-done((bf16[1,73,16,128]{3,2,1,0:T(8,128)(2,1)S(1)}, bf16[1,73,16,128]{3,2,1,0:T(8,128)(2,1)S(1)}, u32[]{:S(2)}, u32[]{:S(2)}) %collective-permute-start.2) | collective-permute-done | bytes 299040 | tf_op jit(solution)/shard_map/ppermute | solution.py:99
  21.6 2.8 %collective-permute-start.6 = (bf16[2,73,16,128]{3,2,1,0:T(8,128)(2,1)S(1)}, bf16[2,73,16,128]{3,2,1,0:T(8,128)(2,1)S(1)}, u32[]{:S(2)}, u32[]{:S(2)}) collective-permute-start(bf16[2,73,16,128]{3,2,1,0:T(8,128)(2,1)S(1)} %constant_dynamic-update-slice_fusion.refs_1_), channel_id=1, source_target_pairs={{0,6},{1,25},{2,4},{3,27},{4,2},{5,29},{6,0},{7,31},{8,14},{9,17},... | collective-permute-start | bytes 1794056 | tf_op jit(solution)/shard_map/ppermute | solution.py:99
  24.4 3.1 %collective-permute-start.15 = (bf16[2,73,16,128]{3,2,1,0:T(8,128)(2,1)S(1)}, bf16[2,73,16,128]{3,2,1,0:T(8,128)(2,1)S(1)}, u32[]{:S(2)}, u32[]{:S(2)}) collective-permute-start(bf16[2,73,16,128]{3,2,1,0:T(8,128)(2,1)S(1)} %constant_dynamic-update-slice_fusion.refs_1_), channel_id=1, source_target_pairs={{0,1},{1,0},{2,3},{3,2},{4,5},{5,4},{6,7},{7,6},{8,9},{9,8},{10,11... | collective-permute-start | bytes 1794056 | tf_op jit(solution)/shard_map/ppermute | solution.py:103
  27.7 1.1 %collective-permute-start.7 = (bf16[2,73,16,128]{3,2,1,0:T(8,128)(2,1)S(1)}, bf16[2,73,16,128]{3,2,1,0:T(8,128)(2,1)S(1)}, u32[]{:S(2)}, u32[]{:S(2)}) collective-permute-start(bf16[2,73,16,128]{3,2,1,0:T(8,128)(2,1)S(1)} %collective-permute-done.3.refs_2_), channel_id=1, source_target_pairs={{0,6},{1,25},{2,4},{3,27},{4,2},{5,29},{6,0},{7,31},{8,14},{9,17},... | collective-permute-start | bytes 1794056 | tf_op jit(solution)/shard_map/ppermute | solution.py:99
  28.8 3.9 %collective-permute-done.6.refs_5_ = bf16[2,73,16,128]{3,2,1,0:T(8,128)(2,1)S(1)} collective-permute-done((bf16[2,73,16,128]{3,2,1,0:T(8,128)(2,1)S(1)}, bf16[2,73,16,128]{3,2,1,0:T(8,128)(2,1)S(1)}, u32[]{:S(2)}, u32[]{:S(2)}) %collective-permute-start.6) | collective-permute-done | bytes 598048 | tf_op jit(solution)/shard_map/ppermute | solution.py:99
  32.7 2.8 %collective-permute-start.16 = (bf16[2,73,16,128]{3,2,1,0:T(8,128)(2,1)S(1)}, bf16[2,73,16,128]{3,2,1,0:T(8,128)(2,1)S(1)}, u32[]{:S(2)}, u32[]{:S(2)}) collective-permute-start(bf16[2,73,16,128]{3,2,1,0:T(8,128)(2,1)S(1)} %collective-permute-done.3.refs_2_), channel_id=1, source_target_pairs={{0,1},{1,0},{2,3},{3,2},{4,5},{5,4},{6,7},{7,6},{8,9},{9,8},{10,11... | collective-permute-start | bytes 1794056 | tf_op jit(solution)/shard_map/ppermute | solution.py:103
  35.5 1.2 %collective-permute-done.4.refs_3_ = bf16[2,73,16,128]{3,2,1,0:T(8,128)(2,1)S(1)} collective-permute-done((bf16[2,73,16,128]{3,2,1,0:T(8,128)(2,1)S(1)}, bf16[2,73,16,128]{3,2,1,0:T(8,128)(2,1)S(1)}, u32[]{:S(2)}, u32[]{:S(2)}) %collective-permute-start.4) | collective-permute-done | bytes 598048 | tf_op jit(solution)/shard_map/ppermute | solution.py:99
  36.7 0.9 %collective-permute-start.19 = (bf16[2,73,16,128]{3,2,1,0:T(8,128)(2,1)S(1)}, bf16[2,73,16,128]{3,2,1,0:T(8,128)(2,1)S(1)}, u32[]{:S(2)}, u32[]{:S(2)}) collective-permute-start(bf16[2,73,16,128]{3,2,1,0:T(8,128)(2,1)S(1)} %collective-permute-done.6.refs_5_), channel_id=1, source_target_pairs={{0,1},{1,0},{2,3},{3,2},{4,5},{5,4},{6,7},{7,6},{8,9},{9,8},{10,11... | collective-permute-start | bytes 1794056 | tf_op jit(solution)/shard_map/ppermute | solution.py:103
  37.5 1.6 %collective-permute-done.7.refs_6_.refs_0_ = bf16[2,73,16,128]{3,2,1,0:T(8,128)(2,1)S(1)} collective-permute-done((bf16[2,73,16,128]{3,2,1,0:T(8,128)(2,1)S(1)}, bf16[2,73,16,128]{3,2,1,0:T(8,128)(2,1)S(1)}, u32[]{:S(2)}, u32[]{:S(2)}) %collective-permute-start.7) | collective-permute-done | bytes 598048 | tf_op jit(solution)/shard_map/ppermute | solution.py:99
  39.1 2.8 %collective-permute-start.12 = (bf16[2,73,16,128]{3,2,1,0:T(8,128)(2,1)S(1)}, bf16[2,73,16,128]{3,2,1,0:T(8,128)(2,1)S(1)}, u32[]{:S(2)}, u32[]{:S(2)}) collective-permute-start(bf16[2,73,16,128]{3,2,1,0:T(8,128)(2,1)S(1)} %collective-permute-done.7.refs_6_.refs_0_), channel_id=1, source_target_pairs={{0,1},{1,0},{2,3},{3,2},{4,5},{5,4},{6,7},{7,6},{8,9},{9,8},{10,11... | collective-permute-start | bytes 1794056 | tf_op jit(solution)/shard_map/ppermute | solution.py:103
  41.9 1.2 %collective-permute-done.8.refs_7_.refs_1_ = bf16[2,73,16,128]{3,2,1,0:T(8,128)(2,1)S(1)} collective-permute-done((bf16[2,73,16,128]{3,2,1,0:T(8,128)(2,1)S(1)}, bf16[2,73,16,128]{3,2,1,0:T(8,128)(2,1)S(1)}, u32[]{:S(2)}, u32[]{:S(2)}) %collective-permute-start.8) | collective-permute-done | bytes 598048 | tf_op jit(solution)/shard_map/ppermute | solution.py:99
  43.1 2.4 %collective-permute-start.13 = (bf16[2,73,16,128]{3,2,1,0:T(8,128)(2,1)S(1)}, bf16[2,73,16,128]{3,2,1,0:T(8,128)(2,1)S(1)}, u32[]{:S(2)}, u32[]{:S(2)}) collective-permute-start(bf16[2,73,16,128]{3,2,1,0:T(8,128)(2,1)S(1)} %collective-permute-done.8.refs_7_.refs_1_), channel_id=1, source_target_pairs={{0,1},{1,0},{2,3},{3,2},{4,5},{5,4},{6,7},{7,6},{8,9},{9,8},{10,11... | collective-permute-start | bytes 1794056 | tf_op jit(solution)/shard_map/ppermute | solution.py:103
  45.5 0.2 tops.1
  45.7 2.6 %collective-permute-start.11 = (bf16[16,16,128]{2,1,0:T(8,128)(2,1)S(1)}, bf16[16,16,128]{2,1,0:T(8,128)(2,1)S(1)}, u32[]{:S(2)}, u32[]{:S(2)}) collective-permute-start(bf16[16,16,128]{2,1,0:T(8,128)(2,1)S(1)} %tops.1), channel_id=1, source_target_pairs={{0,96},{32,64},{64,32},{96,0},{1,97},{33,65},{65,33},{97,1},{2,98}... | collective-permute-start | bytes 196616 | tf_op jit(solution)/shard_map/ppermute | solution.py:341
  48.3 0.5 collective-permute-start.10
  48.8 0.3 collective-permute-start.9
  49.1 1.8 %assemble_early.1.refs_4_ = bf16[2336,16,128]{2,1,0:T(8,128)(2,1)S(1)} custom-call(bf16[2,73,16,128]{3,2,1,0:T(8,128)(2,1)S(1)} %pad_maximum_fusion.refs_0_, bf16[2,73,16,128]{3,2,1,0:T(8,128)(2,1)S(1)} %constant_dynamic-update-slice_fusion.refs_1_, bf16[2,73,16,128]{3,2,1,0:T(8,128)(2,1)S(1)} %collective-permute-done.3.refs_2_, ...), custom_call_target="tpu_custom_call" | custom-call | bytes 4096 | tf_op jit(solution)/shard_map/assemble_early/pallas_call | solution.py:132
  51.3 1.3 %slice-done.1 = s8[4194304]{0:T(1024)(128)(4,1)S(1)} async-done(((s8[16777216]{0:T(1024)(128)(4,1)}), s8[4194304]{0:T(1024)(128)(4,1)S(1)}, s32[]{:S(2)}) %slice-start.1) | async-done | bytes 4194328
  52.5 1.4 %slice-done.2 = s8[4194304]{0:T(1024)(128)(4,1)S(1)} async-done(((s8[16777216]{0:T(1024)(128)(4,1)}), s8[4194304]{0:T(1024)(128)(4,1)S(1)}, s32[]{:S(2)}) %slice-start.2) | async-done | bytes 4194328
  53.9 1.2 %slice-done.3 = s8[4194304]{0:T(1024)(128)(4,1)S(1)} async-done(((s8[16777216]{0:T(1024)(128)(4,1)}), s8[4194304]{0:T(1024)(128)(4,1)S(1)}, s32[]{:S(2)}) %slice-start.3) | async-done | bytes 4194328
  55.1 0.6 copy-done.1
  55.8 5.2 %couple.1 = (f32[64,32,64]{2,1,0:T(8,128)S(1)}, f32[8,32,64]{2,1,0:T(8,128)S(1)}) custom-call(s32[4]{0:T(128)S(1)} %pad_add_fusion.place, s32[16,64]{1,0:T(8,128)S(1)} %bitcast.13, s32[16,64]{1,0:T(8,128)S(1)} %bitcast.14, s32[8,16]{1,0:T(8,128)S(1)} %copy-done.7, s32[8,16]{1,0:T(8,128)S(1)} %copy-done.8, bf16[2336,16,128]{2,1,0:T(8,128)(2,1)S(1)} %assemble_late.1.gathered, ...), custom_call_target="tpu_custom_call" | custom-call | flops 301989888 | bytes 29360128 | tf_op jit(solution)/shard_map/couple/pallas_call | solution.py:253
  61.2 0.9 %collective-permute-start.20 = (bf16[64,16,128]{2,1,0:T(8,128)(2,1)S(1)}, bf16[64,16,128]{2,1,0:T(8,128)(2,1)S(1)}, u32[]{:S(2)}, u32[]{:S(2)}) collective-permute-start(bf16[64,16,128]{2,1,0:T(8,128)(2,1)S(1)} %pad_maximum_fusion.1), channel_id=1, source_target_pairs={{0,1},{1,0},{2,3},{3,2},{4,5},{5,4},{6,7},{7,6},{8,9},{9,8},{10,11... | collective-permute-start | bytes 786440 | tf_op jit(solution)/shard_map/ppermute | solution.py:103
  62.1 1.1 %collective-permute-done.20 = bf16[64,16,128]{2,1,0:T(8,128)(2,1)S(1)} collective-permute-done((bf16[64,16,128]{2,1,0:T(8,128)(2,1)S(1)}, bf16[64,16,128]{2,1,0:T(8,128)(2,1)S(1)}, u32[]{:S(2)}, u32[]{:S(2)}) %collective-permute-start.20) | collective-permute-done | bytes 262176 | tf_op jit(solution)/shard_map/ppermute | solution.py:103
  63.3 2.8 %down.1 = bf16[64,32,256]{2,1,0:T(8,128)(2,1)} custom-call(s32[64]{0:T(128)S(1)} %copy-done.9, s32[4]{0:T(128)S(1)} %pad_add_fusion.place, s32[1,16]{1,0:T(1,128)S(1)} %copy-done.10, bf16[128,16,128]{2,1,0:T(8,128)(2,1)S(1)} %constant_dynamic-update-slice_fusion.2.tops, bf16[1,16,64,64]{3,2,1,0:T(8,128)(2,1)S(1)} %copy-done.3, ...), custom_call_target="tpu_custom_call" | custom-call | flops 83886080 | bytes 6291456 | tf_op jit(solution)/shard_map/down/pallas_call | solution.py:300
  (57 shorter events, 0.8 us)
Async XLA Ops:
  3.1 7.0 %collective-permute-start = (bf16[1,73,16,128]{3,2,1,0:T(8,128)(2,1)S(1)}, bf16[1,73,16,128]{3,2,1,0:T(8,128)(2,1)S(1)}, u32[]{:S(2)}, u32[]{:S(2)}) collective-permute-start(bf16[1,73,16,128]{3,2,1,0:T(8,128)(2,1)S(1)} %bitcast.9), channel_id=1, source_target_pairs={{0,8},{1,3},{2,10},{3,1},{4,12},{5,7},{6,14},{7,5},{8,0},{9,11},{1... | collective-permute-start | bytes 897032 | tf_op jit(solution)/shard_map/ppermute | solution.py:99
  5.6 11.0 %collective-permute-start.1 = (bf16[1,73,16,128]{3,2,1,0:T(8,128)(2,1)S(1)}, bf16[1,73,16,128]{3,2,1,0:T(8,128)(2,1)S(1)}, u32[]{:S(2)}, u32[]{:S(2)}) collective-permute-start(bf16[1,73,16,128]{3,2,1,0:T(8,128)(2,1)S(1)} %bitcast.10), channel_id=1, source_target_pairs={{0,16},{1,5},{2,18},{3,7},{4,20},{5,1},{6,22},{7,3},{8,24},{9,13},... | collective-permute-start | bytes 897032 | tf_op jit(solution)/shard_map/ppermute | solution.py:99
  8.9 12.7 %collective-permute-start.2 = (bf16[1,73,16,128]{3,2,1,0:T(8,128)(2,1)S(1)}, bf16[1,73,16,128]{3,2,1,0:T(8,128)(2,1)S(1)}, u32[]{:S(2)}, u32[]{:S(2)}) collective-permute-start(bf16[1,73,16,128]{3,2,1,0:T(8,128)(2,1)S(1)} %bitcast.11), channel_id=1, source_target_pairs={{0,24},{1,7},{2,26},{3,5},{4,28},{5,3},{6,30},{7,1},{8,16},{9,15},... | collective-permute-start | bytes 897032 | tf_op jit(solution)/shard_map/ppermute | solution.py:99
  10.1 17.4 %collective-permute-start.14 = (bf16[2,73,16,128]{3,2,1,0:T(8,128)(2,1)S(1)}, bf16[2,73,16,128]{3,2,1,0:T(8,128)(2,1)S(1)}, u32[]{:S(2)}, u32[]{:S(2)}) collective-permute-start(bf16[2,73,16,128]{3,2,1,0:T(8,128)(2,1)S(1)} %pad_maximum_fusion.refs_0_), channel_id=1, source_target_pairs={{0,1},{1,0},{2,3},{3,2},{4,5},{5,4},{6,7},{7,6},{8,9},{9,8},{10,11... | collective-permute-start | bytes 1794056 | tf_op jit(solution)/shard_map/ppermute | solution.py:103
  11.5 16.1 %collective-permute-start.5 = (bf16[2,73,16,128]{3,2,1,0:T(8,128)(2,1)S(1)}, bf16[2,73,16,128]{3,2,1,0:T(8,128)(2,1)S(1)}, u32[]{:S(2)}, u32[]{:S(2)}) collective-permute-start(bf16[2,73,16,128]{3,2,1,0:T(8,128)(2,1)S(1)} %pad_maximum_fusion.refs_0_), channel_id=1, source_target_pairs={{0,6},{1,25},{2,4},{3,27},{4,2},{5,29},{6,0},{7,31},{8,14},{9,17},... | collective-permute-start | bytes 1794056 | tf_op jit(solution)/shard_map/ppermute | solution.py:99
  14.3 13.4 %collective-permute-start.3 = (bf16[2,73,16,128]{3,2,1,0:T(8,128)(2,1)S(1)}, bf16[2,73,16,128]{3,2,1,0:T(8,128)(2,1)S(1)}, u32[]{:S(2)}, u32[]{:S(2)}) collective-permute-start(bf16[2,73,16,128]{3,2,1,0:T(8,128)(2,1)S(1)} %pad_maximum_fusion.refs_0_), channel_id=1, source_target_pairs={{0,2},{1,9},{2,0},{3,11},{4,6},{5,13},{6,4},{7,15},{8,10},{9,1},{1... | collective-permute-start | bytes 1794056 | tf_op jit(solution)/shard_map/ppermute | solution.py:99
  21.6 11.1 %collective-permute-start.6 = (bf16[2,73,16,128]{3,2,1,0:T(8,128)(2,1)S(1)}, bf16[2,73,16,128]{3,2,1,0:T(8,128)(2,1)S(1)}, u32[]{:S(2)}, u32[]{:S(2)}) collective-permute-start(bf16[2,73,16,128]{3,2,1,0:T(8,128)(2,1)S(1)} %constant_dynamic-update-slice_fusion.refs_1_), channel_id=1, source_target_pairs={{0,6},{1,25},{2,4},{3,27},{4,2},{5,29},{6,0},{7,31},{8,14},{9,17},... | collective-permute-start | bytes 1794056 | tf_op jit(solution)/shard_map/ppermute | solution.py:99
  24.4 8.3 %collective-permute-start.15 = (bf16[2,73,16,128]{3,2,1,0:T(8,128)(2,1)S(1)}, bf16[2,73,16,128]{3,2,1,0:T(8,128)(2,1)S(1)}, u32[]{:S(2)}, u32[]{:S(2)}) collective-permute-start(bf16[2,73,16,128]{3,2,1,0:T(8,128)(2,1)S(1)} %constant_dynamic-update-slice_fusion.refs_1_), channel_id=1, source_target_pairs={{0,1},{1,0},{2,3},{3,2},{4,5},{5,4},{6,7},{7,6},{8,9},{9,8},{10,11... | collective-permute-start | bytes 1794056 | tf_op jit(solution)/shard_map/ppermute | solution.py:103
  27.5 9.1 %collective-permute-start.4 = (bf16[2,73,16,128]{3,2,1,0:T(8,128)(2,1)S(1)}, bf16[2,73,16,128]{3,2,1,0:T(8,128)(2,1)S(1)}, u32[]{:S(2)}, u32[]{:S(2)}) collective-permute-start(bf16[2,73,16,128]{3,2,1,0:T(8,128)(2,1)S(1)} %constant_dynamic-update-slice_fusion.refs_1_), channel_id=1, source_target_pairs={{0,2},{1,9},{2,0},{3,11},{4,6},{5,13},{6,4},{7,15},{8,10},{9,1},{1... | collective-permute-start | bytes 1794056 | tf_op jit(solution)/shard_map/ppermute | solution.py:99
  27.6 10.0 %collective-permute-start.18 = (bf16[2,73,16,128]{3,2,1,0:T(8,128)(2,1)S(1)}, bf16[2,73,16,128]{3,2,1,0:T(8,128)(2,1)S(1)}, u32[]{:S(2)}, u32[]{:S(2)}) collective-permute-start(bf16[2,73,16,128]{3,2,1,0:T(8,128)(2,1)S(1)} %collective-permute-done.5.refs_4_), channel_id=1, source_target_pairs={{0,1},{1,0},{2,3},{3,2},{4,5},{5,4},{6,7},{7,6},{8,9},{9,8},{10,11... | collective-permute-start | bytes 1794056 | tf_op jit(solution)/shard_map/ppermute | solution.py:103
  27.7 11.4 %collective-permute-start.7 = (bf16[2,73,16,128]{3,2,1,0:T(8,128)(2,1)S(1)}, bf16[2,73,16,128]{3,2,1,0:T(8,128)(2,1)S(1)}, u32[]{:S(2)}, u32[]{:S(2)}) collective-permute-start(bf16[2,73,16,128]{3,2,1,0:T(8,128)(2,1)S(1)} %collective-permute-done.3.refs_2_), channel_id=1, source_target_pairs={{0,6},{1,25},{2,4},{3,27},{4,2},{5,29},{6,0},{7,31},{8,14},{9,17},... | collective-permute-start | bytes 1794056 | tf_op jit(solution)/shard_map/ppermute | solution.py:99
  32.7 10.4 %collective-permute-start.8 = (bf16[2,73,16,128]{3,2,1,0:T(8,128)(2,1)S(1)}, bf16[2,73,16,128]{3,2,1,0:T(8,128)(2,1)S(1)}, u32[]{:S(2)}, u32[]{:S(2)}) collective-permute-start(bf16[2,73,16,128]{3,2,1,0:T(8,128)(2,1)S(1)} %collective-permute-done.6.refs_5_), channel_id=1, source_target_pairs={{0,2},{1,9},{2,0},{3,11},{4,6},{5,13},{6,4},{7,15},{8,10},{9,1},{1... | collective-permute-start | bytes 1794056 | tf_op jit(solution)/shard_map/ppermute | solution.py:99
  32.7 13.0 %collective-permute-start.16 = (bf16[2,73,16,128]{3,2,1,0:T(8,128)(2,1)S(1)}, bf16[2,73,16,128]{3,2,1,0:T(8,128)(2,1)S(1)}, u32[]{:S(2)}, u32[]{:S(2)}) collective-permute-start(bf16[2,73,16,128]{3,2,1,0:T(8,128)(2,1)S(1)} %collective-permute-done.3.refs_2_), channel_id=1, source_target_pairs={{0,1},{1,0},{2,3},{3,2},{4,5},{5,4},{6,7},{7,6},{8,9},{9,8},{10,11... | collective-permute-start | bytes 1794056 | tf_op jit(solution)/shard_map/ppermute | solution.py:103
  36.7 11.6 %collective-permute-start.19 = (bf16[2,73,16,128]{3,2,1,0:T(8,128)(2,1)S(1)}, bf16[2,73,16,128]{3,2,1,0:T(8,128)(2,1)S(1)}, u32[]{:S(2)}, u32[]{:S(2)}) collective-permute-start(bf16[2,73,16,128]{3,2,1,0:T(8,128)(2,1)S(1)} %collective-permute-done.6.refs_5_), channel_id=1, source_target_pairs={{0,1},{1,0},{2,3},{3,2},{4,5},{5,4},{6,7},{7,6},{8,9},{9,8},{10,11... | collective-permute-start | bytes 1794056 | tf_op jit(solution)/shard_map/ppermute | solution.py:103
  37.5 11.3 %collective-permute-start.17 = (bf16[2,73,16,128]{3,2,1,0:T(8,128)(2,1)S(1)}, bf16[2,73,16,128]{3,2,1,0:T(8,128)(2,1)S(1)}, u32[]{:S(2)}, u32[]{:S(2)}) collective-permute-start(bf16[2,73,16,128]{3,2,1,0:T(8,128)(2,1)S(1)} %collective-permute-done.4.refs_3_), channel_id=1, source_target_pairs={{0,1},{1,0},{2,3},{3,2},{4,5},{5,4},{6,7},{7,6},{8,9},{9,8},{10,11... | collective-permute-start | bytes 1794056 | tf_op jit(solution)/shard_map/ppermute | solution.py:103
  39.1 11.9 %collective-permute-start.12 = (bf16[2,73,16,128]{3,2,1,0:T(8,128)(2,1)S(1)}, bf16[2,73,16,128]{3,2,1,0:T(8,128)(2,1)S(1)}, u32[]{:S(2)}, u32[]{:S(2)}) collective-permute-start(bf16[2,73,16,128]{3,2,1,0:T(8,128)(2,1)S(1)} %collective-permute-done.7.refs_6_.refs_0_), channel_id=1, source_target_pairs={{0,1},{1,0},{2,3},{3,2},{4,5},{5,4},{6,7},{7,6},{8,9},{9,8},{10,11... | collective-permute-start | bytes 1794056 | tf_op jit(solution)/shard_map/ppermute | solution.py:103
  43.1 7.9 %collective-permute-start.13 = (bf16[2,73,16,128]{3,2,1,0:T(8,128)(2,1)S(1)}, bf16[2,73,16,128]{3,2,1,0:T(8,128)(2,1)S(1)}, u32[]{:S(2)}, u32[]{:S(2)}) collective-permute-start(bf16[2,73,16,128]{3,2,1,0:T(8,128)(2,1)S(1)} %collective-permute-done.8.refs_7_.refs_1_), channel_id=1, source_target_pairs={{0,1},{1,0},{2,3},{3,2},{4,5},{5,4},{6,7},{7,6},{8,9},{9,8},{10,11... | collective-permute-start | bytes 1794056 | tf_op jit(solution)/shard_map/ppermute | solution.py:103
  45.7 15.3 %collective-permute-start.11 = (bf16[16,16,128]{2,1,0:T(8,128)(2,1)S(1)}, bf16[16,16,128]{2,1,0:T(8,128)(2,1)S(1)}, u32[]{:S(2)}, u32[]{:S(2)}) collective-permute-start(bf16[16,16,128]{2,1,0:T(8,128)(2,1)S(1)} %tops.1), channel_id=1, source_target_pairs={{0,96},{32,64},{64,32},{96,0},{1,97},{33,65},{65,33},{97,1},{2,98}... | collective-permute-start | bytes 196616 | tf_op jit(solution)/shard_map/ppermute | solution.py:341
  48.3 12.8 %collective-permute-start.10 = (bf16[16,16,128]{2,1,0:T(8,128)(2,1)S(1)}, bf16[16,16,128]{2,1,0:T(8,128)(2,1)S(1)}, u32[]{:S(2)}, u32[]{:S(2)}) collective-permute-start(bf16[16,16,128]{2,1,0:T(8,128)(2,1)S(1)} %tops.1), channel_id=1, source_target_pairs={{0,64},{32,96},{64,0},{96,32},{1,65},{33,97},{65,1},{97,33},{2,66}... | collective-permute-start | bytes 196616 | tf_op jit(solution)/shard_map/ppermute | solution.py:341
  48.8 12.3 %collective-permute-start.9 = (bf16[16,16,128]{2,1,0:T(8,128)(2,1)S(1)}, bf16[16,16,128]{2,1,0:T(8,128)(2,1)S(1)}, u32[]{:S(2)}, u32[]{:S(2)}) collective-permute-start(bf16[16,16,128]{2,1,0:T(8,128)(2,1)S(1)} %tops.1), channel_id=1, source_target_pairs={{0,32},{32,0},{64,96},{96,64},{1,33},{33,1},{65,97},{97,65},{2,34}... | collective-permute-start | bytes 196616 | tf_op jit(solution)/shard_map/ppermute | solution.py:341
  50.9 4.8 %copy-start.1 = (bf16[8,16,64,64]{3,2,1,0:T(8,128)(2,1)S(1)}, bf16[8,16,64,64]{3,2,1,0:T(8,128)(2,1)}, u32[]{:S(2)}) copy-start(bf16[8,16,64,64]{3,2,1,0:T(8,128)(2,1)} %parent_coupling.1) | copy-start | bytes 3145732
  50.9 4.8 %copy-start.5 = (s32[64,16]{0,1:T(8,128)S(1)}, s32[64,16]{0,1:T(8,128)}, u32[]{:S(2)}) copy-start(s32[64,16]{0,1:T(8,128)} %param.25) | copy-start | bytes 12292
  50.9 4.8 %copy-start.6 = (s32[64,16]{0,1:T(8,128)S(1)}, s32[64,16]{0,1:T(8,128)}, u32[]{:S(2)}) copy-start(s32[64,16]{0,1:T(8,128)} %param.26) | copy-start | bytes 12292
  51.0 4.8 %copy-start.7 = (s32[8,16]{1,0:T(8,128)S(1)}, s32[8,16]{1,0:T(8,128)}, u32[]{:S(2)}) copy-start(s32[8,16]{1,0:T(8,128)} %parent_owner.1) | copy-start | bytes 1540
  51.0 4.8 %copy-start.8 = (s32[8,16]{1,0:T(8,128)S(1)}, s32[8,16]{1,0:T(8,128)}, u32[]{:S(2)}) copy-start(s32[8,16]{1,0:T(8,128)} %parent_index.1) | copy-start | bytes 1540
  55.7 7.5 %copy-start = (bf16[64,64,256]{2,1,0:T(8,128)(2,1)S(1)}, bf16[64,64,256]{2,1,0:T(8,128)(2,1)}, u32[]{:S(2)}) copy-start(bf16[64,64,256]{2,1,0:T(8,128)(2,1)} %out_basis.1) | copy-start | bytes 6291460
  55.8 7.5 %copy-start.2 = (bf16[64,64,64]{2,1,0:T(8,128)(2,1)S(1)}, bf16[64,64,64]{2,1,0:T(8,128)(2,1)}, u32[]{:S(2)}) copy-start(bf16[64,64,64]{2,1,0:T(8,128)(2,1)} %leaf_descend.1) | copy-start | bytes 1572868
  55.8 7.5 %copy-start.3 = (bf16[1,16,64,64]{3,2,1,0:T(8,128)(2,1)S(1)}, bf16[1,16,64,64]{3,2,1,0:T(8,128)(2,1)}, u32[]{:S(2)}) copy-start(bf16[1,16,64,64]{3,2,1,0:T(8,128)(2,1)} %top_coupling.1) | copy-start | bytes 393220
  55.8 7.5 %copy-start.4 = (bf16[8,64,64]{2,1,0:T(8,128)(2,1)S(1)}, bf16[8,64,64]{2,1,0:T(8,128)(2,1)}, u32[]{:S(2)}) copy-start(bf16[8,64,64]{2,1,0:T(8,128)(2,1)} %parent_descend.1) | copy-start | bytes 196612
  55.8 7.5 %copy-start.9 = (s32[64]{0:T(128)S(1)}, s32[64]{0:T(128)}, u32[]{:S(2)}) copy-start(s32[64]{0:T(128)} %counts.3) | copy-start | bytes 772
  55.8 7.5 %copy-start.10 = (s32[1,16]{1,0:T(1,128)S(1)}, s32[1,16]{1,0:T(1,128)}, u32[]{:S(2)}) copy-start(s32[1,16]{1,0:T(1,128)} %top_source.1) | copy-start | bytes 196
  61.2 2.1 %collective-permute-start.20 = (bf16[64,16,128]{2,1,0:T(8,128)(2,1)S(1)}, bf16[64,16,128]{2,1,0:T(8,128)(2,1)S(1)}, u32[]{:S(2)}, u32[]{:S(2)}) collective-permute-start(bf16[64,16,128]{2,1,0:T(8,128)(2,1)S(1)} %pad_maximum_fusion.1), channel_id=1, source_target_pairs={{0,1},{1,0},{2,3},{3,2},{4,5},{5,4},{6,7},{7,6},{8,9},{9,8},{10,11... | collective-permute-start | bytes 786440 | tf_op jit(solution)/shard_map/ppermute | solution.py:103
  (4 other events, 12.9 us)

commit v3 on v2

--- a/solution.py
+++ b/solution.py
@@ -103,64 +103,38 @@
     return lax.ppermute(x, "c", [(0, 1), (1, 0)])
 
 
-def gather(s):
+def gather(s, staged):
     s = s[None]
     a, o, b = (send(s, False, m) for m in (1, 2, 3))
     near, far = jnp.concatenate([s, a]), jnp.concatenate([o, b])
+    far, staged = lax.optimization_barrier((far, staged))
     near_a, near_b = send(near, True, 1), send(near, True, 3)
     far_a, far_b = send(far, True, 1), send(far, True, 3)
     near_o, far_o = send(near_a, True, 3), send(far_b, True, 1)
     early = [(near, 0), (far, 2), (near_a, 4), (far_a, 6), (near_b, 12), (far_b, 14)]
-    return early, [(near_o, 8), (far_o, 10)]
-
-
-def early_kernel(firsts, *refs):
-    n = len(firsts)
-    out, sem = refs[n:]
-    copies = []
-    for ref, first in zip(refs[:n], firsts):
-        for i in range(2):
-            spot = out.at[pl.ds((first + i) * ROWS, ROWS)]
-            copies.append(pltpu.make_async_copy(ref.at[i], spot, sem.at[len(copies)]))
-            copies[-1].start()
-    for copy in copies:
-        copy.wait()
-
-
-def assemble_early(pieces):
-    n = len(pieces)
-    return pl.pallas_call(
-        functools.partial(early_kernel, [first for _, first in pieces]),
-        in_specs=[pl.BlockSpec(memory_space=pltpu.HBM)] * n,
-        out_specs=pl.BlockSpec(memory_space=pltpu.VMEM),
-        out_shape=jax.ShapeDtypeStruct((32 * ROWS, 16, 128), BF16),
-        scratch_shapes=[pltpu.SemaphoreType.DMA((2 * n,))],
-        compiler_params=pltpu.CompilerParams(vmem_limit_bytes=8 * MIB),
-        cost_estimate=pl.CostEstimate(flops=0, bytes_accessed=4096, transcendentals=0),
-        name="assemble_early",
-    )(*[x for x, _ in pieces])
-
-
-def late_kernel(firsts, *refs):
-    out = refs[len(firsts) + 1]
+    return early, [(near_o, 8), (far_o, 10)], staged
+
+
+def place_kernel(firsts, *refs):
+    out = refs[-1]
     for ref, first in zip(refs, firsts):
         for i in range(2):
             out[(first + i) * ROWS : (first + i + 1) * ROWS] = ref[i]
 
 
-def assemble_late(pieces, gathered):
+def assemble(pieces, *earlier):
     vmem = pl.BlockSpec(memory_space=pltpu.VMEM)
     n = len(pieces)
     return pl.pallas_call(
-        functools.partial(late_kernel, [first for _, first in pieces]),
-        in_specs=[vmem] * (n + 1),
+        functools.partial(place_kernel, [first for _, first in pieces]),
+        in_specs=[vmem] * (n + len(earlier)),
         out_specs=vmem,
         out_shape=jax.ShapeDtypeStruct((32 * ROWS, 16, 128), BF16),
-        input_output_aliases={n: 0},
-        compiler_params=pltpu.CompilerParams(vmem_limit_bytes=8 * MIB),
+        input_output_aliases={n: 0} if earlier else {},
+        compiler_params=pltpu.CompilerParams(vmem_limit_bytes=10 * MIB),
         cost_estimate=pl.CostEstimate(flops=0, bytes_accessed=4096, transcendentals=0),
-        name="assemble_late",
-    )(*[x for x, _ in pieces], gathered)
+        name="assemble",
+    )(*[x for x, _ in pieces], *earlier)
 
 
 def tops_kernel(firsts, *refs):
@@ -205,6 +179,35 @@
     return jnp.concatenate([jnp.concatenate(low, axis=1), jnp.concatenate(high, axis=1)], axis=0)
 
 
+CHUNK = 8
+STAGED = 24
+
+
+def stage_kernel(coupling, out, sem):
+    parts = 4
+    size = out.shape[0] // parts
+    copies = []
+    for k in range(parts):
+        source = coupling.at[pl.ds(k * size, size)]
+        copies.append(pltpu.make_async_copy(source, out.at[pl.ds(k * size, size)], sem.at[k]))
+        copies[k].start()
+    for copy in copies:
+        copy.wait()
+
+
+def stage(coupling, count):
+    return pl.pallas_call(
+        stage_kernel,
+        in_specs=[pl.BlockSpec(memory_space=pltpu.HBM)],
+        out_specs=pl.BlockSpec(memory_space=pltpu.VMEM),
+        out_shape=jax.ShapeDtypeStruct((count,) + coupling.shape[1:], BF16),
+        scratch_shapes=[pltpu.SemaphoreType.DMA((4,))],
+        compiler_params=pltpu.CompilerParams(vmem_limit_bytes=2 * MIB),
+        cost_estimate=pl.CostEstimate(flops=0, bytes_accessed=4096, transcendentals=0),
+        name="stage",
+    )(pltpu.with_memory_space_constraint(coupling, pltpu.HBM))
+
+
 def couple_kernel(
     place,
     far_owner,
@@ -212,60 +215,83 @@
     parent_owner,
     parent_index,
     gathered,
+    head,
     coupling,
     parent_coupling,
     leaf_far,
     parent_far,
+    staged,
+    parent_staged,
     leaf_rows,
     parent_rows,
     leaf_named,
     parent_named,
-    sem,
+    chunk_sem,
+    row_sem,
 ):
+    chunks = []
+    for k in range((LEAF - STAGED) // CHUNK):
+        source = coupling.at[pl.ds(STAGED + k * CHUNK, CHUNK)]
+        chunks.append(pltpu.make_async_copy(source, staged.at[pl.ds(k * CHUNK, CHUNK)], chunk_sem.at[k]))
+    chunks.append(pltpu.make_async_copy(parent_coupling, parent_staged, chunk_sem.at[len(chunks)]))
+    for copy in chunks:
+        copy.start()
     y, z, c = place[1], place[2], place[3]
     leaf_rows[...] = slots(far_owner[...], y, z, c) * ROWS + far_local[...]
     parent_rows[...] = slots(parent_owner[...], y, z, c) * ROWS + LEAF + parent_index[...]
-    copies = [
-        pltpu.make_async_copy(leaf_rows, leaf_named, sem.at[0]),
-        pltpu.make_async_copy(parent_rows, parent_named, sem.at[1]),
+    named = [
+        pltpu.make_async_copy(leaf_rows, leaf_named, row_sem.at[0]),
+        pltpu.make_async_copy(parent_rows, parent_named, row_sem.at[1]),
     ]
-    for copy in copies:
+    for copy in named:
         copy.start()
-    for copy in copies:
-        copy.wait()
-
-    def leaf(b, _):
+    for copy in named:
+        copy.wait()
+    for b in range(STAGED):
         block = picked(lambda j: gathered[leaf_named[j, b]], 16)
-        leaf_far[b] = dot(block, coupling[b].reshape(1024, 64))
-        return 0
-
-    def parent(q, _):
+        leaf_far[b] = dot(block, head[b].reshape(1024, 64))
+    for k in range((LEAF - STAGED) // CHUNK):
+        chunks[k].wait()
+        for i in range(k * CHUNK, (k + 1) * CHUNK):
+            block = picked(lambda j: gathered[leaf_named[j, STAGED + i]], 16)
+            leaf_far[STAGED + i] = dot(block, staged[i].reshape(1024, 64))
+    chunks[-1].wait()
+    for q in range(PARENT):
         block = picked(lambda j: gathered[parent_named[q, j]], 16)
-        parent_far[q] = dot(block, parent_coupling[q].reshape(1024, 64))
-        return 0
-
-    lax.fori_loop(0, LEAF, leaf, 0, unroll=16)
-    lax.fori_loop(0, PARENT, parent, 0, unroll=8)
-
-
-def couple(place, far_owner, far_local, parent_owner, parent_index, gathered, coupling, parent_coupling):
+        parent_far[q] = dot(block, parent_staged[q].reshape(1024, 64))
+
+
+def couple(place, far_owner, far_local, parent_owner, parent_index, gathered, head, coupling, parent_coupling):
     smem, vmem = pl.BlockSpec(memory_space=pltpu.SMEM), pl.BlockSpec(memory_space=pltpu.VMEM)
     return pl.pallas_call(
         couple_kernel,
-        in_specs=[smem] + [vmem] * 7,
+        in_specs=[smem] + [vmem] * 6 + [pl.BlockSpec(memory_space=pltpu.HBM)] * 2,
         out_specs=[vmem, vmem],
         out_shape=[jax.ShapeDtypeStruct((LEAF, 32, 64), F32), jax.ShapeDtypeStruct((PARENT, 32, 64), F32)],
         scratch_shapes=[
+            pltpu.VMEM((LEAF - STAGED,) + coupling.shape[1:], BF16),
+            pltpu.VMEM(parent_coupling.shape, BF16),
             pltpu.VMEM(far_owner.shape, jnp.int32),
             pltpu.VMEM(parent_owner.shape, jnp.int32),
             pltpu.SMEM(far_owner.shape, jnp.int32),
             pltpu.SMEM(parent_owner.shape, jnp.int32),
+            pltpu.SemaphoreType.DMA(((LEAF - STAGED) // CHUNK + 1,)),
             pltpu.SemaphoreType.DMA((2,)),
         ],
-        compiler_params=pltpu.CompilerParams(vmem_limit_bytes=4 * MIB),
+        compiler_params=pltpu.CompilerParams(vmem_limit_bytes=18 * MIB),
         cost_estimate=pl.CostEstimate(flops=2 * 72 * 32 * 64 * 1024, bytes_accessed=28 * MIB, transcendentals=0),
         name="couple",
-    )(place, far_owner, far_local, parent_owner, parent_index, gathered, coupling, parent_coupling)
+    )(
+        place,
+        far_owner,
+        far_local,
+        parent_owner,
+        parent_index,
+        gathered,
+        head,
+        pltpu.with_memory_space_constraint(coupling, pltpu.HBM),
+        pltpu.with_memory_space_constraint(parent_coupling, pltpu.HBM),
+    )
 
 
 def down_kernel(
@@ -333,15 +359,15 @@
 
     hbm = lambda a: pltpu.with_memory_space_constraint(a, pltpu.HBM)
     coeffs = up(*map(hbm, (counts, charges, leaf_basis, leaf_transfer, parent_transfer)))
-    early, late = gather(coeffs)
+    early, late, head = gather(coeffs, stage(leaf_coupling, STAGED))
     swap = lambda pieces: [(other_core(piece), 16 + first) for piece, first in pieces]
-    gathered = assemble_early(early + swap(early))
-    gathered = assemble_late(late + swap(late), gathered)
+    gathered = assemble(early + swap(early))
+    gathered = assemble(late + swap(late), gathered)
     tops = column_tops(early + late)
     planes = [tops] + [lax.ppermute(tops, "x", [(i, i ^ m) for i in range(4)]) for m in (1, 2, 3)]
 
     names = (far_owner.T, far_local.T, parent_owner, parent_index)
-    leaf_far, parent_far = couple(place, *names, gathered, leaf_coupling, parent_coupling)
+    leaf_far, parent_far = couple(place, *names, gathered, head, leaf_coupling, parent_coupling)
     planes, leaf_far = lax.optimization_barrier((planes, leaf_far))
     tops = jnp.concatenate(planes)
     tops = jnp.concatenate([tops, other_core(tops)])

time: 66.2 us -> 56.8 us (0.86)
  waiting for transfers between devices: 17.4 us -> 13.1 us
  local copies, waits for them, and re-layouts: 4.78 us -> 0.63 us
  starting transfers between devices: 30.3 us -> 26.8 us
  Pallas kernels: 13.2 us -> 15.6 us
    ppermute x9, waiting for transfers between devices: 16.2 us -> 12 us  [send(): return lax.ppermute(x, ('y', 'z', 'c'), pairs(second, mask))]
    ppermute x9, starting transfers between devices: 14.3 us -> 10.2 us  [other_core(): return lax.ppermute(x, 'c', [(0, 1), (1, 0)])]
    unnamed x35 -> x24, local copies, waits for them, and re-layouts: 4.71 us -> 0.59 us
    pallas_call x3 -> x4, Pallas kernels: 7.21 us -> 9.55 us  [the longest x1 6.07 us: couple(): pl.pallas_call(couple_kernel, in_specs=[smem] + [vmem] * 6 + [pl.BlockSpe...]
    ppermute x9, starting transfers between devices: 12.6 us -> 13.3 us  [send(): return lax.ppermute(x, ('y', 'z', 'c'), pairs(second, mask))]
  transfers between devices with their start and end apart: 21 -> 21, of which waited for: 8 -> 7; matrix products, arithmetic and copies ran while one was open for 0% -> 0% of each run, Pallas kernels for 11% -> 17%
where the time goes in v3:
time: 56.8 us; the launch traced here: 56.6 us
  starting transfers between devices  26.8 us (47%)
  Pallas kernels  15.6 us (27%)
  waiting for transfers between devices  13.1 us (23%)
  local copies, waits for them, and re-layouts  0.63 us (1%)
    ppermute x9, starting transfers between devices, send(): return lax.ppermute(x, ('y', 'z', 'c'), pairs(second, mask))  13.3 us
    ppermute x9, waiting for transfers between devices, send(): return lax.ppermute(x, ('y', 'z', 'c'), pairs(second, mask))  12 us
    ppermute x9, starting transfers between devices, other_core(): return lax.ppermute(x, 'c', [(0, 1), (1, 0)])  10.2 us
    pallas_call x1, Pallas kernels, couple(): pl.pallas_call(couple_kernel, in_specs=[smem] + [vmem] * 6 + [pl.BlockSpe...  6.07 us
    ppermute x3, starting transfers between devices, body(): lax.ppermute(tops, 'x', [(i, i ^ m) for i in range(4)])  3.33 us
    pallas_call x1, Pallas kernels, up(): pl.pallas_call(up_kernel, in_specs=[hbm] * 5, out_specs=pl.BlockSpec(memo...  2.98 us
    pallas_call x1, Pallas kernels, stage(): pl.pallas_call(stage_kernel, in_specs=[pl.BlockSpec(memory_space=pltpu.HB...  2.87 us
    pallas_call x1, Pallas kernels, down(): pl.pallas_call(down_kernel, in_specs=[smem] * 3 + [vmem] * len(operands),...  2.82 us
  transfers between devices with their start and end apart: 21, of which 7 were waited for; matrix products, arithmetic and copies ran while one was open for 0% of the time, Pallas kernels for 17%

profile of v3, /device:TPU:1, one launch (start us, length us, event | category | flops | bytes accessed | tf_op | source)
XLA Modules:
  0.0 56.6 jit_solution(18398068182105456610)
XLA Ops:
  0.1 3.0 %up.1 = bf16[73,16,128]{2,1,0:T(8,128)(2,1)S(1)} custom-call(s32[64]{0:T(128)} %counts.3, bf16[64,32,256]{2,1,0:T(8,128)(2,1)} %charges, bf16[64,64,256]{2,1,0:T(8,128)(2,1)} %basis.1, bf16[64,64,64]{2,1,0:T(8,128)(2,1)} %transfer.1, bf16[8,64,64]{2,1,0:T(8,128)(2,1)} %parent_transfer.1), custom_call_target="tpu_custom_call" | custom-call | flops 83886080 | bytes 5242880 | tf_op jit(solution)/shard_map/up/pallas_call | solution.py:73
  3.1 2.5 %collective-permute-start = (bf16[1,73,16,128]{3,2,1,0:T(8,128)(2,1)S(1)}, bf16[1,73,16,128]{3,2,1,0:T(8,128)(2,1)S(1)}, u32[]{:S(2)}, u32[]{:S(2)}) collective-permute-start(bf16[1,73,16,128]{3,2,1,0:T(8,128)(2,1)S(1)} %bitcast.7), channel_id=1, source_target_pairs={{0,8},{1,3},{2,10},{3,1},{4,12},{5,7},{6,14},{7,5},{8,0},{9,11},{1... | collective-permute-start | bytes 897032 | tf_op jit(solution)/shard_map/ppermute | solution.py:99
  5.6 2.2 %collective-permute-start.2 = (bf16[1,73,16,128]{3,2,1,0:T(8,128)(2,1)S(1)}, bf16[1,73,16,128]{3,2,1,0:T(8,128)(2,1)S(1)}, u32[]{:S(2)}, u32[]{:S(2)}) collective-permute-start(bf16[1,73,16,128]{3,2,1,0:T(8,128)(2,1)S(1)} %bitcast.8), channel_id=1, source_target_pairs={{0,24},{1,7},{2,26},{3,5},{4,28},{5,3},{6,30},{7,1},{8,16},{9,15},... | collective-permute-start | bytes 897032 | tf_op jit(solution)/shard_map/ppermute | solution.py:99
  7.9 1.1 %collective-permute-start.1 = (bf16[1,73,16,128]{3,2,1,0:T(8,128)(2,1)S(1)}, bf16[1,73,16,128]{3,2,1,0:T(8,128)(2,1)S(1)}, u32[]{:S(2)}, u32[]{:S(2)}) collective-permute-start(bf16[1,73,16,128]{3,2,1,0:T(8,128)(2,1)S(1)} %bitcast.9), channel_id=1, source_target_pairs={{0,16},{1,5},{2,18},{3,7},{4,20},{5,1},{6,22},{7,3},{8,24},{9,13},... | collective-permute-start | bytes 897032 | tf_op jit(solution)/shard_map/ppermute | solution.py:99
  8.9 2.9 %stage.1.head = bf16[24,16,64,64]{3,2,1,0:T(8,128)(2,1)S(1)} custom-call(bf16[64,16,64,64]{3,2,1,0:T(8,128)(2,1)} %coupling.3), custom_call_target="tpu_custom_call" | custom-call | bytes 4096 | tf_op jit(solution)/shard_map/stage/pallas_call | solution.py:199
  11.9 0.3 collective-permute-start.14
  12.2 2.6 %collective-permute-start.5 = (bf16[2,73,16,128]{3,2,1,0:T(8,128)(2,1)S(1)}, bf16[2,73,16,128]{3,2,1,0:T(8,128)(2,1)S(1)}, u32[]{:S(2)}, u32[]{:S(2)}) collective-permute-start(bf16[2,73,16,128]{3,2,1,0:T(8,128)(2,1)S(1)} %pad_maximum_fusion.refs_0_), channel_id=1, source_target_pairs={{0,6},{1,25},{2,4},{3,27},{4,2},{5,29},{6,0},{7,31},{8,14},{9,17},... | collective-permute-start | bytes 1794056 | tf_op jit(solution)/shard_map/ppermute | solution.py:99
  14.8 1.8 %collective-permute-done.1 = bf16[1,73,16,128]{3,2,1,0:T(8,128)(2,1)S(1)} collective-permute-done((bf16[1,73,16,128]{3,2,1,0:T(8,128)(2,1)S(1)}, bf16[1,73,16,128]{3,2,1,0:T(8,128)(2,1)S(1)}, u32[]{:S(2)}, u32[]{:S(2)}) %collective-permute-start.1) | collective-permute-done | bytes 299040 | tf_op jit(solution)/shard_map/ppermute | solution.py:99
  16.6 2.5 %collective-permute-start.6 = (bf16[2,73,16,128]{3,2,1,0:T(8,128)(2,1)S(1)}, bf16[2,73,16,128]{3,2,1,0:T(8,128)(2,1)S(1)}, u32[]{:S(2)}, u32[]{:S(2)}) collective-permute-start(bf16[2,73,16,128]{3,2,1,0:T(8,128)(2,1)S(1)} %pad_maximum_fusion.1.refs_1_), channel_id=1, source_target_pairs={{0,6},{1,25},{2,4},{3,27},{4,2},{5,29},{6,0},{7,31},{8,14},{9,17},... | collective-permute-start | bytes 1794056 | tf_op jit(solution)/shard_map/ppermute | solution.py:99
  19.1 2.6 %collective-permute-start.15 = (bf16[2,73,16,128]{3,2,1,0:T(8,128)(2,1)S(1)}, bf16[2,73,16,128]{3,2,1,0:T(8,128)(2,1)S(1)}, u32[]{:S(2)}, u32[]{:S(2)}) collective-permute-start(bf16[2,73,16,128]{3,2,1,0:T(8,128)(2,1)S(1)} %pad_maximum_fusion.1.refs_1_), channel_id=1, source_target_pairs={{0,1},{1,0},{2,3},{3,2},{4,5},{5,4},{6,7},{7,6},{8,9},{9,8},{10,11... | collective-permute-start | bytes 1794056 | tf_op jit(solution)/shard_map/ppermute | solution.py:103
  21.8 1.7 %collective-permute-done.5.refs_4_ = bf16[2,73,16,128]{3,2,1,0:T(8,128)(2,1)S(1)} collective-permute-done((bf16[2,73,16,128]{3,2,1,0:T(8,128)(2,1)S(1)}, bf16[2,73,16,128]{3,2,1,0:T(8,128)(2,1)S(1)}, u32[]{:S(2)}, u32[]{:S(2)}) %collective-permute-start.5) | collective-permute-done | bytes 598048 | tf_op jit(solution)/shard_map/ppermute | solution.py:99
  23.4 0.8 %collective-permute-start.18 = (bf16[2,73,16,128]{3,2,1,0:T(8,128)(2,1)S(1)}, bf16[2,73,16,128]{3,2,1,0:T(8,128)(2,1)S(1)}, u32[]{:S(2)}, u32[]{:S(2)}) collective-permute-start(bf16[2,73,16,128]{3,2,1,0:T(8,128)(2,1)S(1)} %collective-permute-done.5.refs_4_), channel_id=1, source_target_pairs={{0,1},{1,0},{2,3},{3,2},{4,5},{5,4},{6,7},{7,6},{8,9},{9,8},{10,11... | collective-permute-start | bytes 1794056 | tf_op jit(solution)/shard_map/ppermute | solution.py:103
  24.2 2.3 %collective-permute-start.7 = (bf16[2,73,16,128]{3,2,1,0:T(8,128)(2,1)S(1)}, bf16[2,73,16,128]{3,2,1,0:T(8,128)(2,1)S(1)}, u32[]{:S(2)}, u32[]{:S(2)}) collective-permute-start(bf16[2,73,16,128]{3,2,1,0:T(8,128)(2,1)S(1)} %collective-permute-done.3.refs_2_), channel_id=1, source_target_pairs={{0,6},{1,25},{2,4},{3,27},{4,2},{5,29},{6,0},{7,31},{8,14},{9,17},... | collective-permute-start | bytes 1794056 | tf_op jit(solution)/shard_map/ppermute | solution.py:99
  26.6 3.2 %collective-permute-done.6.refs_5_ = bf16[2,73,16,128]{3,2,1,0:T(8,128)(2,1)S(1)} collective-permute-done((bf16[2,73,16,128]{3,2,1,0:T(8,128)(2,1)S(1)}, bf16[2,73,16,128]{3,2,1,0:T(8,128)(2,1)S(1)}, u32[]{:S(2)}, u32[]{:S(2)}) %collective-permute-start.6) | collective-permute-done | bytes 598048 | tf_op jit(solution)/shard_map/ppermute | solution.py:99
  29.8 0.8 %collective-permute-start.16 = (bf16[2,73,16,128]{3,2,1,0:T(8,128)(2,1)S(1)}, bf16[2,73,16,128]{3,2,1,0:T(8,128)(2,1)S(1)}, u32[]{:S(2)}, u32[]{:S(2)}) collective-permute-start(bf16[2,73,16,128]{3,2,1,0:T(8,128)(2,1)S(1)} %collective-permute-done.3.refs_2_), channel_id=1, source_target_pairs={{0,1},{1,0},{2,3},{3,2},{4,5},{5,4},{6,7},{7,6},{8,9},{9,8},{10,11... | collective-permute-start | bytes 1794056 | tf_op jit(solution)/shard_map/ppermute | solution.py:103
  30.7 0.2 collective-permute-done.4.refs_3_
  30.9 1.8 %collective-permute-start.19 = (bf16[2,73,16,128]{3,2,1,0:T(8,128)(2,1)S(1)}, bf16[2,73,16,128]{3,2,1,0:T(8,128)(2,1)S(1)}, u32[]{:S(2)}, u32[]{:S(2)}) collective-permute-start(bf16[2,73,16,128]{3,2,1,0:T(8,128)(2,1)S(1)} %collective-permute-done.6.refs_5_), channel_id=1, source_target_pairs={{0,1},{1,0},{2,3},{3,2},{4,5},{5,4},{6,7},{7,6},{8,9},{9,8},{10,11... | collective-permute-start | bytes 1794056 | tf_op jit(solution)/shard_map/ppermute | solution.py:103
  32.7 3.6 %collective-permute-done.7.refs_6_.refs_0_ = bf16[2,73,16,128]{3,2,1,0:T(8,128)(2,1)S(1)} collective-permute-done((bf16[2,73,16,128]{3,2,1,0:T(8,128)(2,1)S(1)}, bf16[2,73,16,128]{3,2,1,0:T(8,128)(2,1)S(1)}, u32[]{:S(2)}, u32[]{:S(2)}) %collective-permute-start.7) | collective-permute-done | bytes 598048 | tf_op jit(solution)/shard_map/ppermute | solution.py:99
  36.2 1.2 %collective-permute-start.12 = (bf16[2,73,16,128]{3,2,1,0:T(8,128)(2,1)S(1)}, bf16[2,73,16,128]{3,2,1,0:T(8,128)(2,1)S(1)}, u32[]{:S(2)}, u32[]{:S(2)}) collective-permute-start(bf16[2,73,16,128]{3,2,1,0:T(8,128)(2,1)S(1)} %collective-permute-done.7.refs_6_.refs_0_), channel_id=1, source_target_pairs={{0,1},{1,0},{2,3},{3,2},{4,5},{5,4},{6,7},{7,6},{8,9},{9,8},{10,11... | collective-permute-start | bytes 1794056 | tf_op jit(solution)/shard_map/ppermute | solution.py:103
  37.4 1.5 %collective-permute-done.8.refs_7_.refs_1_ = bf16[2,73,16,128]{3,2,1,0:T(8,128)(2,1)S(1)} collective-permute-done((bf16[2,73,16,128]{3,2,1,0:T(8,128)(2,1)S(1)}, bf16[2,73,16,128]{3,2,1,0:T(8,128)(2,1)S(1)}, u32[]{:S(2)}, u32[]{:S(2)}) %collective-permute-start.8) | collective-permute-done | bytes 598048 | tf_op jit(solution)/shard_map/ppermute | solution.py:99
  38.9 1.7 %collective-permute-start.13 = (bf16[2,73,16,128]{3,2,1,0:T(8,128)(2,1)S(1)}, bf16[2,73,16,128]{3,2,1,0:T(8,128)(2,1)S(1)}, u32[]{:S(2)}, u32[]{:S(2)}) collective-permute-start(bf16[2,73,16,128]{3,2,1,0:T(8,128)(2,1)S(1)} %collective-permute-done.8.refs_7_.refs_1_), channel_id=1, source_target_pairs={{0,1},{1,0},{2,3},{3,2},{4,5},{5,4},{6,7},{7,6},{8,9},{9,8},{10,11... | collective-permute-start | bytes 1794056 | tf_op jit(solution)/shard_map/ppermute | solution.py:103
  40.6 0.2 tops.1
  40.9 2.6 %collective-permute-start.11 = (bf16[16,16,128]{2,1,0:T(8,128)(2,1)S(1)}, bf16[16,16,128]{2,1,0:T(8,128)(2,1)S(1)}, u32[]{:S(2)}, u32[]{:S(2)}) collective-permute-start(bf16[16,16,128]{2,1,0:T(8,128)(2,1)S(1)} %tops.1), channel_id=1, source_target_pairs={{0,96},{32,64},{64,32},{96,0},{1,97},{33,65},{65,33},{97,1},{2,98}... | collective-permute-start | bytes 196616 | tf_op jit(solution)/shard_map/ppermute | solution.py:367
  43.4 0.5 collective-permute-start.10
  44.0 0.3 collective-permute-start.9
  44.2 0.5 assemble.2.refs_4_
  44.8 0.2 assemble.3.gathered
  44.9 0.5 copy-done.4
  45.5 6.1 %couple.1 = (f32[64,32,64]{2,1,0:T(8,128)S(1)}, f32[8,32,64]{2,1,0:T(8,128)S(1)}) custom-call(s32[4]{0:T(128)S(1)} %pad_add_fusion.place, s32[16,64]{1,0:T(8,128)S(1)} %bitcast.11, s32[16,64]{1,0:T(8,128)S(1)} %bitcast.12, s32[8,16]{1,0:T(8,128)S(1)} %copy-done.6, s32[8,16]{1,0:T(8,128)S(1)} %copy-done.7, bf16[2336,16,128]{2,1,0:T(8,128)(2,1)S(1)} %assemble.3.gathered, ...), custom_call_target="tpu_custom_call" | custom-call | flops 301989888 | bytes 29360128 | tf_op jit(solution)/shard_map/couple/pallas_call | solution.py:266
  51.6 0.9 %collective-permute-start.20 = (bf16[64,16,128]{2,1,0:T(8,128)(2,1)S(1)}, bf16[64,16,128]{2,1,0:T(8,128)(2,1)S(1)}, u32[]{:S(2)}, u32[]{:S(2)}) collective-permute-start(bf16[64,16,128]{2,1,0:T(8,128)(2,1)S(1)} %pad_maximum_fusion.2), channel_id=1, source_target_pairs={{0,1},{1,0},{2,3},{3,2},{4,5},{5,4},{6,7},{7,6},{8,9},{9,8},{10,11... | collective-permute-start | bytes 786440 | tf_op jit(solution)/shard_map/ppermute | solution.py:103
  52.6 1.1 %collective-permute-done.20 = bf16[64,16,128]{2,1,0:T(8,128)(2,1)S(1)} collective-permute-done((bf16[64,16,128]{2,1,0:T(8,128)(2,1)S(1)}, bf16[64,16,128]{2,1,0:T(8,128)(2,1)S(1)}, u32[]{:S(2)}, u32[]{:S(2)}) %collective-permute-start.20) | collective-permute-done | bytes 262176 | tf_op jit(solution)/shard_map/ppermute | solution.py:103
  53.8 2.8 %down.1 = bf16[64,32,256]{2,1,0:T(8,128)(2,1)} custom-call(s32[64]{0:T(128)S(1)} %copy-done.8, s32[4]{0:T(128)S(1)} %pad_add_fusion.place, s32[1,16]{1,0:T(1,128)S(1)} %copy-done.9, bf16[128,16,128]{2,1,0:T(8,128)(2,1)S(1)} %constant_dynamic-update-slice_fusion.tops, bf16[1,16,64,64]{3,2,1,0:T(8,128)(2,1)S(1)} %copy-done.2, ...), custom_call_target="tpu_custom_call" | custom-call | flops 83886080 | bytes 6291456 | tf_op jit(solution)/shard_map/down/pallas_call | solution.py:326
  (46 shorter events, 0.4 us)
Async XLA Ops:
  3.1 8.7 %collective-permute-start = (bf16[1,73,16,128]{3,2,1,0:T(8,128)(2,1)S(1)}, bf16[1,73,16,128]{3,2,1,0:T(8,128)(2,1)S(1)}, u32[]{:S(2)}, u32[]{:S(2)}) collective-permute-start(bf16[1,73,16,128]{3,2,1,0:T(8,128)(2,1)S(1)} %bitcast.7), channel_id=1, source_target_pairs={{0,8},{1,3},{2,10},{3,1},{4,12},{5,7},{6,14},{7,5},{8,0},{9,11},{1... | collective-permute-start | bytes 897032 | tf_op jit(solution)/shard_map/ppermute | solution.py:99
  5.6 9.2 %collective-permute-start.2 = (bf16[1,73,16,128]{3,2,1,0:T(8,128)(2,1)S(1)}, bf16[1,73,16,128]{3,2,1,0:T(8,128)(2,1)S(1)}, u32[]{:S(2)}, u32[]{:S(2)}) collective-permute-start(bf16[1,73,16,128]{3,2,1,0:T(8,128)(2,1)S(1)} %bitcast.8), channel_id=1, source_target_pairs={{0,24},{1,7},{2,26},{3,5},{4,28},{5,3},{6,30},{7,1},{8,16},{9,15},... | collective-permute-start | bytes 897032 | tf_op jit(solution)/shard_map/ppermute | solution.py:99
  7.9 8.7 %collective-permute-start.1 = (bf16[1,73,16,128]{3,2,1,0:T(8,128)(2,1)S(1)}, bf16[1,73,16,128]{3,2,1,0:T(8,128)(2,1)S(1)}, u32[]{:S(2)}, u32[]{:S(2)}) collective-permute-start(bf16[1,73,16,128]{3,2,1,0:T(8,128)(2,1)S(1)} %bitcast.9), channel_id=1, source_target_pairs={{0,16},{1,5},{2,18},{3,7},{4,20},{5,1},{6,22},{7,3},{8,24},{9,13},... | collective-permute-start | bytes 897032 | tf_op jit(solution)/shard_map/ppermute | solution.py:99
  11.9 9.9 %collective-permute-start.14 = (bf16[2,73,16,128]{3,2,1,0:T(8,128)(2,1)S(1)}, bf16[2,73,16,128]{3,2,1,0:T(8,128)(2,1)S(1)}, u32[]{:S(2)}, u32[]{:S(2)}) collective-permute-start(bf16[2,73,16,128]{3,2,1,0:T(8,128)(2,1)S(1)} %pad_maximum_fusion.refs_0_), channel_id=1, source_target_pairs={{0,1},{1,0},{2,3},{3,2},{4,5},{5,4},{6,7},{7,6},{8,9},{9,8},{10,11... | collective-permute-start | bytes 1794056 | tf_op jit(solution)/shard_map/ppermute | solution.py:103
  12.2 11.3 %collective-permute-start.5 = (bf16[2,73,16,128]{3,2,1,0:T(8,128)(2,1)S(1)}, bf16[2,73,16,128]{3,2,1,0:T(8,128)(2,1)S(1)}, u32[]{:S(2)}, u32[]{:S(2)}) collective-permute-start(bf16[2,73,16,128]{3,2,1,0:T(8,128)(2,1)S(1)} %pad_maximum_fusion.refs_0_), channel_id=1, source_target_pairs={{0,6},{1,25},{2,4},{3,27},{4,2},{5,29},{6,0},{7,31},{8,14},{9,17},... | collective-permute-start | bytes 1794056 | tf_op jit(solution)/shard_map/ppermute | solution.py:99
  14.8 9.5 %collective-permute-start.3 = (bf16[2,73,16,128]{3,2,1,0:T(8,128)(2,1)S(1)}, bf16[2,73,16,128]{3,2,1,0:T(8,128)(2,1)S(1)}, u32[]{:S(2)}, u32[]{:S(2)}) collective-permute-start(bf16[2,73,16,128]{3,2,1,0:T(8,128)(2,1)S(1)} %pad_maximum_fusion.refs_0_), channel_id=1, source_target_pairs={{0,2},{1,9},{2,0},{3,11},{4,6},{5,13},{6,4},{7,15},{8,10},{9,1},{1... | collective-permute-start | bytes 1794056 | tf_op jit(solution)/shard_map/ppermute | solution.py:99
  16.6 13.2 %collective-permute-start.6 = (bf16[2,73,16,128]{3,2,1,0:T(8,128)(2,1)S(1)}, bf16[2,73,16,128]{3,2,1,0:T(8,128)(2,1)S(1)}, u32[]{:S(2)}, u32[]{:S(2)}) collective-permute-start(bf16[2,73,16,128]{3,2,1,0:T(8,128)(2,1)S(1)} %pad_maximum_fusion.1.refs_1_), channel_id=1, source_target_pairs={{0,6},{1,25},{2,4},{3,27},{4,2},{5,29},{6,0},{7,31},{8,14},{9,17},... | collective-permute-start | bytes 1794056 | tf_op jit(solution)/shard_map/ppermute | solution.py:99
  19.1 10.7 %collective-permute-start.15 = (bf16[2,73,16,128]{3,2,1,0:T(8,128)(2,1)S(1)}, bf16[2,73,16,128]{3,2,1,0:T(8,128)(2,1)S(1)}, u32[]{:S(2)}, u32[]{:S(2)}) collective-permute-start(bf16[2,73,16,128]{3,2,1,0:T(8,128)(2,1)S(1)} %pad_maximum_fusion.1.refs_1_), channel_id=1, source_target_pairs={{0,1},{1,0},{2,3},{3,2},{4,5},{5,4},{6,7},{7,6},{8,9},{9,8},{10,11... | collective-permute-start | bytes 1794056 | tf_op jit(solution)/shard_map/ppermute | solution.py:103
  21.8 9.1 %collective-permute-start.4 = (bf16[2,73,16,128]{3,2,1,0:T(8,128)(2,1)S(1)}, bf16[2,73,16,128]{3,2,1,0:T(8,128)(2,1)S(1)}, u32[]{:S(2)}, u32[]{:S(2)}) collective-permute-start(bf16[2,73,16,128]{3,2,1,0:T(8,128)(2,1)S(1)} %pad_maximum_fusion.1.refs_1_), channel_id=1, source_target_pairs={{0,2},{1,9},{2,0},{3,11},{4,6},{5,13},{6,4},{7,15},{8,10},{9,1},{1... | collective-permute-start | bytes 1794056 | tf_op jit(solution)/shard_map/ppermute | solution.py:99
  23.4 9.3 %collective-permute-start.18 = (bf16[2,73,16,128]{3,2,1,0:T(8,128)(2,1)S(1)}, bf16[2,73,16,128]{3,2,1,0:T(8,128)(2,1)S(1)}, u32[]{:S(2)}, u32[]{:S(2)}) collective-permute-start(bf16[2,73,16,128]{3,2,1,0:T(8,128)(2,1)S(1)} %collective-permute-done.5.refs_4_), channel_id=1, source_target_pairs={{0,1},{1,0},{2,3},{3,2},{4,5},{5,4},{6,7},{7,6},{8,9},{9,8},{10,11... | collective-permute-start | bytes 1794056 | tf_op jit(solution)/shard_map/ppermute | solution.py:103
  24.2 12.0 %collective-permute-start.7 = (bf16[2,73,16,128]{3,2,1,0:T(8,128)(2,1)S(1)}, bf16[2,73,16,128]{3,2,1,0:T(8,128)(2,1)S(1)}, u32[]{:S(2)}, u32[]{:S(2)}) collective-permute-start(bf16[2,73,16,128]{3,2,1,0:T(8,128)(2,1)S(1)} %collective-permute-done.3.refs_2_), channel_id=1, source_target_pairs={{0,6},{1,25},{2,4},{3,27},{4,2},{5,29},{6,0},{7,31},{8,14},{9,17},... | collective-permute-start | bytes 1794056 | tf_op jit(solution)/shard_map/ppermute | solution.py:99
  29.8 9.1 %collective-permute-start.8 = (bf16[2,73,16,128]{3,2,1,0:T(8,128)(2,1)S(1)}, bf16[2,73,16,128]{3,2,1,0:T(8,128)(2,1)S(1)}, u32[]{:S(2)}, u32[]{:S(2)}) collective-permute-start(bf16[2,73,16,128]{3,2,1,0:T(8,128)(2,1)S(1)} %collective-permute-done.6.refs_5_), channel_id=1, source_target_pairs={{0,2},{1,9},{2,0},{3,11},{4,6},{5,13},{6,4},{7,15},{8,10},{9,1},{1... | collective-permute-start | bytes 1794056 | tf_op jit(solution)/shard_map/ppermute | solution.py:99
  29.8 11.0 %collective-permute-start.16 = (bf16[2,73,16,128]{3,2,1,0:T(8,128)(2,1)S(1)}, bf16[2,73,16,128]{3,2,1,0:T(8,128)(2,1)S(1)}, u32[]{:S(2)}, u32[]{:S(2)}) collective-permute-start(bf16[2,73,16,128]{3,2,1,0:T(8,128)(2,1)S(1)} %collective-permute-done.3.refs_2_), channel_id=1, source_target_pairs={{0,1},{1,0},{2,3},{3,2},{4,5},{5,4},{6,7},{7,6},{8,9},{9,8},{10,11... | collective-permute-start | bytes 1794056 | tf_op jit(solution)/shard_map/ppermute | solution.py:103
  30.9 12.6 %collective-permute-start.19 = (bf16[2,73,16,128]{3,2,1,0:T(8,128)(2,1)S(1)}, bf16[2,73,16,128]{3,2,1,0:T(8,128)(2,1)S(1)}, u32[]{:S(2)}, u32[]{:S(2)}) collective-permute-start(bf16[2,73,16,128]{3,2,1,0:T(8,128)(2,1)S(1)} %collective-permute-done.6.refs_5_), channel_id=1, source_target_pairs={{0,1},{1,0},{2,3},{3,2},{4,5},{5,4},{6,7},{7,6},{8,9},{9,8},{10,11... | collective-permute-start | bytes 1794056 | tf_op jit(solution)/shard_map/ppermute | solution.py:103
  32.7 11.3 %collective-permute-start.17 = (bf16[2,73,16,128]{3,2,1,0:T(8,128)(2,1)S(1)}, bf16[2,73,16,128]{3,2,1,0:T(8,128)(2,1)S(1)}, u32[]{:S(2)}, u32[]{:S(2)}) collective-permute-start(bf16[2,73,16,128]{3,2,1,0:T(8,128)(2,1)S(1)} %collective-permute-done.4.refs_3_), channel_id=1, source_target_pairs={{0,1},{1,0},{2,3},{3,2},{4,5},{5,4},{6,7},{7,6},{8,9},{9,8},{10,11... | collective-permute-start | bytes 1794056 | tf_op jit(solution)/shard_map/ppermute | solution.py:103
  36.2 8.5 %collective-permute-start.12 = (bf16[2,73,16,128]{3,2,1,0:T(8,128)(2,1)S(1)}, bf16[2,73,16,128]{3,2,1,0:T(8,128)(2,1)S(1)}, u32[]{:S(2)}, u32[]{:S(2)}) collective-permute-start(bf16[2,73,16,128]{3,2,1,0:T(8,128)(2,1)S(1)} %collective-permute-done.7.refs_6_.refs_0_), channel_id=1, source_target_pairs={{0,1},{1,0},{2,3},{3,2},{4,5},{5,4},{6,7},{7,6},{8,9},{9,8},{10,11... | collective-permute-start | bytes 1794056 | tf_op jit(solution)/shard_map/ppermute | solution.py:103
  38.9 5.8 %collective-permute-start.13 = (bf16[2,73,16,128]{3,2,1,0:T(8,128)(2,1)S(1)}, bf16[2,73,16,128]{3,2,1,0:T(8,128)(2,1)S(1)}, u32[]{:S(2)}, u32[]{:S(2)}) collective-permute-start(bf16[2,73,16,128]{3,2,1,0:T(8,128)(2,1)S(1)} %collective-permute-done.8.refs_7_.refs_1_), channel_id=1, source_target_pairs={{0,1},{1,0},{2,3},{3,2},{4,5},{5,4},{6,7},{7,6},{8,9},{9,8},{10,11... | collective-permute-start | bytes 1794056 | tf_op jit(solution)/shard_map/ppermute | solution.py:103
  40.9 10.7 %collective-permute-start.11 = (bf16[16,16,128]{2,1,0:T(8,128)(2,1)S(1)}, bf16[16,16,128]{2,1,0:T(8,128)(2,1)S(1)}, u32[]{:S(2)}, u32[]{:S(2)}) collective-permute-start(bf16[16,16,128]{2,1,0:T(8,128)(2,1)S(1)} %tops.1), channel_id=1, source_target_pairs={{0,96},{32,64},{64,32},{96,0},{1,97},{33,65},{65,33},{97,1},{2,98}... | collective-permute-start | bytes 196616 | tf_op jit(solution)/shard_map/ppermute | solution.py:367
  43.4 8.1 %collective-permute-start.10 = (bf16[16,16,128]{2,1,0:T(8,128)(2,1)S(1)}, bf16[16,16,128]{2,1,0:T(8,128)(2,1)S(1)}, u32[]{:S(2)}, u32[]{:S(2)}) collective-permute-start(bf16[16,16,128]{2,1,0:T(8,128)(2,1)S(1)} %tops.1), channel_id=1, source_target_pairs={{0,64},{32,96},{64,0},{96,32},{1,65},{33,97},{65,1},{97,33},{2,66}... | collective-permute-start | bytes 196616 | tf_op jit(solution)/shard_map/ppermute | solution.py:367
  44.0 7.6 %collective-permute-start.9 = (bf16[16,16,128]{2,1,0:T(8,128)(2,1)S(1)}, bf16[16,16,128]{2,1,0:T(8,128)(2,1)S(1)}, u32[]{:S(2)}, u32[]{:S(2)}) collective-permute-start(bf16[16,16,128]{2,1,0:T(8,128)(2,1)S(1)} %tops.1), channel_id=1, source_target_pairs={{0,32},{32,0},{64,96},{96,64},{1,33},{33,1},{65,97},{97,65},{2,34}... | collective-permute-start | bytes 196616 | tf_op jit(solution)/shard_map/ppermute | solution.py:367
  44.7 0.7 %copy-start.4 = (s32[64,16]{0,1:T(8,128)S(1)}, s32[64,16]{0,1:T(8,128)}, u32[]{:S(2)}) copy-start(s32[64,16]{0,1:T(8,128)} %param.25) | copy-start | bytes 12292
  44.7 0.7 %copy-start.5 = (s32[64,16]{0,1:T(8,128)S(1)}, s32[64,16]{0,1:T(8,128)}, u32[]{:S(2)}) copy-start(s32[64,16]{0,1:T(8,128)} %param.26) | copy-start | bytes 12292
  44.7 0.7 %copy-start.6 = (s32[8,16]{1,0:T(8,128)S(1)}, s32[8,16]{1,0:T(8,128)}, u32[]{:S(2)}) copy-start(s32[8,16]{1,0:T(8,128)} %parent_owner.1) | copy-start | bytes 1540
  44.7 0.7 %copy-start.7 = (s32[8,16]{1,0:T(8,128)S(1)}, s32[8,16]{1,0:T(8,128)}, u32[]{:S(2)}) copy-start(s32[8,16]{1,0:T(8,128)} %parent_index.1) | copy-start | bytes 1540
  45.4 8.3 %copy-start = (bf16[64,64,256]{2,1,0:T(8,128)(2,1)S(1)}, bf16[64,64,256]{2,1,0:T(8,128)(2,1)}, u32[]{:S(2)}) copy-start(bf16[64,64,256]{2,1,0:T(8,128)(2,1)} %out_basis.1) | copy-start | bytes 6291460
  45.4 8.3 %copy-start.1 = (bf16[64,64,64]{2,1,0:T(8,128)(2,1)S(1)}, bf16[64,64,64]{2,1,0:T(8,128)(2,1)}, u32[]{:S(2)}) copy-start(bf16[64,64,64]{2,1,0:T(8,128)(2,1)} %leaf_descend.1) | copy-start | bytes 1572868
  45.4 8.4 %copy-start.2 = (bf16[1,16,64,64]{3,2,1,0:T(8,128)(2,1)S(1)}, bf16[1,16,64,64]{3,2,1,0:T(8,128)(2,1)}, u32[]{:S(2)}) copy-start(bf16[1,16,64,64]{3,2,1,0:T(8,128)(2,1)} %top_coupling.1) | copy-start | bytes 393220
  45.4 8.4 %copy-start.3 = (bf16[8,64,64]{2,1,0:T(8,128)(2,1)S(1)}, bf16[8,64,64]{2,1,0:T(8,128)(2,1)}, u32[]{:S(2)}) copy-start(bf16[8,64,64]{2,1,0:T(8,128)(2,1)} %parent_descend.1) | copy-start | bytes 196612
  45.4 8.4 %copy-start.8 = (s32[64]{0:T(128)S(1)}, s32[64]{0:T(128)}, u32[]{:S(2)}) copy-start(s32[64]{0:T(128)} %counts.3) | copy-start | bytes 772
  45.5 8.4 %copy-start.9 = (s32[1,16]{1,0:T(1,128)S(1)}, s32[1,16]{1,0:T(1,128)}, u32[]{:S(2)}) copy-start(s32[1,16]{1,0:T(1,128)} %top_source.1) | copy-start | bytes 196
  51.6 2.1 %collective-permute-start.20 = (bf16[64,16,128]{2,1,0:T(8,128)(2,1)S(1)}, bf16[64,16,128]{2,1,0:T(8,128)(2,1)S(1)}, u32[]{:S(2)}, u32[]{:S(2)}) collective-permute-start(bf16[64,16,128]{2,1,0:T(8,128)(2,1)S(1)} %pad_maximum_fusion.2), channel_id=1, source_target_pairs={{0,1},{1,0},{2,3},{3,2},{4,5},{5,4},{6,7},{7,6},{8,9},{9,8},{10,11... | collective-permute-start | bytes 786440 | tf_op jit(solution)/shard_map/ppermute | solution.py:103

commit v4 on v3

--- a/solution.py
+++ b/solution.py
@@ -180,73 +180,62 @@
 
 
 CHUNK = 8
-STAGED = 24
-
-
-def stage_kernel(coupling, out, sem):
+STAGED = 16
+
+
+def stage_kernel(place, *refs):
+    names, coupling, head, leaf_rows, parent_rows, top_rows = refs[:5], refs[5], *refs[6:10]
+    held, sem = refs[10:15], refs[15]
+    reads = [pltpu.make_async_copy(src, dst, sem.at[i]) for i, (src, dst) in enumerate(zip(names, held))]
     parts = 4
-    size = out.shape[0] // parts
+    size = head.shape[0] // parts
     copies = []
     for k in range(parts):
-        source = coupling.at[pl.ds(k * size, size)]
-        copies.append(pltpu.make_async_copy(source, out.at[pl.ds(k * size, size)], sem.at[k]))
-        copies[k].start()
+        part = pl.ds(k * size, size)
+        copies.append(pltpu.make_async_copy(coupling.at[part], head.at[part], sem.at[5 + k]))
+    for copy in reads + copies:
+        copy.start()
+    for copy in reads:
+        copy.wait()
+    x, y, z, c = (place[i] for i in range(4))
+    far_owner, far_local, parent_owner, parent_index, source = (ref[...] for ref in held)
+    leaf_rows[...] = slots(far_owner, y, z, c) * ROWS + far_local
+    parent_rows[...] = slots(parent_owner, y, z, c) * ROWS + LEAF + parent_index
+    slot = slots(source % 32, y, z, c)
+    top_rows[...] = slot // 16 * 64 + ((source // 32) ^ x) * 16 + slot % 16
     for copy in copies:
         copy.wait()
 
 
-def stage(coupling, count):
+def stage(place, far_owner, far_local, parent_owner, parent_index, top_source, coupling, count):
+    smem, vmem = pl.BlockSpec(memory_space=pltpu.SMEM), pl.BlockSpec(memory_space=pltpu.VMEM)
+    names = (far_owner, far_local, parent_owner, parent_index, top_source)
+    hbm = lambda a: pltpu.with_memory_space_constraint(a, pltpu.HBM)
     return pl.pallas_call(
         stage_kernel,
-        in_specs=[pl.BlockSpec(memory_space=pltpu.HBM)],
-        out_specs=pl.BlockSpec(memory_space=pltpu.VMEM),
-        out_shape=jax.ShapeDtypeStruct((count,) + coupling.shape[1:], BF16),
-        scratch_shapes=[pltpu.SemaphoreType.DMA((4,))],
+        in_specs=[smem] + [pl.BlockSpec(memory_space=pltpu.HBM)] * 6,
+        out_specs=[vmem] * 4,
+        out_shape=[jax.ShapeDtypeStruct((count,) + coupling.shape[1:], BF16)]
+        + [jax.ShapeDtypeStruct(x.shape, jnp.int32) for x in (far_owner, parent_owner, top_source)],
+        scratch_shapes=[pltpu.VMEM(x.shape, jnp.int32) for x in names] + [pltpu.SemaphoreType.DMA((9,))],
         compiler_params=pltpu.CompilerParams(vmem_limit_bytes=2 * MIB),
         cost_estimate=pl.CostEstimate(flops=0, bytes_accessed=4096, transcendentals=0),
         name="stage",
-    )(pltpu.with_memory_space_constraint(coupling, pltpu.HBM))
+    )(place, *map(hbm, names), hbm(coupling))
 
 
 def couple_kernel(
-    place,
-    far_owner,
-    far_local,
-    parent_owner,
-    parent_index,
-    gathered,
-    head,
-    coupling,
-    parent_coupling,
-    leaf_far,
-    parent_far,
-    staged,
-    parent_staged,
-    leaf_rows,
-    parent_rows,
-    leaf_named,
-    parent_named,
-    chunk_sem,
-    row_sem,
+    leaf_rows, gathered, head, coupling, parent_coupling, leaf_far, parent_staged, staged, leaf_named, chunk_sem, row_sem
 ):
     chunks = []
     for k in range((LEAF - STAGED) // CHUNK):
         source = coupling.at[pl.ds(STAGED + k * CHUNK, CHUNK)]
         chunks.append(pltpu.make_async_copy(source, staged.at[pl.ds(k * CHUNK, CHUNK)], chunk_sem.at[k]))
     chunks.append(pltpu.make_async_copy(parent_coupling, parent_staged, chunk_sem.at[len(chunks)]))
-    for copy in chunks:
+    named = pltpu.make_async_copy(leaf_rows, leaf_named, row_sem)
+    for copy in [named] + chunks:
         copy.start()
-    y, z, c = place[1], place[2], place[3]
-    leaf_rows[...] = slots(far_owner[...], y, z, c) * ROWS + far_local[...]
-    parent_rows[...] = slots(parent_owner[...], y, z, c) * ROWS + LEAF + parent_index[...]
-    named = [
-        pltpu.make_async_copy(leaf_rows, leaf_named, row_sem.at[0]),
-        pltpu.make_async_copy(parent_rows, parent_named, row_sem.at[1]),
-    ]
-    for copy in named:
-        copy.start()
-    for copy in named:
-        copy.wait()
+    named.wait()
     for b in range(STAGED):
         block = picked(lambda j: gathered[leaf_named[j, b]], 16)
         leaf_far[b] = dot(block, head[b].reshape(1024, 64))
@@ -256,37 +245,49 @@
             block = picked(lambda j: gathered[leaf_named[j, STAGED + i]], 16)
             leaf_far[STAGED + i] = dot(block, staged[i].reshape(1024, 64))
     chunks[-1].wait()
+
+
+def couple_parents_kernel(parent_rows, gathered, coupling, far, named, sem):
+    copy = pltpu.make_async_copy(parent_rows, named, sem)
+    copy.start()
+    copy.wait()
     for q in range(PARENT):
-        block = picked(lambda j: gathered[parent_named[q, j]], 16)
-        parent_far[q] = dot(block, parent_staged[q].reshape(1024, 64))
-
-
-def couple(place, far_owner, far_local, parent_owner, parent_index, gathered, head, coupling, parent_coupling):
-    smem, vmem = pl.BlockSpec(memory_space=pltpu.SMEM), pl.BlockSpec(memory_space=pltpu.VMEM)
+        block = picked(lambda j: gathered[named[q, j]], 16)
+        far[q] = dot(block, coupling[q].reshape(1024, 64))
+
+
+def couple_parents(parent_rows, gathered, coupling):
+    vmem = pl.BlockSpec(memory_space=pltpu.VMEM)
+    return pl.pallas_call(
+        couple_parents_kernel,
+        in_specs=[vmem] * 3,
+        out_specs=vmem,
+        out_shape=jax.ShapeDtypeStruct((PARENT, 32, 64), F32),
+        scratch_shapes=[pltpu.SMEM(parent_rows.shape, jnp.int32), pltpu.SemaphoreType.DMA],
+        compiler_params=pltpu.CompilerParams(vmem_limit_bytes=4 * MIB),
+        cost_estimate=pl.CostEstimate(flops=2 * 8 * 32 * 64 * 1024, bytes_accessed=3 * MIB, transcendentals=0),
+        name="couple_parents",
+    )(parent_rows, gathered, coupling)
+
+
+def couple(leaf_rows, gathered, head, coupling, parent_coupling):
+    vmem = pl.BlockSpec(memory_space=pltpu.VMEM)
     return pl.pallas_call(
         couple_kernel,
-        in_specs=[smem] + [vmem] * 6 + [pl.BlockSpec(memory_space=pltpu.HBM)] * 2,
+        in_specs=[vmem] * 3 + [pl.BlockSpec(memory_space=pltpu.HBM)] * 2,
         out_specs=[vmem, vmem],
-        out_shape=[jax.ShapeDtypeStruct((LEAF, 32, 64), F32), jax.ShapeDtypeStruct((PARENT, 32, 64), F32)],
+        out_shape=[jax.ShapeDtypeStruct((LEAF, 32, 64), F32), jax.ShapeDtypeStruct(parent_coupling.shape, BF16)],
         scratch_shapes=[
             pltpu.VMEM((LEAF - STAGED,) + coupling.shape[1:], BF16),
-            pltpu.VMEM(parent_coupling.shape, BF16),
-            pltpu.VMEM(far_owner.shape, jnp.int32),
-            pltpu.VMEM(parent_owner.shape, jnp.int32),
-            pltpu.SMEM(far_owner.shape, jnp.int32),
-            pltpu.SMEM(parent_owner.shape, jnp.int32),
+            pltpu.SMEM(leaf_rows.shape, jnp.int32),
             pltpu.SemaphoreType.DMA(((LEAF - STAGED) // CHUNK + 1,)),
-            pltpu.SemaphoreType.DMA((2,)),
+            pltpu.SemaphoreType.DMA,
         ],
         compiler_params=pltpu.CompilerParams(vmem_limit_bytes=18 * MIB),
         cost_estimate=pl.CostEstimate(flops=2 * 72 * 32 * 64 * 1024, bytes_accessed=28 * MIB, transcendentals=0),
         name="couple",
     )(
-        place,
-        far_owner,
-        far_local,
-        parent_owner,
-        parent_index,
+        leaf_rows,
         gathered,
         head,
         pltpu.with_memory_space_constraint(coupling, pltpu.HBM),
@@ -295,16 +296,9 @@
 
 
 def down_kernel(
-    counts, place, top_source, tops, top_coupling, parent_far, parent_descend, leaf_far, leaf_descend, out_basis, out, values, sem
+    counts, top_rows, tops, top_coupling, parent_far, parent_descend, leaf_far, leaf_descend, out_basis, out, values, sem
 ):
-    x, y, z, c = (place[i] for i in range(4))
-
-    def top(j):
-        source = top_source[0, j]
-        slot = slots(source % 32, y, z, c)
-        return tops[slot // 16 * 64 + ((source // 32) ^ x) * 16 + slot % 16]
-
-    block = picked(top, 16)
+    block = picked(lambda j: tops[top_rows[0, j]], 16)
     top_field = dot(block, top_coupling[0].reshape(1024, 64)).astype(BF16)
     column = lax.broadcasted_iota(jnp.int32, (32, 256), 1)
     parents = [(parent_far[q] + dot(top_field, parent_descend[q])).astype(BF16) for q in range(PARENT)]
@@ -321,18 +315,18 @@
         copy.wait()
 
 
-def down(counts, place, top_source, *operands):
+def down(counts, top_rows, *operands):
     smem, vmem = pl.BlockSpec(memory_space=pltpu.SMEM), pl.BlockSpec(memory_space=pltpu.VMEM)
     return pl.pallas_call(
         down_kernel,
-        in_specs=[smem] * 3 + [vmem] * len(operands),
+        in_specs=[smem] * 2 + [vmem] * len(operands),
         out_specs=pl.BlockSpec(memory_space=pltpu.HBM),
         out_shape=jax.ShapeDtypeStruct((64, 32, 256), BF16),
         scratch_shapes=[pltpu.VMEM((64, 32, 256), BF16), pltpu.SemaphoreType.DMA((PARENT,))],
         compiler_params=pltpu.CompilerParams(vmem_limit_bytes=4 * MIB),
         cost_estimate=pl.CostEstimate(flops=2 * 64 * 32 * 64 * 320, bytes_accessed=6 * MIB, transcendentals=0),
         name="down",
-    )(counts, place, top_source, *operands)
+    )(counts, top_rows, *operands)
 
 
 def body(
@@ -359,20 +353,22 @@
 
     hbm = lambda a: pltpu.with_memory_space_constraint(a, pltpu.HBM)
     coeffs = up(*map(hbm, (counts, charges, leaf_basis, leaf_transfer, parent_transfer)))
-    early, late, head = gather(coeffs, stage(leaf_coupling, STAGED))
+    names = (far_owner.T, far_local.T, parent_owner, parent_index, top_source)
+    early, late, prepared = gather(coeffs, stage(place, *names, leaf_coupling, STAGED))
+    head, leaf_rows, parent_rows, top_rows = prepared
     swap = lambda pieces: [(other_core(piece), 16 + first) for piece, first in pieces]
     gathered = assemble(early + swap(early))
     gathered = assemble(late + swap(late), gathered)
     tops = column_tops(early + late)
     planes = [tops] + [lax.ppermute(tops, "x", [(i, i ^ m) for i in range(4)]) for m in (1, 2, 3)]
 
-    names = (far_owner.T, far_local.T, parent_owner, parent_index)
-    leaf_far, parent_far = couple(place, *names, gathered, head, leaf_coupling, parent_coupling)
+    leaf_far, parent_staged = couple(leaf_rows, gathered, head, leaf_coupling, parent_coupling)
     planes, leaf_far = lax.optimization_barrier((planes, leaf_far))
     tops = jnp.concatenate(planes)
     tops = jnp.concatenate([tops, other_core(tops)])
+    parent_far = couple_parents(parent_rows, gathered, parent_staged)
     return down(
-        counts, place, top_source, tops, top_coupling, parent_far, parent_descend, leaf_far, leaf_descend, out_basis
+        counts, top_rows, tops, top_coupling, parent_far, parent_descend, leaf_far, leaf_descend, out_basis
     )
 
 

time: 56.8 us -> 55.8 us (0.982)
  waiting for transfers between devices: 13.1 us -> 12 us
    ppermute x9, waiting for transfers between devices: 1.13 us -> 0.02 us  [other_core(): return lax.ppermute(x, 'c', [(0, 1), (1, 0)])]
    pallas_call x3 -> x4, Pallas kernels: 11.7 us -> 11.8 us  [the longest x1 5.33 us: couple(): pl.pallas_call(couple_kernel, in_specs=[vmem] * 3 + [pl.BlockSpec(memory_...]
  transfers between devices with their start and end apart: 21 -> 21, of which waited for: 7 -> 6; matrix products, arithmetic and copies ran while one was open for 0% -> 0% of each run, Pallas kernels for 17% -> 18%
where the time goes in v4:
time: 55.8 us; the launch traced here: 55.6 us
  starting transfers between devices  26.9 us (48%)
  Pallas kernels  15.6 us (28%)
  waiting for transfers between devices  12 us (22%)
  local copies, waits for them, and re-layouts  0.75 us (1%)
    ppermute x9, starting transfers between devices, send(): return lax.ppermute(x, ('y', 'z', 'c'), pairs(second, mask))  13.3 us
    ppermute x9, waiting for transfers between devices, send(): return lax.ppermute(x, ('y', 'z', 'c'), pairs(second, mask))  11.9 us
    ppermute x9, starting transfers between devices, other_core(): return lax.ppermute(x, 'c', [(0, 1), (1, 0)])  10.2 us
    pallas_call x1, Pallas kernels, couple(): pl.pallas_call(couple_kernel, in_specs=[vmem] * 3 + [pl.BlockSpec(memory_...  5.33 us
    ppermute x3, starting transfers between devices, body(): lax.ppermute(tops, 'x', [(i, i ^ m) for i in range(4)])  3.33 us
    pallas_call x1, Pallas kernels, up(): pl.pallas_call(up_kernel, in_specs=[hbm] * 5, out_specs=pl.BlockSpec(memo...  2.98 us
    pallas_call x1, Pallas kernels, stage(): pl.pallas_call(stage_kernel, in_specs=[smem] + [pl.BlockSpec(memory_space...  2.87 us
    pallas_call x1, Pallas kernels, down(): pl.pallas_call(down_kernel, in_specs=[smem] * 2 + [vmem] * len(operands),...  2.43 us
  transfers between devices with their start and end apart: 21, of which 6 were waited for; matrix products, arithmetic and copies ran while one was open for 0% of the time, Pallas kernels for 18%

profile of v4, /device:TPU:1, one launch (start us, length us, event | category | flops | bytes accessed | tf_op | source)
XLA Modules:
  0.0 55.6 jit_solution(8322172358863847577)
XLA Ops:
  0.1 3.0 %up.1 = bf16[73,16,128]{2,1,0:T(8,128)(2,1)S(1)} custom-call(s32[64]{0:T(128)} %counts.3, bf16[64,32,256]{2,1,0:T(8,128)(2,1)} %charges, bf16[64,64,256]{2,1,0:T(8,128)(2,1)} %basis.1, bf16[64,64,64]{2,1,0:T(8,128)(2,1)} %transfer.1, bf16[8,64,64]{2,1,0:T(8,128)(2,1)} %parent_transfer.1), custom_call_target="tpu_custom_call" | custom-call | flops 83886080 | bytes 5242880 | tf_op jit(solution)/shard_map/up/pallas_call | solution.py:73
  3.1 2.5 %collective-permute-start.2 = (bf16[1,73,16,128]{3,2,1,0:T(8,128)(2,1)S(1)}, bf16[1,73,16,128]{3,2,1,0:T(8,128)(2,1)S(1)}, u32[]{:S(2)}, u32[]{:S(2)}) collective-permute-start(bf16[1,73,16,128]{3,2,1,0:T(8,128)(2,1)S(1)} %bitcast.7), channel_id=1, source_target_pairs={{0,8},{1,3},{2,10},{3,1},{4,12},{5,7},{6,14},{7,5},{8,0},{9,11},{1... | collective-permute-start | bytes 897032 | tf_op jit(solution)/shard_map/ppermute | solution.py:99
  5.6 2.2 %collective-permute-start.1 = (bf16[1,73,16,128]{3,2,1,0:T(8,128)(2,1)S(1)}, bf16[1,73,16,128]{3,2,1,0:T(8,128)(2,1)S(1)}, u32[]{:S(2)}, u32[]{:S(2)}) collective-permute-start(bf16[1,73,16,128]{3,2,1,0:T(8,128)(2,1)S(1)} %bitcast.8), channel_id=1, source_target_pairs={{0,24},{1,7},{2,26},{3,5},{4,28},{5,3},{6,30},{7,1},{8,16},{9,15},... | collective-permute-start | bytes 897032 | tf_op jit(solution)/shard_map/ppermute | solution.py:99
  7.9 1.1 %collective-permute-start = (bf16[1,73,16,128]{3,2,1,0:T(8,128)(2,1)S(1)}, bf16[1,73,16,128]{3,2,1,0:T(8,128)(2,1)S(1)}, u32[]{:S(2)}, u32[]{:S(2)}) collective-permute-start(bf16[1,73,16,128]{3,2,1,0:T(8,128)(2,1)S(1)} %bitcast.9), channel_id=1, source_target_pairs={{0,16},{1,5},{2,18},{3,7},{4,20},{5,1},{6,22},{7,3},{8,24},{9,13},... | collective-permute-start | bytes 897032 | tf_op jit(solution)/shard_map/ppermute | solution.py:99
  8.9 2.9 %stage.1 = (bf16[16,16,64,64]{3,2,1,0:T(8,128)(2,1)S(1)}, s32[16,64]{1,0:T(8,128)S(1)}, s32[8,16]{1,0:T(8,128)S(1)}, s32[1,16]{1,0:T(1,128)S(1)}) custom-call(s32[4]{0:T(128)S(1)} %pad_add_fusion.place, s32[16,64]{1,0:T(8,128)} %bitcast.11, s32[16,64]{1,0:T(8,128)} %bitcast.12, s32[8,16]{1,0:T(8,128)} %refs_2_.1, s32[8,16]{1,0:T(8,128)} %refs_3_.1, ...), custom_call_target="tpu_custom_call" | custom-call | bytes 4096 | tf_op jit(solution)/shard_map/stage/pallas_call | solution.py:214
  11.9 0.3 collective-permute-start.14
  12.2 2.6 %collective-permute-start.5 = (bf16[2,73,16,128]{3,2,1,0:T(8,128)(2,1)S(1)}, bf16[2,73,16,128]{3,2,1,0:T(8,128)(2,1)S(1)}, u32[]{:S(2)}, u32[]{:S(2)}) collective-permute-start(bf16[2,73,16,128]{3,2,1,0:T(8,128)(2,1)S(1)} %pad_maximum_fusion.1.refs_0_), channel_id=1, source_target_pairs={{0,6},{1,25},{2,4},{3,27},{4,2},{5,29},{6,0},{7,31},{8,14},{9,17},... | collective-permute-start | bytes 1794056 | tf_op jit(solution)/shard_map/ppermute | solution.py:99
  14.8 1.8 %collective-permute-done = bf16[1,73,16,128]{3,2,1,0:T(8,128)(2,1)S(1)} collective-permute-done((bf16[1,73,16,128]{3,2,1,0:T(8,128)(2,1)S(1)}, bf16[1,73,16,128]{3,2,1,0:T(8,128)(2,1)S(1)}, u32[]{:S(2)}, u32[]{:S(2)}) %collective-permute-start) | collective-permute-done | bytes 299040 | tf_op jit(solution)/shard_map/ppermute | solution.py:99
  16.6 2.5 %collective-permute-start.6 = (bf16[2,73,16,128]{3,2,1,0:T(8,128)(2,1)S(1)}, bf16[2,73,16,128]{3,2,1,0:T(8,128)(2,1)S(1)}, u32[]{:S(2)}, u32[]{:S(2)}) collective-permute-start(bf16[2,73,16,128]{3,2,1,0:T(8,128)(2,1)S(1)} %pad_maximum_fusion.refs_1_), channel_id=1, source_target_pairs={{0,6},{1,25},{2,4},{3,27},{4,2},{5,29},{6,0},{7,31},{8,14},{9,17},... | collective-permute-start | bytes 1794056 | tf_op jit(solution)/shard_map/ppermute | solution.py:99
  19.1 2.6 %collective-permute-start.15 = (bf16[2,73,16,128]{3,2,1,0:T(8,128)(2,1)S(1)}, bf16[2,73,16,128]{3,2,1,0:T(8,128)(2,1)S(1)}, u32[]{:S(2)}, u32[]{:S(2)}) collective-permute-start(bf16[2,73,16,128]{3,2,1,0:T(8,128)(2,1)S(1)} %pad_maximum_fusion.refs_1_), channel_id=1, source_target_pairs={{0,1},{1,0},{2,3},{3,2},{4,5},{5,4},{6,7},{7,6},{8,9},{9,8},{10,11... | collective-permute-start | bytes 1794056 | tf_op jit(solution)/shard_map/ppermute | solution.py:103
  21.8 1.7 %collective-permute-done.5.refs_4_ = bf16[2,73,16,128]{3,2,1,0:T(8,128)(2,1)S(1)} collective-permute-done((bf16[2,73,16,128]{3,2,1,0:T(8,128)(2,1)S(1)}, bf16[2,73,16,128]{3,2,1,0:T(8,128)(2,1)S(1)}, u32[]{:S(2)}, u32[]{:S(2)}) %collective-permute-start.5) | collective-permute-done | bytes 598048 | tf_op jit(solution)/shard_map/ppermute | solution.py:99
  23.4 0.8 %collective-permute-start.18 = (bf16[2,73,16,128]{3,2,1,0:T(8,128)(2,1)S(1)}, bf16[2,73,16,128]{3,2,1,0:T(8,128)(2,1)S(1)}, u32[]{:S(2)}, u32[]{:S(2)}) collective-permute-start(bf16[2,73,16,128]{3,2,1,0:T(8,128)(2,1)S(1)} %collective-permute-done.5.refs_4_), channel_id=1, source_target_pairs={{0,1},{1,0},{2,3},{3,2},{4,5},{5,4},{6,7},{7,6},{8,9},{9,8},{10,11... | collective-permute-start | bytes 1794056 | tf_op jit(solution)/shard_map/ppermute | solution.py:103
  24.3 2.3 %collective-permute-start.7 = (bf16[2,73,16,128]{3,2,1,0:T(8,128)(2,1)S(1)}, bf16[2,73,16,128]{3,2,1,0:T(8,128)(2,1)S(1)}, u32[]{:S(2)}, u32[]{:S(2)}) collective-permute-start(bf16[2,73,16,128]{3,2,1,0:T(8,128)(2,1)S(1)} %collective-permute-done.3.refs_2_), channel_id=1, source_target_pairs={{0,6},{1,25},{2,4},{3,27},{4,2},{5,29},{6,0},{7,31},{8,14},{9,17},... | collective-permute-start | bytes 1794056 | tf_op jit(solution)/shard_map/ppermute | solution.py:99
  26.6 3.2 %collective-permute-done.6.refs_5_ = bf16[2,73,16,128]{3,2,1,0:T(8,128)(2,1)S(1)} collective-permute-done((bf16[2,73,16,128]{3,2,1,0:T(8,128)(2,1)S(1)}, bf16[2,73,16,128]{3,2,1,0:T(8,128)(2,1)S(1)}, u32[]{:S(2)}, u32[]{:S(2)}) %collective-permute-start.6) | collective-permute-done | bytes 598048 | tf_op jit(solution)/shard_map/ppermute | solution.py:99
  29.8 0.8 %collective-permute-start.16 = (bf16[2,73,16,128]{3,2,1,0:T(8,128)(2,1)S(1)}, bf16[2,73,16,128]{3,2,1,0:T(8,128)(2,1)S(1)}, u32[]{:S(2)}, u32[]{:S(2)}) collective-permute-start(bf16[2,73,16,128]{3,2,1,0:T(8,128)(2,1)S(1)} %collective-permute-done.3.refs_2_), channel_id=1, source_target_pairs={{0,1},{1,0},{2,3},{3,2},{4,5},{5,4},{6,7},{7,6},{8,9},{9,8},{10,11... | collective-permute-start | bytes 1794056 | tf_op jit(solution)/shard_map/ppermute | solution.py:103
  30.7 0.2 collective-permute-done.4.refs_3_
  30.9 1.8 %collective-permute-start.19 = (bf16[2,73,16,128]{3,2,1,0:T(8,128)(2,1)S(1)}, bf16[2,73,16,128]{3,2,1,0:T(8,128)(2,1)S(1)}, u32[]{:S(2)}, u32[]{:S(2)}) collective-permute-start(bf16[2,73,16,128]{3,2,1,0:T(8,128)(2,1)S(1)} %collective-permute-done.6.refs_5_), channel_id=1, source_target_pairs={{0,1},{1,0},{2,3},{3,2},{4,5},{5,4},{6,7},{7,6},{8,9},{9,8},{10,11... | collective-permute-start | bytes 1794056 | tf_op jit(solution)/shard_map/ppermute | solution.py:103
  32.7 3.5 %collective-permute-done.7.refs_6_.refs_0_ = bf16[2,73,16,128]{3,2,1,0:T(8,128)(2,1)S(1)} collective-permute-done((bf16[2,73,16,128]{3,2,1,0:T(8,128)(2,1)S(1)}, bf16[2,73,16,128]{3,2,1,0:T(8,128)(2,1)S(1)}, u32[]{:S(2)}, u32[]{:S(2)}) %collective-permute-start.7) | collective-permute-done | bytes 598048 | tf_op jit(solution)/shard_map/ppermute | solution.py:99
  36.2 1.2 %collective-permute-start.12 = (bf16[2,73,16,128]{3,2,1,0:T(8,128)(2,1)S(1)}, bf16[2,73,16,128]{3,2,1,0:T(8,128)(2,1)S(1)}, u32[]{:S(2)}, u32[]{:S(2)}) collective-permute-start(bf16[2,73,16,128]{3,2,1,0:T(8,128)(2,1)S(1)} %collective-permute-done.7.refs_6_.refs_0_), channel_id=1, source_target_pairs={{0,1},{1,0},{2,3},{3,2},{4,5},{5,4},{6,7},{7,6},{8,9},{9,8},{10,11... | collective-permute-start | bytes 1794056 | tf_op jit(solution)/shard_map/ppermute | solution.py:103
  37.5 1.5 %collective-permute-done.8.refs_7_.refs_1_ = bf16[2,73,16,128]{3,2,1,0:T(8,128)(2,1)S(1)} collective-permute-done((bf16[2,73,16,128]{3,2,1,0:T(8,128)(2,1)S(1)}, bf16[2,73,16,128]{3,2,1,0:T(8,128)(2,1)S(1)}, u32[]{:S(2)}, u32[]{:S(2)}) %collective-permute-start.8) | collective-permute-done | bytes 598048 | tf_op jit(solution)/shard_map/ppermute | solution.py:99
  38.9 1.7 %collective-permute-start.13 = (bf16[2,73,16,128]{3,2,1,0:T(8,128)(2,1)S(1)}, bf16[2,73,16,128]{3,2,1,0:T(8,128)(2,1)S(1)}, u32[]{:S(2)}, u32[]{:S(2)}) collective-permute-start(bf16[2,73,16,128]{3,2,1,0:T(8,128)(2,1)S(1)} %collective-permute-done.8.refs_7_.refs_1_), channel_id=1, source_target_pairs={{0,1},{1,0},{2,3},{3,2},{4,5},{5,4},{6,7},{7,6},{8,9},{9,8},{10,11... | collective-permute-start | bytes 1794056 | tf_op jit(solution)/shard_map/ppermute | solution.py:103
  40.6 0.2 tops.1
  40.9 2.6 %collective-permute-start.11 = (bf16[16,16,128]{2,1,0:T(8,128)(2,1)S(1)}, bf16[16,16,128]{2,1,0:T(8,128)(2,1)S(1)}, u32[]{:S(2)}, u32[]{:S(2)}) collective-permute-start(bf16[16,16,128]{2,1,0:T(8,128)(2,1)S(1)} %tops.1), channel_id=1, source_target_pairs={{0,96},{32,64},{64,32},{96,0},{1,97},{33,65},{65,33},{97,1},{2,98}... | collective-permute-start | bytes 196616 | tf_op jit(solution)/shard_map/ppermute | solution.py:363
  43.4 0.5 collective-permute-start.10
  44.0 0.3 collective-permute-start.9
  44.2 0.5 assemble.2.refs_4_
  44.9 5.3 %couple.1 = (f32[64,32,64]{2,1,0:T(8,128)S(1)}, bf16[8,16,64,64]{3,2,1,0:T(8,128)(2,1)S(1)}) custom-call(s32[16,64]{1,0:T(8,128)S(1)} %get-tuple-element.31.leaf_rows, bf16[2336,16,128]{2,1,0:T(8,128)(2,1)S(1)} %assemble.3.gathered, bf16[16,16,64,64]{3,2,1,0:T(8,128)(2,1)S(1)} %get-tuple-element.32.head, bf16[64,16,64,64]{3,2,1,0:T(8,128)(2,1)} %coupling.1, ...), custom_call_target="tpu_custom_call" | custom-call | flops 301989888 | bytes 29360128 | tf_op jit(solution)/shard_map/couple/pallas_call | solution.py:275
  50.3 0.9 %collective-permute-start.20 = (bf16[64,16,128]{2,1,0:T(8,128)(2,1)S(1)}, bf16[64,16,128]{2,1,0:T(8,128)(2,1)S(1)}, u32[]{:S(2)}, u32[]{:S(2)}) collective-permute-start(bf16[64,16,128]{2,1,0:T(8,128)(2,1)S(1)} %pad_maximum_fusion.2), channel_id=1, source_target_pairs={{0,1},{1,0},{2,3},{3,2},{4,5},{5,4},{6,7},{7,6},{8,9},{9,8},{10,11... | collective-permute-start | bytes 786440 | tf_op jit(solution)/shard_map/ppermute | solution.py:103
  51.3 1.1 %couple_parents.1.parent_far = f32[8,32,64]{2,1,0:T(8,128)S(1)} custom-call(s32[8,16]{1,0:T(8,128)S(1)} %get-tuple-element.38.parent_rows, bf16[2336,16,128]{2,1,0:T(8,128)(2,1)S(1)} %assemble.3.gathered, bf16[8,16,64,64]{3,2,1,0:T(8,128)(2,1)S(1)} %get-tuple-element.39.coupling), custom_call_target="tpu_custom_call" | custom-call | flops 33554432 | bytes 3145728 | tf_op jit(solution)/shard_map/couple_parents/pallas_call | solution.py:261
  52.5 0.3 copy-done
  52.9 0.3 copy-done.1
  53.2 2.4 %down.1 = bf16[64,32,256]{2,1,0:T(8,128)(2,1)} custom-call(s32[64]{0:T(128)S(1)} %copy-done.4, s32[1,16]{1,0:T(1,128)S(1)} %get-tuple-element.29.top_rows, bf16[128,16,128]{2,1,0:T(8,128)(2,1)S(1)} %constant_dynamic-update-slice_fusion.tops, bf16[1,16,64,64]{3,2,1,0:T(8,128)(2,1)S(1)} %copy-done.2, f32[8,32,64]{2,1,0:T(8,128)S(1)} %couple_parents.1.parent_far, ...), custom_call_target="tpu_custom_call" | custom-call | flops 83886080 | bytes 6291456 | tf_op jit(solution)/shard_map/down/pallas_call | solution.py:320
  (37 shorter events, 0.6 us)
Async XLA Ops:
  3.1 8.7 %collective-permute-start.2 = (bf16[1,73,16,128]{3,2,1,0:T(8,128)(2,1)S(1)}, bf16[1,73,16,128]{3,2,1,0:T(8,128)(2,1)S(1)}, u32[]{:S(2)}, u32[]{:S(2)}) collective-permute-start(bf16[1,73,16,128]{3,2,1,0:T(8,128)(2,1)S(1)} %bitcast.7), channel_id=1, source_target_pairs={{0,8},{1,3},{2,10},{3,1},{4,12},{5,7},{6,14},{7,5},{8,0},{9,11},{1... | collective-permute-start | bytes 897032 | tf_op jit(solution)/shard_map/ppermute | solution.py:99
  5.6 9.2 %collective-permute-start.1 = (bf16[1,73,16,128]{3,2,1,0:T(8,128)(2,1)S(1)}, bf16[1,73,16,128]{3,2,1,0:T(8,128)(2,1)S(1)}, u32[]{:S(2)}, u32[]{:S(2)}) collective-permute-start(bf16[1,73,16,128]{3,2,1,0:T(8,128)(2,1)S(1)} %bitcast.8), channel_id=1, source_target_pairs={{0,24},{1,7},{2,26},{3,5},{4,28},{5,3},{6,30},{7,1},{8,16},{9,15},... | collective-permute-start | bytes 897032 | tf_op jit(solution)/shard_map/ppermute | solution.py:99
  7.9 8.7 %collective-permute-start = (bf16[1,73,16,128]{3,2,1,0:T(8,128)(2,1)S(1)}, bf16[1,73,16,128]{3,2,1,0:T(8,128)(2,1)S(1)}, u32[]{:S(2)}, u32[]{:S(2)}) collective-permute-start(bf16[1,73,16,128]{3,2,1,0:T(8,128)(2,1)S(1)} %bitcast.9), channel_id=1, source_target_pairs={{0,16},{1,5},{2,18},{3,7},{4,20},{5,1},{6,22},{7,3},{8,24},{9,13},... | collective-permute-start | bytes 897032 | tf_op jit(solution)/shard_map/ppermute | solution.py:99
  11.9 9.9 %collective-permute-start.14 = (bf16[2,73,16,128]{3,2,1,0:T(8,128)(2,1)S(1)}, bf16[2,73,16,128]{3,2,1,0:T(8,128)(2,1)S(1)}, u32[]{:S(2)}, u32[]{:S(2)}) collective-permute-start(bf16[2,73,16,128]{3,2,1,0:T(8,128)(2,1)S(1)} %pad_maximum_fusion.1.refs_0_), channel_id=1, source_target_pairs={{0,1},{1,0},{2,3},{3,2},{4,5},{5,4},{6,7},{7,6},{8,9},{9,8},{10,11... | collective-permute-start | bytes 1794056 | tf_op jit(solution)/shard_map/ppermute | solution.py:103
  12.2 11.3 %collective-permute-start.5 = (bf16[2,73,16,128]{3,2,1,0:T(8,128)(2,1)S(1)}, bf16[2,73,16,128]{3,2,1,0:T(8,128)(2,1)S(1)}, u32[]{:S(2)}, u32[]{:S(2)}) collective-permute-start(bf16[2,73,16,128]{3,2,1,0:T(8,128)(2,1)S(1)} %pad_maximum_fusion.1.refs_0_), channel_id=1, source_target_pairs={{0,6},{1,25},{2,4},{3,27},{4,2},{5,29},{6,0},{7,31},{8,14},{9,17},... | collective-permute-start | bytes 1794056 | tf_op jit(solution)/shard_map/ppermute | solution.py:99
  14.8 9.5 %collective-permute-start.3 = (bf16[2,73,16,128]{3,2,1,0:T(8,128)(2,1)S(1)}, bf16[2,73,16,128]{3,2,1,0:T(8,128)(2,1)S(1)}, u32[]{:S(2)}, u32[]{:S(2)}) collective-permute-start(bf16[2,73,16,128]{3,2,1,0:T(8,128)(2,1)S(1)} %pad_maximum_fusion.1.refs_0_), channel_id=1, source_target_pairs={{0,2},{1,9},{2,0},{3,11},{4,6},{5,13},{6,4},{7,15},{8,10},{9,1},{1... | collective-permute-start | bytes 1794056 | tf_op jit(solution)/shard_map/ppermute | solution.py:99
  16.6 13.2 %collective-permute-start.6 = (bf16[2,73,16,128]{3,2,1,0:T(8,128)(2,1)S(1)}, bf16[2,73,16,128]{3,2,1,0:T(8,128)(2,1)S(1)}, u32[]{:S(2)}, u32[]{:S(2)}) collective-permute-start(bf16[2,73,16,128]{3,2,1,0:T(8,128)(2,1)S(1)} %pad_maximum_fusion.refs_1_), channel_id=1, source_target_pairs={{0,6},{1,25},{2,4},{3,27},{4,2},{5,29},{6,0},{7,31},{8,14},{9,17},... | collective-permute-start | bytes 1794056 | tf_op jit(solution)/shard_map/ppermute | solution.py:99
  19.1 10.7 %collective-permute-start.15 = (bf16[2,73,16,128]{3,2,1,0:T(8,128)(2,1)S(1)}, bf16[2,73,16,128]{3,2,1,0:T(8,128)(2,1)S(1)}, u32[]{:S(2)}, u32[]{:S(2)}) collective-permute-start(bf16[2,73,16,128]{3,2,1,0:T(8,128)(2,1)S(1)} %pad_maximum_fusion.refs_1_), channel_id=1, source_target_pairs={{0,1},{1,0},{2,3},{3,2},{4,5},{5,4},{6,7},{7,6},{8,9},{9,8},{10,11... | collective-permute-start | bytes 1794056 | tf_op jit(solution)/shard_map/ppermute | solution.py:103
  21.8 9.1 %collective-permute-start.4 = (bf16[2,73,16,128]{3,2,1,0:T(8,128)(2,1)S(1)}, bf16[2,73,16,128]{3,2,1,0:T(8,128)(2,1)S(1)}, u32[]{:S(2)}, u32[]{:S(2)}) collective-permute-start(bf16[2,73,16,128]{3,2,1,0:T(8,128)(2,1)S(1)} %pad_maximum_fusion.refs_1_), channel_id=1, source_target_pairs={{0,2},{1,9},{2,0},{3,11},{4,6},{5,13},{6,4},{7,15},{8,10},{9,1},{1... | collective-permute-start | bytes 1794056 | tf_op jit(solution)/shard_map/ppermute | solution.py:99
  23.4 9.3 %collective-permute-start.18 = (bf16[2,73,16,128]{3,2,1,0:T(8,128)(2,1)S(1)}, bf16[2,73,16,128]{3,2,1,0:T(8,128)(2,1)S(1)}, u32[]{:S(2)}, u32[]{:S(2)}) collective-permute-start(bf16[2,73,16,128]{3,2,1,0:T(8,128)(2,1)S(1)} %collective-permute-done.5.refs_4_), channel_id=1, source_target_pairs={{0,1},{1,0},{2,3},{3,2},{4,5},{5,4},{6,7},{7,6},{8,9},{9,8},{10,11... | collective-permute-start | bytes 1794056 | tf_op jit(solution)/shard_map/ppermute | solution.py:103
  24.3 12.0 %collective-permute-start.7 = (bf16[2,73,16,128]{3,2,1,0:T(8,128)(2,1)S(1)}, bf16[2,73,16,128]{3,2,1,0:T(8,128)(2,1)S(1)}, u32[]{:S(2)}, u32[]{:S(2)}) collective-permute-start(bf16[2,73,16,128]{3,2,1,0:T(8,128)(2,1)S(1)} %collective-permute-done.3.refs_2_), channel_id=1, source_target_pairs={{0,6},{1,25},{2,4},{3,27},{4,2},{5,29},{6,0},{7,31},{8,14},{9,17},... | collective-permute-start | bytes 1794056 | tf_op jit(solution)/shard_map/ppermute | solution.py:99
  29.8 9.1 %collective-permute-start.8 = (bf16[2,73,16,128]{3,2,1,0:T(8,128)(2,1)S(1)}, bf16[2,73,16,128]{3,2,1,0:T(8,128)(2,1)S(1)}, u32[]{:S(2)}, u32[]{:S(2)}) collective-permute-start(bf16[2,73,16,128]{3,2,1,0:T(8,128)(2,1)S(1)} %collective-permute-done.6.refs_5_), channel_id=1, source_target_pairs={{0,2},{1,9},{2,0},{3,11},{4,6},{5,13},{6,4},{7,15},{8,10},{9,1},{1... | collective-permute-start | bytes 1794056 | tf_op jit(solution)/shard_map/ppermute | solution.py:99
  29.8 11.0 %collective-permute-start.16 = (bf16[2,73,16,128]{3,2,1,0:T(8,128)(2,1)S(1)}, bf16[2,73,16,128]{3,2,1,0:T(8,128)(2,1)S(1)}, u32[]{:S(2)}, u32[]{:S(2)}) collective-permute-start(bf16[2,73,16,128]{3,2,1,0:T(8,128)(2,1)S(1)} %collective-permute-done.3.refs_2_), channel_id=1, source_target_pairs={{0,1},{1,0},{2,3},{3,2},{4,5},{5,4},{6,7},{7,6},{8,9},{9,8},{10,11... | collective-permute-start | bytes 1794056 | tf_op jit(solution)/shard_map/ppermute | solution.py:103
  30.9 12.6 %collective-permute-start.19 = (bf16[2,73,16,128]{3,2,1,0:T(8,128)(2,1)S(1)}, bf16[2,73,16,128]{3,2,1,0:T(8,128)(2,1)S(1)}, u32[]{:S(2)}, u32[]{:S(2)}) collective-permute-start(bf16[2,73,16,128]{3,2,1,0:T(8,128)(2,1)S(1)} %collective-permute-done.6.refs_5_), channel_id=1, source_target_pairs={{0,1},{1,0},{2,3},{3,2},{4,5},{5,4},{6,7},{7,6},{8,9},{9,8},{10,11... | collective-permute-start | bytes 1794056 | tf_op jit(solution)/shard_map/ppermute | solution.py:103
  32.7 11.3 %collective-permute-start.17 = (bf16[2,73,16,128]{3,2,1,0:T(8,128)(2,1)S(1)}, bf16[2,73,16,128]{3,2,1,0:T(8,128)(2,1)S(1)}, u32[]{:S(2)}, u32[]{:S(2)}) collective-permute-start(bf16[2,73,16,128]{3,2,1,0:T(8,128)(2,1)S(1)} %collective-permute-done.4.refs_3_), channel_id=1, source_target_pairs={{0,1},{1,0},{2,3},{3,2},{4,5},{5,4},{6,7},{7,6},{8,9},{9,8},{10,11... | collective-permute-start | bytes 1794056 | tf_op jit(solution)/shard_map/ppermute | solution.py:103
  36.2 8.5 %collective-permute-start.12 = (bf16[2,73,16,128]{3,2,1,0:T(8,128)(2,1)S(1)}, bf16[2,73,16,128]{3,2,1,0:T(8,128)(2,1)S(1)}, u32[]{:S(2)}, u32[]{:S(2)}) collective-permute-start(bf16[2,73,16,128]{3,2,1,0:T(8,128)(2,1)S(1)} %collective-permute-done.7.refs_6_.refs_0_), channel_id=1, source_target_pairs={{0,1},{1,0},{2,3},{3,2},{4,5},{5,4},{6,7},{7,6},{8,9},{9,8},{10,11... | collective-permute-start | bytes 1794056 | tf_op jit(solution)/shard_map/ppermute | solution.py:103
  38.9 5.8 %collective-permute-start.13 = (bf16[2,73,16,128]{3,2,1,0:T(8,128)(2,1)S(1)}, bf16[2,73,16,128]{3,2,1,0:T(8,128)(2,1)S(1)}, u32[]{:S(2)}, u32[]{:S(2)}) collective-permute-start(bf16[2,73,16,128]{3,2,1,0:T(8,128)(2,1)S(1)} %collective-permute-done.8.refs_7_.refs_1_), channel_id=1, source_target_pairs={{0,1},{1,0},{2,3},{3,2},{4,5},{5,4},{6,7},{7,6},{8,9},{9,8},{10,11... | collective-permute-start | bytes 1794056 | tf_op jit(solution)/shard_map/ppermute | solution.py:103
  40.9 9.3 %collective-permute-start.11 = (bf16[16,16,128]{2,1,0:T(8,128)(2,1)S(1)}, bf16[16,16,128]{2,1,0:T(8,128)(2,1)S(1)}, u32[]{:S(2)}, u32[]{:S(2)}) collective-permute-start(bf16[16,16,128]{2,1,0:T(8,128)(2,1)S(1)} %tops.1), channel_id=1, source_target_pairs={{0,96},{32,64},{64,32},{96,0},{1,97},{33,65},{65,33},{97,1},{2,98}... | collective-permute-start | bytes 196616 | tf_op jit(solution)/shard_map/ppermute | solution.py:363
  43.4 6.8 %collective-permute-start.10 = (bf16[16,16,128]{2,1,0:T(8,128)(2,1)S(1)}, bf16[16,16,128]{2,1,0:T(8,128)(2,1)S(1)}, u32[]{:S(2)}, u32[]{:S(2)}) collective-permute-start(bf16[16,16,128]{2,1,0:T(8,128)(2,1)S(1)} %tops.1), channel_id=1, source_target_pairs={{0,64},{32,96},{64,0},{96,32},{1,65},{33,97},{65,1},{97,33},{2,66}... | collective-permute-start | bytes 196616 | tf_op jit(solution)/shard_map/ppermute | solution.py:363
  44.0 6.3 %collective-permute-start.9 = (bf16[16,16,128]{2,1,0:T(8,128)(2,1)S(1)}, bf16[16,16,128]{2,1,0:T(8,128)(2,1)S(1)}, u32[]{:S(2)}, u32[]{:S(2)}) collective-permute-start(bf16[16,16,128]{2,1,0:T(8,128)(2,1)S(1)} %tops.1), channel_id=1, source_target_pairs={{0,32},{32,0},{64,96},{96,64},{1,33},{33,1},{65,97},{97,65},{2,34}... | collective-permute-start | bytes 196616 | tf_op jit(solution)/shard_map/ppermute | solution.py:363
  50.3 2.2 %collective-permute-start.20 = (bf16[64,16,128]{2,1,0:T(8,128)(2,1)S(1)}, bf16[64,16,128]{2,1,0:T(8,128)(2,1)S(1)}, u32[]{:S(2)}, u32[]{:S(2)}) collective-permute-start(bf16[64,16,128]{2,1,0:T(8,128)(2,1)S(1)} %pad_maximum_fusion.2), channel_id=1, source_target_pairs={{0,1},{1,0},{2,3},{3,2},{4,5},{5,4},{6,7},{7,6},{8,9},{9,8},{10,11... | collective-permute-start | bytes 786440 | tf_op jit(solution)/shard_map/ppermute | solution.py:103
  51.3 1.6 %copy-start = (bf16[64,64,256]{2,1,0:T(8,128)(2,1)S(1)}, bf16[64,64,256]{2,1,0:T(8,128)(2,1)}, u32[]{:S(2)}) copy-start(bf16[64,64,256]{2,1,0:T(8,128)(2,1)} %out_basis.1) | copy-start | bytes 6291460
  51.3 1.8 %copy-start.1 = (bf16[64,64,64]{2,1,0:T(8,128)(2,1)S(1)}, bf16[64,64,64]{2,1,0:T(8,128)(2,1)}, u32[]{:S(2)}) copy-start(bf16[64,64,64]{2,1,0:T(8,128)(2,1)} %leaf_descend.1) | copy-start | bytes 1572868
  51.3 1.9 %copy-start.2 = (bf16[1,16,64,64]{3,2,1,0:T(8,128)(2,1)S(1)}, bf16[1,16,64,64]{3,2,1,0:T(8,128)(2,1)}, u32[]{:S(2)}) copy-start(bf16[1,16,64,64]{3,2,1,0:T(8,128)(2,1)} %top_coupling.1) | copy-start | bytes 393220
  51.3 1.9 %copy-start.3 = (bf16[8,64,64]{2,1,0:T(8,128)(2,1)S(1)}, bf16[8,64,64]{2,1,0:T(8,128)(2,1)}, u32[]{:S(2)}) copy-start(bf16[8,64,64]{2,1,0:T(8,128)(2,1)} %parent_descend.1) | copy-start | bytes 196612
  51.3 1.9 %copy-start.4 = (s32[64]{0:T(128)S(1)}, s32[64]{0:T(128)}, u32[]{:S(2)}) copy-start(s32[64]{0:T(128)} %counts.3) | copy-start | bytes 772

commit v5 on v4

--- a/solution.py
+++ b/solution.py
@@ -12,6 +12,7 @@
 F32 = jnp.float32
 LEAF, PARENT = 64, 8
 ROWS = LEAF + PARENT + 1
+MORE = 16
 NT = (((1,), (1,)), ((), ()))
 MIB = 1 << 20
 
@@ -103,16 +104,17 @@
     return lax.ppermute(x, "c", [(0, 1), (1, 0)])
 
 
-def gather(s, staged):
+def gather(s, staged, more):
     s = s[None]
     a, o, b = (send(s, False, m) for m in (1, 2, 3))
     near, far = jnp.concatenate([s, a]), jnp.concatenate([o, b])
     far, staged = lax.optimization_barrier((far, staged))
     near_a, near_b = send(near, True, 1), send(near, True, 3)
     far_a, far_b = send(far, True, 1), send(far, True, 3)
+    near_b, more = lax.optimization_barrier((near_b, more))
     near_o, far_o = send(near_a, True, 3), send(far_b, True, 1)
     early = [(near, 0), (far, 2), (near_a, 4), (far_a, 6), (near_b, 12), (far_b, 14)]
-    return early, [(near_o, 8), (far_o, 10)], staged
+    return early, [(near_o, 8), (far_o, 10)], staged, more
 
 
 def place_kernel(firsts, *refs):
@@ -224,12 +226,37 @@
     )(place, *map(hbm, names), hbm(coupling))
 
 
+def stage_more_kernel(coupling, out, sem):
+    parts = 4
+    size = out.shape[0] // parts
+    copies = []
+    for k in range(parts):
+        source = coupling.at[pl.ds(STAGED + k * size, size)]
+        copies.append(pltpu.make_async_copy(source, out.at[pl.ds(k * size, size)], sem.at[k]))
+        copies[k].start()
+    for copy in copies:
+        copy.wait()
+
+
+def stage_more(coupling):
+    return pl.pallas_call(
+        stage_more_kernel,
+        in_specs=[pl.BlockSpec(memory_space=pltpu.HBM)],
+        out_specs=pl.BlockSpec(memory_space=pltpu.VMEM),
+        out_shape=jax.ShapeDtypeStruct((MORE,) + coupling.shape[1:], BF16),
+        scratch_shapes=[pltpu.SemaphoreType.DMA((4,))],
+        compiler_params=pltpu.CompilerParams(vmem_limit_bytes=2 * MIB),
+        cost_estimate=pl.CostEstimate(flops=0, bytes_accessed=4096, transcendentals=0),
+        name="stage_more",
+    )(pltpu.with_memory_space_constraint(coupling, pltpu.HBM))
+
+
 def couple_kernel(
-    leaf_rows, gathered, head, coupling, parent_coupling, leaf_far, parent_staged, staged, leaf_named, chunk_sem, row_sem
+    leaf_rows, gathered, head, more, coupling, parent_coupling, leaf_far, parent_staged, staged, leaf_named, chunk_sem, row_sem
 ):
     chunks = []
-    for k in range((LEAF - STAGED) // CHUNK):
-        source = coupling.at[pl.ds(STAGED + k * CHUNK, CHUNK)]
+    for k in range((LEAF - STAGED - MORE) // CHUNK):
+        source = coupling.at[pl.ds(STAGED + MORE + k * CHUNK, CHUNK)]
         chunks.append(pltpu.make_async_copy(source, staged.at[pl.ds(k * CHUNK, CHUNK)], chunk_sem.at[k]))
     chunks.append(pltpu.make_async_copy(parent_coupling, parent_staged, chunk_sem.at[len(chunks)]))
     named = pltpu.make_async_copy(leaf_rows, leaf_named, row_sem)
@@ -239,11 +266,14 @@
     for b in range(STAGED):
         block = picked(lambda j: gathered[leaf_named[j, b]], 16)
         leaf_far[b] = dot(block, head[b].reshape(1024, 64))
-    for k in range((LEAF - STAGED) // CHUNK):
+    for i in range(MORE):
+        block = picked(lambda j: gathered[leaf_named[j, STAGED + i]], 16)
+        leaf_far[STAGED + i] = dot(block, more[i].reshape(1024, 64))
+    for k in range((LEAF - STAGED - MORE) // CHUNK):
         chunks[k].wait()
         for i in range(k * CHUNK, (k + 1) * CHUNK):
-            block = picked(lambda j: gathered[leaf_named[j, STAGED + i]], 16)
-            leaf_far[STAGED + i] = dot(block, staged[i].reshape(1024, 64))
+            block = picked(lambda j: gathered[leaf_named[j, STAGED + MORE + i]], 16)
+            leaf_far[STAGED + MORE + i] = dot(block, staged[i].reshape(1024, 64))
     chunks[-1].wait()
 
 
@@ -270,17 +300,17 @@
     )(parent_rows, gathered, coupling)
 
 
-def couple(leaf_rows, gathered, head, coupling, parent_coupling):
+def couple(leaf_rows, gathered, head, more, coupling, parent_coupling):
     vmem = pl.BlockSpec(memory_space=pltpu.VMEM)
     return pl.pallas_call(
         couple_kernel,
-        in_specs=[vmem] * 3 + [pl.BlockSpec(memory_space=pltpu.HBM)] * 2,
+        in_specs=[vmem] * 4 + [pl.BlockSpec(memory_space=pltpu.HBM)] * 2,
         out_specs=[vmem, vmem],
         out_shape=[jax.ShapeDtypeStruct((LEAF, 32, 64), F32), jax.ShapeDtypeStruct(parent_coupling.shape, BF16)],
         scratch_shapes=[
-            pltpu.VMEM((LEAF - STAGED,) + coupling.shape[1:], BF16),
+            pltpu.VMEM((LEAF - STAGED - MORE,) + coupling.shape[1:], BF16),
             pltpu.SMEM(leaf_rows.shape, jnp.int32),
-            pltpu.SemaphoreType.DMA(((LEAF - STAGED) // CHUNK + 1,)),
+            pltpu.SemaphoreType.DMA(((LEAF - STAGED - MORE) // CHUNK + 1,)),
             pltpu.SemaphoreType.DMA,
         ],
         compiler_params=pltpu.CompilerParams(vmem_limit_bytes=18 * MIB),
@@ -290,6 +320,7 @@
         leaf_rows,
         gathered,
         head,
+        more,
         pltpu.with_memory_space_constraint(coupling, pltpu.HBM),
         pltpu.with_memory_space_constraint(parent_coupling, pltpu.HBM),
     )
@@ -354,7 +385,7 @@
     hbm = lambda a: pltpu.with_memory_space_constraint(a, pltpu.HBM)
     coeffs = up(*map(hbm, (counts, charges, leaf_basis, leaf_transfer, parent_transfer)))
     names = (far_owner.T, far_local.T, parent_owner, parent_index, top_source)
-    early, late, prepared = gather(coeffs, stage(place, *names, leaf_coupling, STAGED))
+    early, late, prepared, more = gather(coeffs, stage(place, *names, leaf_coupling, STAGED), stage_more(leaf_coupling))
     head, leaf_rows, parent_rows, top_rows = prepared
     swap = lambda pieces: [(other_core(piece), 16 + first) for piece, first in pieces]
     gathered = assemble(early + swap(early))
@@ -362,7 +393,7 @@
     tops = column_tops(early + late)
     planes = [tops] + [lax.ppermute(tops, "x", [(i, i ^ m) for i in range(4)]) for m in (1, 2, 3)]
 
-    leaf_far, parent_staged = couple(leaf_rows, gathered, head, leaf_coupling, parent_coupling)
+    leaf_far, parent_staged = couple(leaf_rows, gathered, head, more, leaf_coupling, parent_coupling)
     planes, leaf_far = lax.optimization_barrier((planes, leaf_far))
     tops = jnp.concatenate(planes)
     tops = jnp.concatenate([tops, other_core(tops)])

time: 55.8 us -> 54.8 us (0.982)
  waiting for transfers between devices: 12 us -> 9.76 us
  Pallas kernels: 15.6 us -> 16.9 us
    ppermute x9, waiting for transfers between devices: 11.9 us -> 9.73 us  [send(): return lax.ppermute(x, ('y', 'z', 'c'), pairs(second, mask))]
    pallas_call x1 -> x2, Pallas kernels: 5.33 us -> 6.6 us  [the longest x1 4.39 us: couple(): pl.pallas_call(couple_kernel, in_specs=[vmem] * 4 + [pl.BlockSpec(memory_...]
  transfers between devices with their start and end apart: 21 -> 21, of which waited for: 6 -> 5; matrix products, arithmetic and copies ran while one was open for 0% -> 0% of each run, Pallas kernels for 18% -> 21%
where the time goes in v5:
time: 54.8 us; the launch traced here: 54.7 us
  starting transfers between devices  26.8 us (49%)
  Pallas kernels  16.9 us (31%)
  waiting for transfers between devices  9.76 us (18%)
  local copies, waits for them, and re-layouts  0.74 us (1%)
    ppermute x9, starting transfers between devices, send(): return lax.ppermute(x, ('y', 'z', 'c'), pairs(second, mask))  13.3 us
    ppermute x9, starting transfers between devices, other_core(): return lax.ppermute(x, 'c', [(0, 1), (1, 0)])  10.2 us
    ppermute x9, waiting for transfers between devices, send(): return lax.ppermute(x, ('y', 'z', 'c'), pairs(second, mask))  9.73 us
    pallas_call x1, Pallas kernels, couple(): pl.pallas_call(couple_kernel, in_specs=[vmem] * 4 + [pl.BlockSpec(memory_...  4.39 us
    ppermute x3, starting transfers between devices, body(): lax.ppermute(tops, 'x', [(i, i ^ m) for i in range(4)])  3.33 us
    pallas_call x1, Pallas kernels, up(): pl.pallas_call(up_kernel, in_specs=[hbm] * 5, out_specs=pl.BlockSpec(memo...  2.98 us
    pallas_call x1, Pallas kernels, stage(): pl.pallas_call(stage_kernel, in_specs=[smem] + [pl.BlockSpec(memory_space...  2.87 us
    pallas_call x1, Pallas kernels, down(): pl.pallas_call(down_kernel, in_specs=[smem] * 2 + [vmem] * len(operands),...  2.43 us
  transfers between devices with their start and end apart: 21, of which 5 were waited for; matrix products, arithmetic and copies ran while one was open for 0% of the time, Pallas kernels for 21%

profile of v5, /device:TPU:1, one launch (start us, length us, event | category | flops | bytes accessed | tf_op | source)
XLA Modules:
  0.0 54.7 jit_solution(15546160524862450689)
XLA Ops:
  0.1 3.0 %up.1 = bf16[73,16,128]{2,1,0:T(8,128)(2,1)S(1)} custom-call(s32[64]{0:T(128)} %counts.3, bf16[64,32,256]{2,1,0:T(8,128)(2,1)} %charges, bf16[64,64,256]{2,1,0:T(8,128)(2,1)} %basis.1, bf16[64,64,64]{2,1,0:T(8,128)(2,1)} %transfer.1, bf16[8,64,64]{2,1,0:T(8,128)(2,1)} %parent_transfer.1), custom_call_target="tpu_custom_call" | custom-call | flops 83886080 | bytes 5242880 | tf_op jit(solution)/shard_map/up/pallas_call | solution.py:74
  3.1 2.5 %collective-permute-start.2 = (bf16[1,73,16,128]{3,2,1,0:T(8,128)(2,1)S(1)}, bf16[1,73,16,128]{3,2,1,0:T(8,128)(2,1)S(1)}, u32[]{:S(2)}, u32[]{:S(2)}) collective-permute-start(bf16[1,73,16,128]{3,2,1,0:T(8,128)(2,1)S(1)} %bitcast.7), channel_id=1, source_target_pairs={{0,8},{1,3},{2,10},{3,1},{4,12},{5,7},{6,14},{7,5},{8,0},{9,11},{1... | collective-permute-start | bytes 897032 | tf_op jit(solution)/shard_map/ppermute | solution.py:100
  5.6 2.2 %collective-permute-start.1 = (bf16[1,73,16,128]{3,2,1,0:T(8,128)(2,1)S(1)}, bf16[1,73,16,128]{3,2,1,0:T(8,128)(2,1)S(1)}, u32[]{:S(2)}, u32[]{:S(2)}) collective-permute-start(bf16[1,73,16,128]{3,2,1,0:T(8,128)(2,1)S(1)} %bitcast.8), channel_id=1, source_target_pairs={{0,24},{1,7},{2,26},{3,5},{4,28},{5,3},{6,30},{7,1},{8,16},{9,15},... | collective-permute-start | bytes 897032 | tf_op jit(solution)/shard_map/ppermute | solution.py:100
  7.9 1.1 %collective-permute-start = (bf16[1,73,16,128]{3,2,1,0:T(8,128)(2,1)S(1)}, bf16[1,73,16,128]{3,2,1,0:T(8,128)(2,1)S(1)}, u32[]{:S(2)}, u32[]{:S(2)}) collective-permute-start(bf16[1,73,16,128]{3,2,1,0:T(8,128)(2,1)S(1)} %bitcast.9), channel_id=1, source_target_pairs={{0,16},{1,5},{2,18},{3,7},{4,20},{5,1},{6,22},{7,3},{8,24},{9,13},... | collective-permute-start | bytes 897032 | tf_op jit(solution)/shard_map/ppermute | solution.py:100
  8.9 2.9 %stage.1 = (bf16[16,16,64,64]{3,2,1,0:T(8,128)(2,1)S(1)}, s32[16,64]{1,0:T(8,128)S(1)}, s32[8,16]{1,0:T(8,128)S(1)}, s32[1,16]{1,0:T(1,128)S(1)}) custom-call(s32[4]{0:T(128)S(1)} %pad_add_fusion.place, s32[16,64]{1,0:T(8,128)} %bitcast.11, s32[16,64]{1,0:T(8,128)} %bitcast.12, s32[8,16]{1,0:T(8,128)} %refs_2_.1, s32[8,16]{1,0:T(8,128)} %refs_3_.1, ...), custom_call_target="tpu_custom_call" | custom-call | bytes 4096 | tf_op jit(solution)/shard_map/stage/pallas_call | solution.py:216
  11.9 0.3 collective-permute-start.14
  12.2 2.6 %collective-permute-start.5 = (bf16[2,73,16,128]{3,2,1,0:T(8,128)(2,1)S(1)}, bf16[2,73,16,128]{3,2,1,0:T(8,128)(2,1)S(1)}, u32[]{:S(2)}, u32[]{:S(2)}) collective-permute-start(bf16[2,73,16,128]{3,2,1,0:T(8,128)(2,1)S(1)} %pad_maximum_fusion.1.refs_0_), channel_id=1, source_target_pairs={{0,6},{1,25},{2,4},{3,27},{4,2},{5,29},{6,0},{7,31},{8,14},{9,17},... | collective-permute-start | bytes 1794056 | tf_op jit(solution)/shard_map/ppermute | solution.py:100
  14.8 1.8 %collective-permute-done = bf16[1,73,16,128]{3,2,1,0:T(8,128)(2,1)S(1)} collective-permute-done((bf16[1,73,16,128]{3,2,1,0:T(8,128)(2,1)S(1)}, bf16[1,73,16,128]{3,2,1,0:T(8,128)(2,1)S(1)}, u32[]{:S(2)}, u32[]{:S(2)}) %collective-permute-start) | collective-permute-done | bytes 299040 | tf_op jit(solution)/shard_map/ppermute | solution.py:100
  16.6 2.5 %collective-permute-start.6 = (bf16[2,73,16,128]{3,2,1,0:T(8,128)(2,1)S(1)}, bf16[2,73,16,128]{3,2,1,0:T(8,128)(2,1)S(1)}, u32[]{:S(2)}, u32[]{:S(2)}) collective-permute-start(bf16[2,73,16,128]{3,2,1,0:T(8,128)(2,1)S(1)} %pad_maximum_fusion.refs_1_), channel_id=1, source_target_pairs={{0,6},{1,25},{2,4},{3,27},{4,2},{5,29},{6,0},{7,31},{8,14},{9,17},... | collective-permute-start | bytes 1794056 | tf_op jit(solution)/shard_map/ppermute | solution.py:100
  19.1 2.6 %collective-permute-start.15 = (bf16[2,73,16,128]{3,2,1,0:T(8,128)(2,1)S(1)}, bf16[2,73,16,128]{3,2,1,0:T(8,128)(2,1)S(1)}, u32[]{:S(2)}, u32[]{:S(2)}) collective-permute-start(bf16[2,73,16,128]{3,2,1,0:T(8,128)(2,1)S(1)} %pad_maximum_fusion.refs_1_), channel_id=1, source_target_pairs={{0,1},{1,0},{2,3},{3,2},{4,5},{5,4},{6,7},{7,6},{8,9},{9,8},{10,11... | collective-permute-start | bytes 1794056 | tf_op jit(solution)/shard_map/ppermute | solution.py:104
  21.8 2.1 %collective-permute-done.3.refs_2_ = bf16[2,73,16,128]{3,2,1,0:T(8,128)(2,1)S(1)} collective-permute-done((bf16[2,73,16,128]{3,2,1,0:T(8,128)(2,1)S(1)}, bf16[2,73,16,128]{3,2,1,0:T(8,128)(2,1)S(1)}, u32[]{:S(2)}, u32[]{:S(2)}) %collective-permute-start.3) | collective-permute-done | bytes 598048 | tf_op jit(solution)/shard_map/ppermute | solution.py:100
  23.9 2.4 %collective-permute-start.16 = (bf16[2,73,16,128]{3,2,1,0:T(8,128)(2,1)S(1)}, bf16[2,73,16,128]{3,2,1,0:T(8,128)(2,1)S(1)}, u32[]{:S(2)}, u32[]{:S(2)}) collective-permute-start(bf16[2,73,16,128]{3,2,1,0:T(8,128)(2,1)S(1)} %collective-permute-done.3.refs_2_), channel_id=1, source_target_pairs={{0,1},{1,0},{2,3},{3,2},{4,5},{5,4},{6,7},{7,6},{8,9},{9,8},{10,11... | collective-permute-start | bytes 1794056 | tf_op jit(solution)/shard_map/ppermute | solution.py:104
  26.3 2.3 %collective-permute-start.7 = (bf16[2,73,16,128]{3,2,1,0:T(8,128)(2,1)S(1)}, bf16[2,73,16,128]{3,2,1,0:T(8,128)(2,1)S(1)}, u32[]{:S(2)}, u32[]{:S(2)}) collective-permute-start(bf16[2,73,16,128]{3,2,1,0:T(8,128)(2,1)S(1)} %collective-permute-done.3.refs_2_), channel_id=1, source_target_pairs={{0,6},{1,25},{2,4},{3,27},{4,2},{5,29},{6,0},{7,31},{8,14},{9,17},... | collective-permute-start | bytes 1794056 | tf_op jit(solution)/shard_map/ppermute | solution.py:100
  28.6 1.2 %collective-permute-done.6.refs_5_ = bf16[2,73,16,128]{3,2,1,0:T(8,128)(2,1)S(1)} collective-permute-done((bf16[2,73,16,128]{3,2,1,0:T(8,128)(2,1)S(1)}, bf16[2,73,16,128]{3,2,1,0:T(8,128)(2,1)S(1)}, u32[]{:S(2)}, u32[]{:S(2)}) %collective-permute-start.6) | collective-permute-done | bytes 598048 | tf_op jit(solution)/shard_map/ppermute | solution.py:100
  29.8 2.2 %stage_more.1.more = bf16[16,16,64,64]{3,2,1,0:T(8,128)(2,1)S(1)} custom-call(bf16[64,16,64,64]{3,2,1,0:T(8,128)(2,1)} %coupling.3), custom_call_target="tpu_custom_call" | custom-call | bytes 4096 | tf_op jit(solution)/shard_map/stage_more/pallas_call | solution.py:242
  32.1 0.9 %collective-permute-start.18 = (bf16[2,73,16,128]{3,2,1,0:T(8,128)(2,1)S(1)}, bf16[2,73,16,128]{3,2,1,0:T(8,128)(2,1)S(1)}, u32[]{:S(2)}, u32[]{:S(2)}) collective-permute-start(bf16[2,73,16,128]{3,2,1,0:T(8,128)(2,1)S(1)} %collective-permute-done.5.refs_4_), channel_id=1, source_target_pairs={{0,1},{1,0},{2,3},{3,2},{4,5},{5,4},{6,7},{7,6},{8,9},{9,8},{10,11... | collective-permute-start | bytes 1794056 | tf_op jit(solution)/shard_map/ppermute | solution.py:104
  33.1 0.4 collective-permute-start.17
  33.5 3.1 %collective-permute-done.7.refs_6_.refs_0_ = bf16[2,73,16,128]{3,2,1,0:T(8,128)(2,1)S(1)} collective-permute-done((bf16[2,73,16,128]{3,2,1,0:T(8,128)(2,1)S(1)}, bf16[2,73,16,128]{3,2,1,0:T(8,128)(2,1)S(1)}, u32[]{:S(2)}, u32[]{:S(2)}) %collective-permute-start.7) | collective-permute-done | bytes 598048 | tf_op jit(solution)/shard_map/ppermute | solution.py:100
  36.6 0.9 %collective-permute-start.12 = (bf16[2,73,16,128]{3,2,1,0:T(8,128)(2,1)S(1)}, bf16[2,73,16,128]{3,2,1,0:T(8,128)(2,1)S(1)}, u32[]{:S(2)}, u32[]{:S(2)}) collective-permute-start(bf16[2,73,16,128]{3,2,1,0:T(8,128)(2,1)S(1)} %collective-permute-done.7.refs_6_.refs_0_), channel_id=1, source_target_pairs={{0,1},{1,0},{2,3},{3,2},{4,5},{5,4},{6,7},{7,6},{8,9},{9,8},{10,11... | collective-permute-start | bytes 1794056 | tf_op jit(solution)/shard_map/ppermute | solution.py:104
  37.5 1.5 %collective-permute-done.8.refs_7_.refs_1_ = bf16[2,73,16,128]{3,2,1,0:T(8,128)(2,1)S(1)} collective-permute-done((bf16[2,73,16,128]{3,2,1,0:T(8,128)(2,1)S(1)}, bf16[2,73,16,128]{3,2,1,0:T(8,128)(2,1)S(1)}, u32[]{:S(2)}, u32[]{:S(2)}) %collective-permute-start.8) | collective-permute-done | bytes 598048 | tf_op jit(solution)/shard_map/ppermute | solution.py:100
  38.9 1.7 %collective-permute-start.13 = (bf16[2,73,16,128]{3,2,1,0:T(8,128)(2,1)S(1)}, bf16[2,73,16,128]{3,2,1,0:T(8,128)(2,1)S(1)}, u32[]{:S(2)}, u32[]{:S(2)}) collective-permute-start(bf16[2,73,16,128]{3,2,1,0:T(8,128)(2,1)S(1)} %collective-permute-done.8.refs_7_.refs_1_), channel_id=1, source_target_pairs={{0,1},{1,0},{2,3},{3,2},{4,5},{5,4},{6,7},{7,6},{8,9},{9,8},{10,11... | collective-permute-start | bytes 1794056 | tf_op jit(solution)/shard_map/ppermute | solution.py:104
  40.6 0.2 tops.1
  40.9 2.6 %collective-permute-start.11 = (bf16[16,16,128]{2,1,0:T(8,128)(2,1)S(1)}, bf16[16,16,128]{2,1,0:T(8,128)(2,1)S(1)}, u32[]{:S(2)}, u32[]{:S(2)}) collective-permute-start(bf16[16,16,128]{2,1,0:T(8,128)(2,1)S(1)} %tops.1), channel_id=1, source_target_pairs={{0,96},{32,64},{64,32},{96,0},{1,97},{33,65},{65,33},{97,1},{2,98}... | collective-permute-start | bytes 196616 | tf_op jit(solution)/shard_map/ppermute | solution.py:394
  43.4 0.5 collective-permute-start.10
  44.0 0.3 collective-permute-start.9
  44.2 0.5 assemble.2.refs_4_
  44.9 4.4 %couple.1 = (f32[64,32,64]{2,1,0:T(8,128)S(1)}, bf16[8,16,64,64]{3,2,1,0:T(8,128)(2,1)S(1)}) custom-call(s32[16,64]{1,0:T(8,128)S(1)} %get-tuple-element.34.leaf_rows, bf16[2336,16,128]{2,1,0:T(8,128)(2,1)S(1)} %assemble.3.gathered, bf16[16,16,64,64]{3,2,1,0:T(8,128)(2,1)S(1)} %get-tuple-element.35.head, bf16[16,16,64,64]{3,2,1,0:T(8,128)(2,1)S(1)} %stage_more.1.more, ...), custom_call_target="tpu_custom_call" | custom-call | flops 301989888 | bytes 29360128 | tf_op jit(solution)/shard_map/couple/pallas_call | solution.py:305
  49.4 0.9 %collective-permute-start.20 = (bf16[64,16,128]{2,1,0:T(8,128)(2,1)S(1)}, bf16[64,16,128]{2,1,0:T(8,128)(2,1)S(1)}, u32[]{:S(2)}, u32[]{:S(2)}) collective-permute-start(bf16[64,16,128]{2,1,0:T(8,128)(2,1)S(1)} %pad_maximum_fusion.2), channel_id=1, source_target_pairs={{0,1},{1,0},{2,3},{3,2},{4,5},{5,4},{6,7},{7,6},{8,9},{9,8},{10,11... | collective-permute-start | bytes 786440 | tf_op jit(solution)/shard_map/ppermute | solution.py:104
  50.4 1.1 %couple_parents.1.parent_far = f32[8,32,64]{2,1,0:T(8,128)S(1)} custom-call(s32[8,16]{1,0:T(8,128)S(1)} %get-tuple-element.42.parent_rows, bf16[2336,16,128]{2,1,0:T(8,128)(2,1)S(1)} %assemble.3.gathered, bf16[8,16,64,64]{3,2,1,0:T(8,128)(2,1)S(1)} %get-tuple-element.43.coupling), custom_call_target="tpu_custom_call" | custom-call | flops 33554432 | bytes 3145728 | tf_op jit(solution)/shard_map/couple_parents/pallas_call | solution.py:291
  51.6 0.3 copy-done
  51.9 0.3 copy-done.1
  52.2 2.4 %down.1 = bf16[64,32,256]{2,1,0:T(8,128)(2,1)} custom-call(s32[64]{0:T(128)S(1)} %copy-done.4, s32[1,16]{1,0:T(1,128)S(1)} %get-tuple-element.31.top_rows, bf16[128,16,128]{2,1,0:T(8,128)(2,1)S(1)} %constant_dynamic-update-slice_fusion.tops, bf16[1,16,64,64]{3,2,1,0:T(8,128)(2,1)S(1)} %copy-done.2, f32[8,32,64]{2,1,0:T(8,128)S(1)} %couple_parents.1.parent_far, ...), custom_call_target="tpu_custom_call" | custom-call | flops 83886080 | bytes 6291456 | tf_op jit(solution)/shard_map/down/pallas_call | solution.py:351
  (38 shorter events, 0.7 us)
Async XLA Ops:
  3.1 8.7 %collective-permute-start.2 = (bf16[1,73,16,128]{3,2,1,0:T(8,128)(2,1)S(1)}, bf16[1,73,16,128]{3,2,1,0:T(8,128)(2,1)S(1)}, u32[]{:S(2)}, u32[]{:S(2)}) collective-permute-start(bf16[1,73,16,128]{3,2,1,0:T(8,128)(2,1)S(1)} %bitcast.7), channel_id=1, source_target_pairs={{0,8},{1,3},{2,10},{3,1},{4,12},{5,7},{6,14},{7,5},{8,0},{9,11},{1... | collective-permute-start | bytes 897032 | tf_op jit(solution)/shard_map/ppermute | solution.py:100
  5.6 9.2 %collective-permute-start.1 = (bf16[1,73,16,128]{3,2,1,0:T(8,128)(2,1)S(1)}, bf16[1,73,16,128]{3,2,1,0:T(8,128)(2,1)S(1)}, u32[]{:S(2)}, u32[]{:S(2)}) collective-permute-start(bf16[1,73,16,128]{3,2,1,0:T(8,128)(2,1)S(1)} %bitcast.8), channel_id=1, source_target_pairs={{0,24},{1,7},{2,26},{3,5},{4,28},{5,3},{6,30},{7,1},{8,16},{9,15},... | collective-permute-start | bytes 897032 | tf_op jit(solution)/shard_map/ppermute | solution.py:100
  7.9 8.7 %collective-permute-start = (bf16[1,73,16,128]{3,2,1,0:T(8,128)(2,1)S(1)}, bf16[1,73,16,128]{3,2,1,0:T(8,128)(2,1)S(1)}, u32[]{:S(2)}, u32[]{:S(2)}) collective-permute-start(bf16[1,73,16,128]{3,2,1,0:T(8,128)(2,1)S(1)} %bitcast.9), channel_id=1, source_target_pairs={{0,16},{1,5},{2,18},{3,7},{4,20},{5,1},{6,22},{7,3},{8,24},{9,13},... | collective-permute-start | bytes 897032 | tf_op jit(solution)/shard_map/ppermute | solution.py:100
  11.9 9.9 %collective-permute-start.14 = (bf16[2,73,16,128]{3,2,1,0:T(8,128)(2,1)S(1)}, bf16[2,73,16,128]{3,2,1,0:T(8,128)(2,1)S(1)}, u32[]{:S(2)}, u32[]{:S(2)}) collective-permute-start(bf16[2,73,16,128]{3,2,1,0:T(8,128)(2,1)S(1)} %pad_maximum_fusion.1.refs_0_), channel_id=1, source_target_pairs={{0,1},{1,0},{2,3},{3,2},{4,5},{5,4},{6,7},{7,6},{8,9},{9,8},{10,11... | collective-permute-start | bytes 1794056 | tf_op jit(solution)/shard_map/ppermute | solution.py:104
  12.2 14.1 %collective-permute-start.5 = (bf16[2,73,16,128]{3,2,1,0:T(8,128)(2,1)S(1)}, bf16[2,73,16,128]{3,2,1,0:T(8,128)(2,1)S(1)}, u32[]{:S(2)}, u32[]{:S(2)}) collective-permute-start(bf16[2,73,16,128]{3,2,1,0:T(8,128)(2,1)S(1)} %pad_maximum_fusion.1.refs_0_), channel_id=1, source_target_pairs={{0,6},{1,25},{2,4},{3,27},{4,2},{5,29},{6,0},{7,31},{8,14},{9,17},... | collective-permute-start | bytes 1794056 | tf_op jit(solution)/shard_map/ppermute | solution.py:100
  14.8 9.1 %collective-permute-start.3 = (bf16[2,73,16,128]{3,2,1,0:T(8,128)(2,1)S(1)}, bf16[2,73,16,128]{3,2,1,0:T(8,128)(2,1)S(1)}, u32[]{:S(2)}, u32[]{:S(2)}) collective-permute-start(bf16[2,73,16,128]{3,2,1,0:T(8,128)(2,1)S(1)} %pad_maximum_fusion.1.refs_0_), channel_id=1, source_target_pairs={{0,2},{1,9},{2,0},{3,11},{4,6},{5,13},{6,4},{7,15},{8,10},{9,1},{1... | collective-permute-start | bytes 1794056 | tf_op jit(solution)/shard_map/ppermute | solution.py:100
  16.6 13.2 %collective-permute-start.6 = (bf16[2,73,16,128]{3,2,1,0:T(8,128)(2,1)S(1)}, bf16[2,73,16,128]{3,2,1,0:T(8,128)(2,1)S(1)}, u32[]{:S(2)}, u32[]{:S(2)}) collective-permute-start(bf16[2,73,16,128]{3,2,1,0:T(8,128)(2,1)S(1)} %pad_maximum_fusion.refs_1_), channel_id=1, source_target_pairs={{0,6},{1,25},{2,4},{3,27},{4,2},{5,29},{6,0},{7,31},{8,14},{9,17},... | collective-permute-start | bytes 1794056 | tf_op jit(solution)/shard_map/ppermute | solution.py:100
  19.1 12.9 %collective-permute-start.15 = (bf16[2,73,16,128]{3,2,1,0:T(8,128)(2,1)S(1)}, bf16[2,73,16,128]{3,2,1,0:T(8,128)(2,1)S(1)}, u32[]{:S(2)}, u32[]{:S(2)}) collective-permute-start(bf16[2,73,16,128]{3,2,1,0:T(8,128)(2,1)S(1)} %pad_maximum_fusion.refs_1_), channel_id=1, source_target_pairs={{0,1},{1,0},{2,3},{3,2},{4,5},{5,4},{6,7},{7,6},{8,9},{9,8},{10,11... | collective-permute-start | bytes 1794056 | tf_op jit(solution)/shard_map/ppermute | solution.py:104
  21.8 11.2 %collective-permute-start.4 = (bf16[2,73,16,128]{3,2,1,0:T(8,128)(2,1)S(1)}, bf16[2,73,16,128]{3,2,1,0:T(8,128)(2,1)S(1)}, u32[]{:S(2)}, u32[]{:S(2)}) collective-permute-start(bf16[2,73,16,128]{3,2,1,0:T(8,128)(2,1)S(1)} %pad_maximum_fusion.refs_1_), channel_id=1, source_target_pairs={{0,2},{1,9},{2,0},{3,11},{4,6},{5,13},{6,4},{7,15},{8,10},{9,1},{1... | collective-permute-start | bytes 1794056 | tf_op jit(solution)/shard_map/ppermute | solution.py:100
  23.9 9.2 %collective-permute-start.16 = (bf16[2,73,16,128]{3,2,1,0:T(8,128)(2,1)S(1)}, bf16[2,73,16,128]{3,2,1,0:T(8,128)(2,1)S(1)}, u32[]{:S(2)}, u32[]{:S(2)}) collective-permute-start(bf16[2,73,16,128]{3,2,1,0:T(8,128)(2,1)S(1)} %collective-permute-done.3.refs_2_), channel_id=1, source_target_pairs={{0,1},{1,0},{2,3},{3,2},{4,5},{5,4},{6,7},{7,6},{8,9},{9,8},{10,11... | collective-permute-start | bytes 1794056 | tf_op jit(solution)/shard_map/ppermute | solution.py:104
  26.3 10.3 %collective-permute-start.7 = (bf16[2,73,16,128]{3,2,1,0:T(8,128)(2,1)S(1)}, bf16[2,73,16,128]{3,2,1,0:T(8,128)(2,1)S(1)}, u32[]{:S(2)}, u32[]{:S(2)}) collective-permute-start(bf16[2,73,16,128]{3,2,1,0:T(8,128)(2,1)S(1)} %collective-permute-done.3.refs_2_), channel_id=1, source_target_pairs={{0,6},{1,25},{2,4},{3,27},{4,2},{5,29},{6,0},{7,31},{8,14},{9,17},... | collective-permute-start | bytes 1794056 | tf_op jit(solution)/shard_map/ppermute | solution.py:100
  29.8 9.1 %collective-permute-start.8 = (bf16[2,73,16,128]{3,2,1,0:T(8,128)(2,1)S(1)}, bf16[2,73,16,128]{3,2,1,0:T(8,128)(2,1)S(1)}, u32[]{:S(2)}, u32[]{:S(2)}) collective-permute-start(bf16[2,73,16,128]{3,2,1,0:T(8,128)(2,1)S(1)} %collective-permute-done.6.refs_5_), channel_id=1, source_target_pairs={{0,2},{1,9},{2,0},{3,11},{4,6},{5,13},{6,4},{7,15},{8,10},{9,1},{1... | collective-permute-start | bytes 1794056 | tf_op jit(solution)/shard_map/ppermute | solution.py:100
  32.1 8.8 %collective-permute-start.18 = (bf16[2,73,16,128]{3,2,1,0:T(8,128)(2,1)S(1)}, bf16[2,73,16,128]{3,2,1,0:T(8,128)(2,1)S(1)}, u32[]{:S(2)}, u32[]{:S(2)}) collective-permute-start(bf16[2,73,16,128]{3,2,1,0:T(8,128)(2,1)S(1)} %collective-permute-done.5.refs_4_), channel_id=1, source_target_pairs={{0,1},{1,0},{2,3},{3,2},{4,5},{5,4},{6,7},{7,6},{8,9},{9,8},{10,11... | collective-permute-start | bytes 1794056 | tf_op jit(solution)/shard_map/ppermute | solution.py:104
  33.0 10.5 %collective-permute-start.19 = (bf16[2,73,16,128]{3,2,1,0:T(8,128)(2,1)S(1)}, bf16[2,73,16,128]{3,2,1,0:T(8,128)(2,1)S(1)}, u32[]{:S(2)}, u32[]{:S(2)}) collective-permute-start(bf16[2,73,16,128]{3,2,1,0:T(8,128)(2,1)S(1)} %collective-permute-done.6.refs_5_), channel_id=1, source_target_pairs={{0,1},{1,0},{2,3},{3,2},{4,5},{5,4},{6,7},{7,6},{8,9},{9,8},{10,11... | collective-permute-start | bytes 1794056 | tf_op jit(solution)/shard_map/ppermute | solution.py:104
  33.1 10.9 %collective-permute-start.17 = (bf16[2,73,16,128]{3,2,1,0:T(8,128)(2,1)S(1)}, bf16[2,73,16,128]{3,2,1,0:T(8,128)(2,1)S(1)}, u32[]{:S(2)}, u32[]{:S(2)}) collective-permute-start(bf16[2,73,16,128]{3,2,1,0:T(8,128)(2,1)S(1)} %collective-permute-done.4.refs_3_), channel_id=1, source_target_pairs={{0,1},{1,0},{2,3},{3,2},{4,5},{5,4},{6,7},{7,6},{8,9},{9,8},{10,11... | collective-permute-start | bytes 1794056 | tf_op jit(solution)/shard_map/ppermute | solution.py:104
  36.6 8.1 %collective-permute-start.12 = (bf16[2,73,16,128]{3,2,1,0:T(8,128)(2,1)S(1)}, bf16[2,73,16,128]{3,2,1,0:T(8,128)(2,1)S(1)}, u32[]{:S(2)}, u32[]{:S(2)}) collective-permute-start(bf16[2,73,16,128]{3,2,1,0:T(8,128)(2,1)S(1)} %collective-permute-done.7.refs_6_.refs_0_), channel_id=1, source_target_pairs={{0,1},{1,0},{2,3},{3,2},{4,5},{5,4},{6,7},{7,6},{8,9},{9,8},{10,11... | collective-permute-start | bytes 1794056 | tf_op jit(solution)/shard_map/ppermute | solution.py:104
  38.9 5.8 %collective-permute-start.13 = (bf16[2,73,16,128]{3,2,1,0:T(8,128)(2,1)S(1)}, bf16[2,73,16,128]{3,2,1,0:T(8,128)(2,1)S(1)}, u32[]{:S(2)}, u32[]{:S(2)}) collective-permute-start(bf16[2,73,16,128]{3,2,1,0:T(8,128)(2,1)S(1)} %collective-permute-done.8.refs_7_.refs_1_), channel_id=1, source_target_pairs={{0,1},{1,0},{2,3},{3,2},{4,5},{5,4},{6,7},{7,6},{8,9},{9,8},{10,11... | collective-permute-start | bytes 1794056 | tf_op jit(solution)/shard_map/ppermute | solution.py:104
  40.9 8.4 %collective-permute-start.11 = (bf16[16,16,128]{2,1,0:T(8,128)(2,1)S(1)}, bf16[16,16,128]{2,1,0:T(8,128)(2,1)S(1)}, u32[]{:S(2)}, u32[]{:S(2)}) collective-permute-start(bf16[16,16,128]{2,1,0:T(8,128)(2,1)S(1)} %tops.1), channel_id=1, source_target_pairs={{0,96},{32,64},{64,32},{96,0},{1,97},{33,65},{65,33},{97,1},{2,98}... | collective-permute-start | bytes 196616 | tf_op jit(solution)/shard_map/ppermute | solution.py:394
  43.4 5.9 %collective-permute-start.10 = (bf16[16,16,128]{2,1,0:T(8,128)(2,1)S(1)}, bf16[16,16,128]{2,1,0:T(8,128)(2,1)S(1)}, u32[]{:S(2)}, u32[]{:S(2)}) collective-permute-start(bf16[16,16,128]{2,1,0:T(8,128)(2,1)S(1)} %tops.1), channel_id=1, source_target_pairs={{0,64},{32,96},{64,0},{96,32},{1,65},{33,97},{65,1},{97,33},{2,66}... | collective-permute-start | bytes 196616 | tf_op jit(solution)/shard_map/ppermute | solution.py:394
  44.0 5.3 %collective-permute-start.9 = (bf16[16,16,128]{2,1,0:T(8,128)(2,1)S(1)}, bf16[16,16,128]{2,1,0:T(8,128)(2,1)S(1)}, u32[]{:S(2)}, u32[]{:S(2)}) collective-permute-start(bf16[16,16,128]{2,1,0:T(8,128)(2,1)S(1)} %tops.1), channel_id=1, source_target_pairs={{0,32},{32,0},{64,96},{96,64},{1,33},{33,1},{65,97},{97,65},{2,34}... | collective-permute-start | bytes 196616 | tf_op jit(solution)/shard_map/ppermute | solution.py:394
  49.4 2.2 %collective-permute-start.20 = (bf16[64,16,128]{2,1,0:T(8,128)(2,1)S(1)}, bf16[64,16,128]{2,1,0:T(8,128)(2,1)S(1)}, u32[]{:S(2)}, u32[]{:S(2)}) collective-permute-start(bf16[64,16,128]{2,1,0:T(8,128)(2,1)S(1)} %pad_maximum_fusion.2), channel_id=1, source_target_pairs={{0,1},{1,0},{2,3},{3,2},{4,5},{5,4},{6,7},{7,6},{8,9},{9,8},{10,11... | collective-permute-start | bytes 786440 | tf_op jit(solution)/shard_map/ppermute | solution.py:104
  50.3 1.6 %copy-start = (bf16[64,64,256]{2,1,0:T(8,128)(2,1)S(1)}, bf16[64,64,256]{2,1,0:T(8,128)(2,1)}, u32[]{:S(2)}) copy-start(bf16[64,64,256]{2,1,0:T(8,128)(2,1)} %out_basis.1) | copy-start | bytes 6291460
  50.3 1.8 %copy-start.1 = (bf16[64,64,64]{2,1,0:T(8,128)(2,1)S(1)}, bf16[64,64,64]{2,1,0:T(8,128)(2,1)}, u32[]{:S(2)}) copy-start(bf16[64,64,64]{2,1,0:T(8,128)(2,1)} %leaf_descend.1) | copy-start | bytes 1572868
  50.3 1.9 %copy-start.2 = (bf16[1,16,64,64]{3,2,1,0:T(8,128)(2,1)S(1)}, bf16[1,16,64,64]{3,2,1,0:T(8,128)(2,1)}, u32[]{:S(2)}) copy-start(bf16[1,16,64,64]{3,2,1,0:T(8,128)(2,1)} %top_coupling.1) | copy-start | bytes 393220
  50.3 1.9 %copy-start.3 = (bf16[8,64,64]{2,1,0:T(8,128)(2,1)S(1)}, bf16[8,64,64]{2,1,0:T(8,128)(2,1)}, u32[]{:S(2)}) copy-start(bf16[8,64,64]{2,1,0:T(8,128)(2,1)} %parent_descend.1) | copy-start | bytes 196612
  50.4 1.9 %copy-start.4 = (s32[64]{0:T(128)S(1)}, s32[64]{0:T(128)}, u32[]{:S(2)}) copy-start(s32[64]{0:T(128)} %counts.3) | copy-start | bytes 772

commit v6 on v5

--- a/solution.py
+++ b/solution.py
@@ -327,8 +327,14 @@
 
 
 def down_kernel(
-    counts, top_rows, tops, top_coupling, parent_far, parent_descend, leaf_far, leaf_descend, out_basis, out, values, sem
+    count_source, row_source, tops, top_coupling, parent_far, parent_descend, leaf_far, leaf_descend, out_basis, out, values, counts, top_rows, sem
 ):
+    row_copy = pltpu.make_async_copy(row_source, top_rows, sem.at[PARENT])
+    count_copy = pltpu.make_async_copy(count_source, counts, sem.at[PARENT + 1])
+    row_copy.start()
+    count_copy.start()
+    row_copy.wait()
+    count_copy.wait()
     block = picked(lambda j: tops[top_rows[0, j]], 16)
     top_field = dot(block, top_coupling[0].reshape(1024, 64)).astype(BF16)
     column = lax.broadcasted_iota(jnp.int32, (32, 256), 1)
@@ -347,17 +353,22 @@
 
 
 def down(counts, top_rows, *operands):
-    smem, vmem = pl.BlockSpec(memory_space=pltpu.SMEM), pl.BlockSpec(memory_space=pltpu.VMEM)
+    hbm, vmem = pl.BlockSpec(memory_space=pltpu.HBM), pl.BlockSpec(memory_space=pltpu.VMEM)
     return pl.pallas_call(
         down_kernel,
-        in_specs=[smem] * 2 + [vmem] * len(operands),
+        in_specs=[hbm, vmem] + [vmem] * len(operands),
         out_specs=pl.BlockSpec(memory_space=pltpu.HBM),
         out_shape=jax.ShapeDtypeStruct((64, 32, 256), BF16),
-        scratch_shapes=[pltpu.VMEM((64, 32, 256), BF16), pltpu.SemaphoreType.DMA((PARENT,))],
+        scratch_shapes=[
+            pltpu.VMEM((64, 32, 256), BF16),
+            pltpu.SMEM(counts.shape, jnp.int32),
+            pltpu.SMEM(top_rows.shape, jnp.int32),
+            pltpu.SemaphoreType.DMA((PARENT + 2,)),
+        ],
         compiler_params=pltpu.CompilerParams(vmem_limit_bytes=4 * MIB),
         cost_estimate=pl.CostEstimate(flops=2 * 64 * 32 * 64 * 320, bytes_accessed=6 * MIB, transcendentals=0),
         name="down",
-    )(counts, top_rows, *operands)
+    )(pltpu.with_memory_space_constraint(counts, pltpu.HBM), top_rows, *operands)
 
 
 def body(

time: 54.8 us -> 55 us (level)
  no operation moved by 1% of the time
where the time goes in v6:
time: 55 us; the launch traced here: 54.8 us
  starting transfers between devices  26.9 us (49%)
  Pallas kernels  17 us (31%)
  waiting for transfers between devices  9.76 us (18%)
  local copies, waits for them, and re-layouts  0.75 us (1%)
    ppermute x9, starting transfers between devices, send(): return lax.ppermute(x, ('y', 'z', 'c'), pairs(second, mask))  13.3 us
    ppermute x9, starting transfers between devices, other_core(): return lax.ppermute(x, 'c', [(0, 1), (1, 0)])  10.2 us
    ppermute x9, waiting for transfers between devices, send(): return lax.ppermute(x, ('y', 'z', 'c'), pairs(second, mask))  9.73 us
    pallas_call x1, Pallas kernels, couple(): pl.pallas_call(couple_kernel, in_specs=[vmem] * 4 + [pl.BlockSpec(memory_...  4.39 us
    ppermute x3, starting transfers between devices, body(): lax.ppermute(tops, 'x', [(i, i ^ m) for i in range(4)])  3.33 us
    pallas_call x1, Pallas kernels, up(): pl.pallas_call(up_kernel, in_specs=[hbm] * 5, out_specs=pl.BlockSpec(memo...  2.98 us
    pallas_call x1, Pallas kernels, stage(): pl.pallas_call(stage_kernel, in_specs=[smem] + [pl.BlockSpec(memory_space...  2.87 us
    pallas_call x1, Pallas kernels, down(): pl.pallas_call(down_kernel, in_specs=[hbm, vmem] + [vmem] * len(operands)...  2.57 us
  transfers between devices with their start and end apart: 21, of which 5 were waited for; matrix products, arithmetic and copies ran while one was open for 0% of the time, Pallas kernels for 21%

profile of v6, /device:TPU:1, one launch (start us, length us, event | category | flops | bytes accessed | tf_op | source)
XLA Modules:
  0.0 54.8 jit_solution(16190534988562546720)
XLA Ops:
  0.1 3.0 %up.1 = bf16[73,16,128]{2,1,0:T(8,128)(2,1)S(1)} custom-call(s32[64]{0:T(128)} %count_source.1, bf16[64,32,256]{2,1,0:T(8,128)(2,1)} %charges, bf16[64,64,256]{2,1,0:T(8,128)(2,1)} %basis.1, bf16[64,64,64]{2,1,0:T(8,128)(2,1)} %transfer.1, bf16[8,64,64]{2,1,0:T(8,128)(2,1)} %parent_transfer.1), custom_call_target="tpu_custom_call" | custom-call | flops 83886080 | bytes 5242880 | tf_op jit(solution)/shard_map/up/pallas_call | solution.py:74
  3.1 2.5 %collective-permute-start.2 = (bf16[1,73,16,128]{3,2,1,0:T(8,128)(2,1)S(1)}, bf16[1,73,16,128]{3,2,1,0:T(8,128)(2,1)S(1)}, u32[]{:S(2)}, u32[]{:S(2)}) collective-permute-start(bf16[1,73,16,128]{3,2,1,0:T(8,128)(2,1)S(1)} %bitcast.7), channel_id=1, source_target_pairs={{0,8},{1,3},{2,10},{3,1},{4,12},{5,7},{6,14},{7,5},{8,0},{9,11},{1... | collective-permute-start | bytes 897032 | tf_op jit(solution)/shard_map/ppermute | solution.py:100
  5.6 2.2 %collective-permute-start.1 = (bf16[1,73,16,128]{3,2,1,0:T(8,128)(2,1)S(1)}, bf16[1,73,16,128]{3,2,1,0:T(8,128)(2,1)S(1)}, u32[]{:S(2)}, u32[]{:S(2)}) collective-permute-start(bf16[1,73,16,128]{3,2,1,0:T(8,128)(2,1)S(1)} %bitcast.8), channel_id=1, source_target_pairs={{0,24},{1,7},{2,26},{3,5},{4,28},{5,3},{6,30},{7,1},{8,16},{9,15},... | collective-permute-start | bytes 897032 | tf_op jit(solution)/shard_map/ppermute | solution.py:100
  7.9 1.1 %collective-permute-start = (bf16[1,73,16,128]{3,2,1,0:T(8,128)(2,1)S(1)}, bf16[1,73,16,128]{3,2,1,0:T(8,128)(2,1)S(1)}, u32[]{:S(2)}, u32[]{:S(2)}) collective-permute-start(bf16[1,73,16,128]{3,2,1,0:T(8,128)(2,1)S(1)} %bitcast.9), channel_id=1, source_target_pairs={{0,16},{1,5},{2,18},{3,7},{4,20},{5,1},{6,22},{7,3},{8,24},{9,13},... | collective-permute-start | bytes 897032 | tf_op jit(solution)/shard_map/ppermute | solution.py:100
  8.9 2.9 %stage.1 = (bf16[16,16,64,64]{3,2,1,0:T(8,128)(2,1)S(1)}, s32[16,64]{1,0:T(8,128)S(1)}, s32[8,16]{1,0:T(8,128)S(1)}, s32[1,16]{1,0:T(1,128)S(1)}) custom-call(s32[4]{0:T(128)S(1)} %pad_add_fusion.place, s32[16,64]{1,0:T(8,128)} %bitcast.11, s32[16,64]{1,0:T(8,128)} %bitcast.12, s32[8,16]{1,0:T(8,128)} %refs_2_.1, s32[8,16]{1,0:T(8,128)} %refs_3_.1, ...), custom_call_target="tpu_custom_call" | custom-call | bytes 4096 | tf_op jit(solution)/shard_map/stage/pallas_call | solution.py:216
  11.9 0.3 collective-permute-start.14
  12.2 2.6 %collective-permute-start.5 = (bf16[2,73,16,128]{3,2,1,0:T(8,128)(2,1)S(1)}, bf16[2,73,16,128]{3,2,1,0:T(8,128)(2,1)S(1)}, u32[]{:S(2)}, u32[]{:S(2)}) collective-permute-start(bf16[2,73,16,128]{3,2,1,0:T(8,128)(2,1)S(1)} %pad_maximum_fusion.1.refs_0_), channel_id=1, source_target_pairs={{0,6},{1,25},{2,4},{3,27},{4,2},{5,29},{6,0},{7,31},{8,14},{9,17},... | collective-permute-start | bytes 1794056 | tf_op jit(solution)/shard_map/ppermute | solution.py:100
  14.8 1.8 %collective-permute-done = bf16[1,73,16,128]{3,2,1,0:T(8,128)(2,1)S(1)} collective-permute-done((bf16[1,73,16,128]{3,2,1,0:T(8,128)(2,1)S(1)}, bf16[1,73,16,128]{3,2,1,0:T(8,128)(2,1)S(1)}, u32[]{:S(2)}, u32[]{:S(2)}) %collective-permute-start) | collective-permute-done | bytes 299040 | tf_op jit(solution)/shard_map/ppermute | solution.py:100
  16.6 2.5 %collective-permute-start.6 = (bf16[2,73,16,128]{3,2,1,0:T(8,128)(2,1)S(1)}, bf16[2,73,16,128]{3,2,1,0:T(8,128)(2,1)S(1)}, u32[]{:S(2)}, u32[]{:S(2)}) collective-permute-start(bf16[2,73,16,128]{3,2,1,0:T(8,128)(2,1)S(1)} %pad_maximum_fusion.refs_1_), channel_id=1, source_target_pairs={{0,6},{1,25},{2,4},{3,27},{4,2},{5,29},{6,0},{7,31},{8,14},{9,17},... | collective-permute-start | bytes 1794056 | tf_op jit(solution)/shard_map/ppermute | solution.py:100
  19.1 2.6 %collective-permute-start.15 = (bf16[2,73,16,128]{3,2,1,0:T(8,128)(2,1)S(1)}, bf16[2,73,16,128]{3,2,1,0:T(8,128)(2,1)S(1)}, u32[]{:S(2)}, u32[]{:S(2)}) collective-permute-start(bf16[2,73,16,128]{3,2,1,0:T(8,128)(2,1)S(1)} %pad_maximum_fusion.refs_1_), channel_id=1, source_target_pairs={{0,1},{1,0},{2,3},{3,2},{4,5},{5,4},{6,7},{7,6},{8,9},{9,8},{10,11... | collective-permute-start | bytes 1794056 | tf_op jit(solution)/shard_map/ppermute | solution.py:104
  21.8 2.1 %collective-permute-done.3.refs_2_ = bf16[2,73,16,128]{3,2,1,0:T(8,128)(2,1)S(1)} collective-permute-done((bf16[2,73,16,128]{3,2,1,0:T(8,128)(2,1)S(1)}, bf16[2,73,16,128]{3,2,1,0:T(8,128)(2,1)S(1)}, u32[]{:S(2)}, u32[]{:S(2)}) %collective-permute-start.3) | collective-permute-done | bytes 598048 | tf_op jit(solution)/shard_map/ppermute | solution.py:100
  23.9 2.4 %collective-permute-start.16 = (bf16[2,73,16,128]{3,2,1,0:T(8,128)(2,1)S(1)}, bf16[2,73,16,128]{3,2,1,0:T(8,128)(2,1)S(1)}, u32[]{:S(2)}, u32[]{:S(2)}) collective-permute-start(bf16[2,73,16,128]{3,2,1,0:T(8,128)(2,1)S(1)} %collective-permute-done.3.refs_2_), channel_id=1, source_target_pairs={{0,1},{1,0},{2,3},{3,2},{4,5},{5,4},{6,7},{7,6},{8,9},{9,8},{10,11... | collective-permute-start | bytes 1794056 | tf_op jit(solution)/shard_map/ppermute | solution.py:104
  26.3 2.3 %collective-permute-start.7 = (bf16[2,73,16,128]{3,2,1,0:T(8,128)(2,1)S(1)}, bf16[2,73,16,128]{3,2,1,0:T(8,128)(2,1)S(1)}, u32[]{:S(2)}, u32[]{:S(2)}) collective-permute-start(bf16[2,73,16,128]{3,2,1,0:T(8,128)(2,1)S(1)} %collective-permute-done.3.refs_2_), channel_id=1, source_target_pairs={{0,6},{1,25},{2,4},{3,27},{4,2},{5,29},{6,0},{7,31},{8,14},{9,17},... | collective-permute-start | bytes 1794056 | tf_op jit(solution)/shard_map/ppermute | solution.py:100
  28.6 1.2 %collective-permute-done.6.refs_5_ = bf16[2,73,16,128]{3,2,1,0:T(8,128)(2,1)S(1)} collective-permute-done((bf16[2,73,16,128]{3,2,1,0:T(8,128)(2,1)S(1)}, bf16[2,73,16,128]{3,2,1,0:T(8,128)(2,1)S(1)}, u32[]{:S(2)}, u32[]{:S(2)}) %collective-permute-start.6) | collective-permute-done | bytes 598048 | tf_op jit(solution)/shard_map/ppermute | solution.py:100
  29.8 2.2 %stage_more.1.more = bf16[16,16,64,64]{3,2,1,0:T(8,128)(2,1)S(1)} custom-call(bf16[64,16,64,64]{3,2,1,0:T(8,128)(2,1)} %coupling.3), custom_call_target="tpu_custom_call" | custom-call | bytes 4096 | tf_op jit(solution)/shard_map/stage_more/pallas_call | solution.py:242
  32.1 0.9 %collective-permute-start.18 = (bf16[2,73,16,128]{3,2,1,0:T(8,128)(2,1)S(1)}, bf16[2,73,16,128]{3,2,1,0:T(8,128)(2,1)S(1)}, u32[]{:S(2)}, u32[]{:S(2)}) collective-permute-start(bf16[2,73,16,128]{3,2,1,0:T(8,128)(2,1)S(1)} %collective-permute-done.5.refs_4_), channel_id=1, source_target_pairs={{0,1},{1,0},{2,3},{3,2},{4,5},{5,4},{6,7},{7,6},{8,9},{9,8},{10,11... | collective-permute-start | bytes 1794056 | tf_op jit(solution)/shard_map/ppermute | solution.py:104
  33.1 0.4 collective-permute-start.17
  33.5 3.1 %collective-permute-done.7.refs_6_.refs_0_ = bf16[2,73,16,128]{3,2,1,0:T(8,128)(2,1)S(1)} collective-permute-done((bf16[2,73,16,128]{3,2,1,0:T(8,128)(2,1)S(1)}, bf16[2,73,16,128]{3,2,1,0:T(8,128)(2,1)S(1)}, u32[]{:S(2)}, u32[]{:S(2)}) %collective-permute-start.7) | collective-permute-done | bytes 598048 | tf_op jit(solution)/shard_map/ppermute | solution.py:100
  36.6 0.9 %collective-permute-start.12 = (bf16[2,73,16,128]{3,2,1,0:T(8,128)(2,1)S(1)}, bf16[2,73,16,128]{3,2,1,0:T(8,128)(2,1)S(1)}, u32[]{:S(2)}, u32[]{:S(2)}) collective-permute-start(bf16[2,73,16,128]{3,2,1,0:T(8,128)(2,1)S(1)} %collective-permute-done.7.refs_6_.refs_0_), channel_id=1, source_target_pairs={{0,1},{1,0},{2,3},{3,2},{4,5},{5,4},{6,7},{7,6},{8,9},{9,8},{10,11... | collective-permute-start | bytes 1794056 | tf_op jit(solution)/shard_map/ppermute | solution.py:104
  37.5 1.5 %collective-permute-done.8.refs_7_.refs_1_ = bf16[2,73,16,128]{3,2,1,0:T(8,128)(2,1)S(1)} collective-permute-done((bf16[2,73,16,128]{3,2,1,0:T(8,128)(2,1)S(1)}, bf16[2,73,16,128]{3,2,1,0:T(8,128)(2,1)S(1)}, u32[]{:S(2)}, u32[]{:S(2)}) %collective-permute-start.8) | collective-permute-done | bytes 598048 | tf_op jit(solution)/shard_map/ppermute | solution.py:100
  38.9 1.7 %collective-permute-start.13 = (bf16[2,73,16,128]{3,2,1,0:T(8,128)(2,1)S(1)}, bf16[2,73,16,128]{3,2,1,0:T(8,128)(2,1)S(1)}, u32[]{:S(2)}, u32[]{:S(2)}) collective-permute-start(bf16[2,73,16,128]{3,2,1,0:T(8,128)(2,1)S(1)} %collective-permute-done.8.refs_7_.refs_1_), channel_id=1, source_target_pairs={{0,1},{1,0},{2,3},{3,2},{4,5},{5,4},{6,7},{7,6},{8,9},{9,8},{10,11... | collective-permute-start | bytes 1794056 | tf_op jit(solution)/shard_map/ppermute | solution.py:104
  40.6 0.2 tops.1
  40.9 2.6 %collective-permute-start.11 = (bf16[16,16,128]{2,1,0:T(8,128)(2,1)S(1)}, bf16[16,16,128]{2,1,0:T(8,128)(2,1)S(1)}, u32[]{:S(2)}, u32[]{:S(2)}) collective-permute-start(bf16[16,16,128]{2,1,0:T(8,128)(2,1)S(1)} %tops.1), channel_id=1, source_target_pairs={{0,96},{32,64},{64,32},{96,0},{1,97},{33,65},{65,33},{97,1},{2,98}... | collective-permute-start | bytes 196616 | tf_op jit(solution)/shard_map/ppermute | solution.py:405
  43.4 0.5 collective-permute-start.10
  44.0 0.3 collective-permute-start.9
  44.2 0.5 assemble.2.refs_4_
  44.9 4.4 %couple.1 = (f32[64,32,64]{2,1,0:T(8,128)S(1)}, bf16[8,16,64,64]{3,2,1,0:T(8,128)(2,1)S(1)}) custom-call(s32[16,64]{1,0:T(8,128)S(1)} %get-tuple-element.34.leaf_rows, bf16[2336,16,128]{2,1,0:T(8,128)(2,1)S(1)} %assemble.3.gathered, bf16[16,16,64,64]{3,2,1,0:T(8,128)(2,1)S(1)} %get-tuple-element.35.head, bf16[16,16,64,64]{3,2,1,0:T(8,128)(2,1)S(1)} %stage_more.1.more, ...), custom_call_target="tpu_custom_call" | custom-call | flops 301989888 | bytes 29360128 | tf_op jit(solution)/shard_map/couple/pallas_call | solution.py:305
  49.4 0.9 %collective-permute-start.20 = (bf16[64,16,128]{2,1,0:T(8,128)(2,1)S(1)}, bf16[64,16,128]{2,1,0:T(8,128)(2,1)S(1)}, u32[]{:S(2)}, u32[]{:S(2)}) collective-permute-start(bf16[64,16,128]{2,1,0:T(8,128)(2,1)S(1)} %pad_maximum_fusion.2), channel_id=1, source_target_pairs={{0,1},{1,0},{2,3},{3,2},{4,5},{5,4},{6,7},{7,6},{8,9},{9,8},{10,11... | collective-permute-start | bytes 786440 | tf_op jit(solution)/shard_map/ppermute | solution.py:104
  50.4 1.1 %couple_parents.1.parent_far = f32[8,32,64]{2,1,0:T(8,128)S(1)} custom-call(s32[8,16]{1,0:T(8,128)S(1)} %get-tuple-element.42.parent_rows, bf16[2336,16,128]{2,1,0:T(8,128)(2,1)S(1)} %assemble.3.gathered, bf16[8,16,64,64]{3,2,1,0:T(8,128)(2,1)S(1)} %get-tuple-element.43.coupling), custom_call_target="tpu_custom_call" | custom-call | flops 33554432 | bytes 3145728 | tf_op jit(solution)/shard_map/couple_parents/pallas_call | solution.py:291
  51.6 0.3 copy-done
  51.9 0.3 copy-done.1
  52.3 2.6 %down.1 = bf16[64,32,256]{2,1,0:T(8,128)(2,1)} custom-call(s32[64]{0:T(128)} %count_source.1, s32[1,16]{1,0:T(1,128)S(1)} %get-tuple-element.31.row_source, bf16[128,16,128]{2,1,0:T(8,128)(2,1)S(1)} %constant_dynamic-update-slice_fusion.tops, bf16[1,16,64,64]{3,2,1,0:T(8,128)(2,1)S(1)} %copy-done.2, f32[8,32,64]{2,1,0:T(8,128)S(1)} %couple_parents.1.parent_far, ...), custom_call_target="tpu_custom_call" | custom-call | flops 83886080 | bytes 6291456 | tf_op jit(solution)/shard_map/down/pallas_call | solution.py:357
  (36 shorter events, 0.7 us)
Async XLA Ops:
  3.1 8.7 %collective-permute-start.2 = (bf16[1,73,16,128]{3,2,1,0:T(8,128)(2,1)S(1)}, bf16[1,73,16,128]{3,2,1,0:T(8,128)(2,1)S(1)}, u32[]{:S(2)}, u32[]{:S(2)}) collective-permute-start(bf16[1,73,16,128]{3,2,1,0:T(8,128)(2,1)S(1)} %bitcast.7), channel_id=1, source_target_pairs={{0,8},{1,3},{2,10},{3,1},{4,12},{5,7},{6,14},{7,5},{8,0},{9,11},{1... | collective-permute-start | bytes 897032 | tf_op jit(solution)/shard_map/ppermute | solution.py:100
  5.6 9.2 %collective-permute-start.1 = (bf16[1,73,16,128]{3,2,1,0:T(8,128)(2,1)S(1)}, bf16[1,73,16,128]{3,2,1,0:T(8,128)(2,1)S(1)}, u32[]{:S(2)}, u32[]{:S(2)}) collective-permute-start(bf16[1,73,16,128]{3,2,1,0:T(8,128)(2,1)S(1)} %bitcast.8), channel_id=1, source_target_pairs={{0,24},{1,7},{2,26},{3,5},{4,28},{5,3},{6,30},{7,1},{8,16},{9,15},... | collective-permute-start | bytes 897032 | tf_op jit(solution)/shard_map/ppermute | solution.py:100
  7.9 8.7 %collective-permute-start = (bf16[1,73,16,128]{3,2,1,0:T(8,128)(2,1)S(1)}, bf16[1,73,16,128]{3,2,1,0:T(8,128)(2,1)S(1)}, u32[]{:S(2)}, u32[]{:S(2)}) collective-permute-start(bf16[1,73,16,128]{3,2,1,0:T(8,128)(2,1)S(1)} %bitcast.9), channel_id=1, source_target_pairs={{0,16},{1,5},{2,18},{3,7},{4,20},{5,1},{6,22},{7,3},{8,24},{9,13},... | collective-permute-start | bytes 897032 | tf_op jit(solution)/shard_map/ppermute | solution.py:100
  11.9 9.9 %collective-permute-start.14 = (bf16[2,73,16,128]{3,2,1,0:T(8,128)(2,1)S(1)}, bf16[2,73,16,128]{3,2,1,0:T(8,128)(2,1)S(1)}, u32[]{:S(2)}, u32[]{:S(2)}) collective-permute-start(bf16[2,73,16,128]{3,2,1,0:T(8,128)(2,1)S(1)} %pad_maximum_fusion.1.refs_0_), channel_id=1, source_target_pairs={{0,1},{1,0},{2,3},{3,2},{4,5},{5,4},{6,7},{7,6},{8,9},{9,8},{10,11... | collective-permute-start | bytes 1794056 | tf_op jit(solution)/shard_map/ppermute | solution.py:104
  12.2 14.1 %collective-permute-start.5 = (bf16[2,73,16,128]{3,2,1,0:T(8,128)(2,1)S(1)}, bf16[2,73,16,128]{3,2,1,0:T(8,128)(2,1)S(1)}, u32[]{:S(2)}, u32[]{:S(2)}) collective-permute-start(bf16[2,73,16,128]{3,2,1,0:T(8,128)(2,1)S(1)} %pad_maximum_fusion.1.refs_0_), channel_id=1, source_target_pairs={{0,6},{1,25},{2,4},{3,27},{4,2},{5,29},{6,0},{7,31},{8,14},{9,17},... | collective-permute-start | bytes 1794056 | tf_op jit(solution)/shard_map/ppermute | solution.py:100
  14.8 9.1 %collective-permute-start.3 = (bf16[2,73,16,128]{3,2,1,0:T(8,128)(2,1)S(1)}, bf16[2,73,16,128]{3,2,1,0:T(8,128)(2,1)S(1)}, u32[]{:S(2)}, u32[]{:S(2)}) collective-permute-start(bf16[2,73,16,128]{3,2,1,0:T(8,128)(2,1)S(1)} %pad_maximum_fusion.1.refs_0_), channel_id=1, source_target_pairs={{0,2},{1,9},{2,0},{3,11},{4,6},{5,13},{6,4},{7,15},{8,10},{9,1},{1... | collective-permute-start | bytes 1794056 | tf_op jit(solution)/shard_map/ppermute | solution.py:100
  16.6 13.2 %collective-permute-start.6 = (bf16[2,73,16,128]{3,2,1,0:T(8,128)(2,1)S(1)}, bf16[2,73,16,128]{3,2,1,0:T(8,128)(2,1)S(1)}, u32[]{:S(2)}, u32[]{:S(2)}) collective-permute-start(bf16[2,73,16,128]{3,2,1,0:T(8,128)(2,1)S(1)} %pad_maximum_fusion.refs_1_), channel_id=1, source_target_pairs={{0,6},{1,25},{2,4},{3,27},{4,2},{5,29},{6,0},{7,31},{8,14},{9,17},... | collective-permute-start | bytes 1794056 | tf_op jit(solution)/shard_map/ppermute | solution.py:100
  19.1 12.9 %collective-permute-start.15 = (bf16[2,73,16,128]{3,2,1,0:T(8,128)(2,1)S(1)}, bf16[2,73,16,128]{3,2,1,0:T(8,128)(2,1)S(1)}, u32[]{:S(2)}, u32[]{:S(2)}) collective-permute-start(bf16[2,73,16,128]{3,2,1,0:T(8,128)(2,1)S(1)} %pad_maximum_fusion.refs_1_), channel_id=1, source_target_pairs={{0,1},{1,0},{2,3},{3,2},{4,5},{5,4},{6,7},{7,6},{8,9},{9,8},{10,11... | collective-permute-start | bytes 1794056 | tf_op jit(solution)/shard_map/ppermute | solution.py:104
  21.8 11.2 %collective-permute-start.4 = (bf16[2,73,16,128]{3,2,1,0:T(8,128)(2,1)S(1)}, bf16[2,73,16,128]{3,2,1,0:T(8,128)(2,1)S(1)}, u32[]{:S(2)}, u32[]{:S(2)}) collective-permute-start(bf16[2,73,16,128]{3,2,1,0:T(8,128)(2,1)S(1)} %pad_maximum_fusion.refs_1_), channel_id=1, source_target_pairs={{0,2},{1,9},{2,0},{3,11},{4,6},{5,13},{6,4},{7,15},{8,10},{9,1},{1... | collective-permute-start | bytes 1794056 | tf_op jit(solution)/shard_map/ppermute | solution.py:100
  23.9 9.2 %collective-permute-start.16 = (bf16[2,73,16,128]{3,2,1,0:T(8,128)(2,1)S(1)}, bf16[2,73,16,128]{3,2,1,0:T(8,128)(2,1)S(1)}, u32[]{:S(2)}, u32[]{:S(2)}) collective-permute-start(bf16[2,73,16,128]{3,2,1,0:T(8,128)(2,1)S(1)} %collective-permute-done.3.refs_2_), channel_id=1, source_target_pairs={{0,1},{1,0},{2,3},{3,2},{4,5},{5,4},{6,7},{7,6},{8,9},{9,8},{10,11... | collective-permute-start | bytes 1794056 | tf_op jit(solution)/shard_map/ppermute | solution.py:104
  26.3 10.3 %collective-permute-start.7 = (bf16[2,73,16,128]{3,2,1,0:T(8,128)(2,1)S(1)}, bf16[2,73,16,128]{3,2,1,0:T(8,128)(2,1)S(1)}, u32[]{:S(2)}, u32[]{:S(2)}) collective-permute-start(bf16[2,73,16,128]{3,2,1,0:T(8,128)(2,1)S(1)} %collective-permute-done.3.refs_2_), channel_id=1, source_target_pairs={{0,6},{1,25},{2,4},{3,27},{4,2},{5,29},{6,0},{7,31},{8,14},{9,17},... | collective-permute-start | bytes 1794056 | tf_op jit(solution)/shard_map/ppermute | solution.py:100
  29.8 9.1 %collective-permute-start.8 = (bf16[2,73,16,128]{3,2,1,0:T(8,128)(2,1)S(1)}, bf16[2,73,16,128]{3,2,1,0:T(8,128)(2,1)S(1)}, u32[]{:S(2)}, u32[]{:S(2)}) collective-permute-start(bf16[2,73,16,128]{3,2,1,0:T(8,128)(2,1)S(1)} %collective-permute-done.6.refs_5_), channel_id=1, source_target_pairs={{0,2},{1,9},{2,0},{3,11},{4,6},{5,13},{6,4},{7,15},{8,10},{9,1},{1... | collective-permute-start | bytes 1794056 | tf_op jit(solution)/shard_map/ppermute | solution.py:100
  32.1 8.8 %collective-permute-start.18 = (bf16[2,73,16,128]{3,2,1,0:T(8,128)(2,1)S(1)}, bf16[2,73,16,128]{3,2,1,0:T(8,128)(2,1)S(1)}, u32[]{:S(2)}, u32[]{:S(2)}) collective-permute-start(bf16[2,73,16,128]{3,2,1,0:T(8,128)(2,1)S(1)} %collective-permute-done.5.refs_4_), channel_id=1, source_target_pairs={{0,1},{1,0},{2,3},{3,2},{4,5},{5,4},{6,7},{7,6},{8,9},{9,8},{10,11... | collective-permute-start | bytes 1794056 | tf_op jit(solution)/shard_map/ppermute | solution.py:104
  33.0 10.5 %collective-permute-start.19 = (bf16[2,73,16,128]{3,2,1,0:T(8,128)(2,1)S(1)}, bf16[2,73,16,128]{3,2,1,0:T(8,128)(2,1)S(1)}, u32[]{:S(2)}, u32[]{:S(2)}) collective-permute-start(bf16[2,73,16,128]{3,2,1,0:T(8,128)(2,1)S(1)} %collective-permute-done.6.refs_5_), channel_id=1, source_target_pairs={{0,1},{1,0},{2,3},{3,2},{4,5},{5,4},{6,7},{7,6},{8,9},{9,8},{10,11... | collective-permute-start | bytes 1794056 | tf_op jit(solution)/shard_map/ppermute | solution.py:104
  33.1 10.9 %collective-permute-start.17 = (bf16[2,73,16,128]{3,2,1,0:T(8,128)(2,1)S(1)}, bf16[2,73,16,128]{3,2,1,0:T(8,128)(2,1)S(1)}, u32[]{:S(2)}, u32[]{:S(2)}) collective-permute-start(bf16[2,73,16,128]{3,2,1,0:T(8,128)(2,1)S(1)} %collective-permute-done.4.refs_3_), channel_id=1, source_target_pairs={{0,1},{1,0},{2,3},{3,2},{4,5},{5,4},{6,7},{7,6},{8,9},{9,8},{10,11... | collective-permute-start | bytes 1794056 | tf_op jit(solution)/shard_map/ppermute | solution.py:104
  36.6 8.1 %collective-permute-start.12 = (bf16[2,73,16,128]{3,2,1,0:T(8,128)(2,1)S(1)}, bf16[2,73,16,128]{3,2,1,0:T(8,128)(2,1)S(1)}, u32[]{:S(2)}, u32[]{:S(2)}) collective-permute-start(bf16[2,73,16,128]{3,2,1,0:T(8,128)(2,1)S(1)} %collective-permute-done.7.refs_6_.refs_0_), channel_id=1, source_target_pairs={{0,1},{1,0},{2,3},{3,2},{4,5},{5,4},{6,7},{7,6},{8,9},{9,8},{10,11... | collective-permute-start | bytes 1794056 | tf_op jit(solution)/shard_map/ppermute | solution.py:104
  38.9 5.8 %collective-permute-start.13 = (bf16[2,73,16,128]{3,2,1,0:T(8,128)(2,1)S(1)}, bf16[2,73,16,128]{3,2,1,0:T(8,128)(2,1)S(1)}, u32[]{:S(2)}, u32[]{:S(2)}) collective-permute-start(bf16[2,73,16,128]{3,2,1,0:T(8,128)(2,1)S(1)} %collective-permute-done.8.refs_7_.refs_1_), channel_id=1, source_target_pairs={{0,1},{1,0},{2,3},{3,2},{4,5},{5,4},{6,7},{7,6},{8,9},{9,8},{10,11... | collective-permute-start | bytes 1794056 | tf_op jit(solution)/shard_map/ppermute | solution.py:104
  40.9 8.4 %collective-permute-start.11 = (bf16[16,16,128]{2,1,0:T(8,128)(2,1)S(1)}, bf16[16,16,128]{2,1,0:T(8,128)(2,1)S(1)}, u32[]{:S(2)}, u32[]{:S(2)}) collective-permute-start(bf16[16,16,128]{2,1,0:T(8,128)(2,1)S(1)} %tops.1), channel_id=1, source_target_pairs={{0,96},{32,64},{64,32},{96,0},{1,97},{33,65},{65,33},{97,1},{2,98}... | collective-permute-start | bytes 196616 | tf_op jit(solution)/shard_map/ppermute | solution.py:405
  43.4 5.8 %collective-permute-start.10 = (bf16[16,16,128]{2,1,0:T(8,128)(2,1)S(1)}, bf16[16,16,128]{2,1,0:T(8,128)(2,1)S(1)}, u32[]{:S(2)}, u32[]{:S(2)}) collective-permute-start(bf16[16,16,128]{2,1,0:T(8,128)(2,1)S(1)} %tops.1), channel_id=1, source_target_pairs={{0,64},{32,96},{64,0},{96,32},{1,65},{33,97},{65,1},{97,33},{2,66}... | collective-permute-start | bytes 196616 | tf_op jit(solution)/shard_map/ppermute | solution.py:405
  44.0 5.3 %collective-permute-start.9 = (bf16[16,16,128]{2,1,0:T(8,128)(2,1)S(1)}, bf16[16,16,128]{2,1,0:T(8,128)(2,1)S(1)}, u32[]{:S(2)}, u32[]{:S(2)}) collective-permute-start(bf16[16,16,128]{2,1,0:T(8,128)(2,1)S(1)} %tops.1), channel_id=1, source_target_pairs={{0,32},{32,0},{64,96},{96,64},{1,33},{33,1},{65,97},{97,65},{2,34}... | collective-permute-start | bytes 196616 | tf_op jit(solution)/shard_map/ppermute | solution.py:405
  49.4 2.2 %collective-permute-start.20 = (bf16[64,16,128]{2,1,0:T(8,128)(2,1)S(1)}, bf16[64,16,128]{2,1,0:T(8,128)(2,1)S(1)}, u32[]{:S(2)}, u32[]{:S(2)}) collective-permute-start(bf16[64,16,128]{2,1,0:T(8,128)(2,1)S(1)} %pad_maximum_fusion.2), channel_id=1, source_target_pairs={{0,1},{1,0},{2,3},{3,2},{4,5},{5,4},{6,7},{7,6},{8,9},{9,8},{10,11... | collective-permute-start | bytes 786440 | tf_op jit(solution)/shard_map/ppermute | solution.py:104
  50.3 1.6 %copy-start = (bf16[64,64,256]{2,1,0:T(8,128)(2,1)S(1)}, bf16[64,64,256]{2,1,0:T(8,128)(2,1)}, u32[]{:S(2)}) copy-start(bf16[64,64,256]{2,1,0:T(8,128)(2,1)} %out_basis.1) | copy-start | bytes 6291460
  50.3 1.8 %copy-start.1 = (bf16[64,64,64]{2,1,0:T(8,128)(2,1)S(1)}, bf16[64,64,64]{2,1,0:T(8,128)(2,1)}, u32[]{:S(2)}) copy-start(bf16[64,64,64]{2,1,0:T(8,128)(2,1)} %leaf_descend.1) | copy-start | bytes 1572868
  50.3 1.9 %copy-start.2 = (bf16[1,16,64,64]{3,2,1,0:T(8,128)(2,1)S(1)}, bf16[1,16,64,64]{3,2,1,0:T(8,128)(2,1)}, u32[]{:S(2)}) copy-start(bf16[1,16,64,64]{3,2,1,0:T(8,128)(2,1)} %top_coupling.1) | copy-start | bytes 393220
  50.4 1.9 %copy-start.3 = (bf16[8,64,64]{2,1,0:T(8,128)(2,1)S(1)}, bf16[8,64,64]{2,1,0:T(8,128)(2,1)}, u32[]{:S(2)}) copy-start(bf16[8,64,64]{2,1,0:T(8,128)(2,1)} %parent_descend.1) | copy-start | bytes 196612
